TPU v7x, 32 devices: a whole 2x2x4 slice. The times are simulated.
32 devices in a mesh: fsdp: 8 (over z, x), tensor: 4 (over y, core).
Axes of the slice: x: 2, y: 2, z: 4, core: 2. Of those that a mesh axis runs over, the one named last changes fastest.
Arguments:
- tokens: bfloat16 [8, 2, 512, 2048], P('fsdp', None, 'tensor'), may hold values from -6 to 6
- lengths: int32 [8], P('fsdp'), may hold values from 512 to 1024, as said below
- w_query: bfloat16 [2048, 2048], P('fsdp', 'tensor'), may hold values from -0.5 to 0.5
- w_key: bfloat16 [2048, 512], P('fsdp', 'tensor'), may hold values from -0.5 to 0.5
- w_value: bfloat16 [2048, 512], P('fsdp', 'tensor'), may hold values from -0.125 to 0.125
- w_out: bfloat16 [2048, 2048], P('tensor', 'fsdp'), may hold values from -3 to 3
- w_gate: bfloat16 [2048, 8192], P('fsdp', 'tensor'), may hold values from -0.125 to 0.125
- w_up: bfloat16 [2048, 8192], P('fsdp', 'tensor'), may hold values from -0.125 to 0.125
- w_down: bfloat16 [8192, 2048], P('tensor', 'fsdp'), may hold values from -0.5 to 0.5
- gain_attn: bfloat16 [2048], P('fsdp'), may hold values from 0.5 to 1.5
- gain_mlp: bfloat16 [2048], P('fsdp'), may hold values from 0.5 to 1.5
- cotangent: bfloat16 [8, 2, 512, 2048], P('fsdp', None, 'tensor'), may hold values from -6 to 6
Outputs:
- output: float32 [8, 2, 512, 2048], P('fsdp', None, 'tensor')
- input_grad: float32 [8, 2, 512, 2048], P('fsdp', None, 'tensor')
- grad_query: float32 [2048, 2048], P('fsdp', 'tensor')
- grad_key: float32 [2048, 512], P('fsdp', 'tensor')
- grad_value: float32 [2048, 512], P('fsdp', 'tensor')
- grad_out: float32 [2048, 2048], P('tensor', 'fsdp')
- grad_gate: float32 [2048, 8192], P('fsdp', 'tensor')
- grad_up: float32 [2048, 8192], P('fsdp', 'tensor')
- grad_down: float32 [8192, 2048], P('tensor', 'fsdp')
- grad_gain_attn: float32 [2048], P(('fsdp', 'tensor'))
- grad_gain_mlp: float32 [2048], P(('fsdp', 'tensor'))
Inputs may be any that keep to these rules, and one draw needn't show every extreme that they name: `lengths`: valid slots of each sequence; some sequence has all 1024 slots valid.
All inputs are finite; a program needn't handle non-finite values.
Results may differ from a plain program's by a relative error of at most 0.019.
Values may be sent and summed in bfloat16 or wider, within the bound.
No kernel may reach another device: no remote copies, remote signals or barrier semaphores. Data moves between devices by JAX's collectives and lax.ppermute only.
A program may use at most 256 MiB of HBM per device.

v0:
```python
import jax
import jax.numpy as jnp
from jax import lax
from jax.sharding import PartitionSpec as P

HEAD_DIM = 64


EPS = 1e-05
MULT = 0.015625
RESIDUAL = 0.22
THETA = 10000000.0
NEGATIVE = -1e30


def normalize(values, gain):
    factor = lax.rsqrt(jnp.mean(values * values, -1, keepdims=True) + EPS)
    return (values * factor * gain, factor)


def norm_back(values, factor, gain, incoming):
    scaled_in = values * factor
    gain_part = jnp.sum(incoming * scaled_in, 0)
    weighted = incoming * gain
    back = factor * (weighted - scaled_in * jnp.mean(weighted * scaled_in, -1, keepdims=True))
    return (back, gain_part)


def rope_tables(positions, half):
    freqs = jnp.exp(-jnp.log(THETA) * jnp.arange(half).astype(jnp.float32) / half)
    angles = positions[:, None] * freqs[None, :]
    return (jnp.cos(angles)[:, None, :], jnp.sin(angles)[:, None, :])


def rotate(values, cosines, sines):
    half = values.shape[-1] // 2
    first = values[..., :half]
    second = values[..., half:]
    return jnp.concatenate([first * cosines - second * sines, second * cosines + first * sines], -1)


def unrotate(values, cosines, sines):
    half = values.shape[-1] // 2
    first = values[..., :half]
    second = values[..., half:]
    return jnp.concatenate([first * cosines + second * sines, second * cosines - first * sines], -1)


def shards(
    tokens,
    lengths,
    w_query,
    w_key,
    w_value,
    w_out,
    w_gate,
    w_up,
    w_down,
    gain_attn,
    gain_mlp,
    cotangent,
):
    tensor_count = lax.axis_size("tensor")
    tensor_rank = lax.axis_index("tensor")
    fsdp_count = lax.axis_size("fsdp")
    micro_count = tokens.shape[1]
    local_rows = tokens.shape[2]
    query_rows = local_rows * tensor_count
    total_rows = micro_count * query_rows
    length = lengths[0]
    heads_here = w_query.shape[1] // HEAD_DIM
    groups_here = w_key.shape[1] // HEAD_DIM
    repeat = heads_here // groups_here
    cosines, sines = rope_tables(jnp.arange(total_rows).astype(jnp.float32), HEAD_DIM // 2)

    def fetch():
        return (
            lax.all_gather(w_query, "fsdp", axis=0, tiled=True),
            lax.all_gather(w_key, "fsdp", axis=0, tiled=True),
            lax.all_gather(w_value, "fsdp", axis=0, tiled=True),
            lax.all_gather(w_out, "fsdp", axis=1, tiled=True),
            lax.all_gather(w_gate, "fsdp", axis=0, tiled=True),
            lax.all_gather(w_up, "fsdp", axis=0, tiled=True),
            lax.all_gather(w_down, "fsdp", axis=1, tiled=True),
            lax.all_gather(gain_attn, "fsdp", axis=0, tiled=True),
            lax.all_gather(gain_mlp, "fsdp", axis=0, tiled=True),
        )

    def gather_rows(values):
        return lax.all_gather(values, "tensor", axis=0, tiled=True)

    def scatter_rows(values):
        return lax.psum_scatter(values, "tensor", scatter_dimension=0, tiled=True)

    def masked_scores(grouped, keys_seen, batch_index):
        key_place = jnp.arange(keys_seen.shape[0])
        query_place = batch_index * query_rows + jnp.arange(query_rows)
        allowed = (key_place[None, :] <= query_place[:, None]) & (key_place[None, :] < length)
        scores = MULT * jnp.einsum(
            "qgrd,kgd->grqk", grouped, keys_seen, preferred_element_type=jnp.float32
        )
        return jnp.where(allowed, scores, NEGATIVE)

    key_parts = []
    value_parts = []
    saved = []
    outputs = []
    for batch_index in range(micro_count):
        current = fetch()
        (
            query_weight,
            key_weight,
            value_weight,
            out_weight,
            gate_weight,
            up_weight,
            down_weight,
            attn_gain,
            mlp_gain,
        ) = current
        start_row = batch_index * query_rows
        cos_part = cosines[start_row : start_row + query_rows]
        sin_part = sines[start_row : start_row + query_rows]
        stream = tokens[0, batch_index].astype(jnp.float32)
        normed, attn_factor = normalize(stream, attn_gain.astype(jnp.float32))
        normed_all = gather_rows(normed.astype(jnp.bfloat16))
        queries = jnp.dot(normed_all, query_weight, preferred_element_type=jnp.float32)
        queries = rotate(
            queries.reshape(query_rows, heads_here, HEAD_DIM), cos_part, sin_part
        ).astype(jnp.bfloat16)
        keys_new = jnp.dot(normed_all, key_weight, preferred_element_type=jnp.float32)
        keys_new = rotate(
            keys_new.reshape(query_rows, groups_here, HEAD_DIM), cos_part, sin_part
        ).astype(jnp.bfloat16)
        values_new = jnp.dot(normed_all, value_weight, preferred_element_type=jnp.float32).astype(
            jnp.bfloat16
        )
        key_parts.append(keys_new)
        value_parts.append(values_new.reshape(query_rows, groups_here, HEAD_DIM))
        keys_seen = jnp.concatenate(key_parts, 0)
        values_seen = jnp.concatenate(value_parts, 0)
        grouped = queries.reshape(query_rows, groups_here, repeat, HEAD_DIM)
        scores = masked_scores(grouped, keys_seen, batch_index)
        top = jnp.max(scores, -1, keepdims=True)
        expd = jnp.exp(scores - top)
        totals = jnp.sum(expd, -1, keepdims=True)
        probs = expd / totals
        log_total = top + jnp.log(totals)
        mixed = jnp.einsum(
            "grqk,kgd->qgrd",
            probs.astype(jnp.bfloat16),
            values_seen,
            preferred_element_type=jnp.float32,
        )
        mixed = mixed.reshape(query_rows, heads_here * HEAD_DIM).astype(jnp.bfloat16)
        attended = scatter_rows(jnp.dot(mixed, out_weight, preferred_element_type=jnp.float32))
        middle = stream + RESIDUAL * attended
        second, mlp_factor = normalize(middle, mlp_gain.astype(jnp.float32))
        second_all = gather_rows(second.astype(jnp.bfloat16))
        gate = jnp.dot(second_all, gate_weight, preferred_element_type=jnp.float32)
        up_proj = jnp.dot(second_all, up_weight, preferred_element_type=jnp.float32)
        hidden = (jax.nn.silu(gate) * up_proj).astype(jnp.bfloat16)
        branch = scatter_rows(jnp.dot(hidden, down_weight, preferred_element_type=jnp.float32))
        place = start_row + tensor_rank * local_rows + jnp.arange(local_rows)
        valid = (place < length).astype(jnp.float32)[:, None]
        outputs.append(valid * (middle + RESIDUAL * branch))
        saved.append(
            (
                stream,
                attn_factor,
                normed_all,
                grouped,
                log_total,
                mixed,
                middle,
                mlp_factor,
                second_all,
                gate,
                up_proj,
                hidden,
                valid,
            )
        )
    query_total = jnp.zeros((w_query.shape[0] * fsdp_count, w_query.shape[1]), jnp.float32)
    key_total = jnp.zeros((w_key.shape[0] * fsdp_count, w_key.shape[1]), jnp.float32)
    value_total = jnp.zeros((w_value.shape[0] * fsdp_count, w_value.shape[1]), jnp.float32)
    out_total = jnp.zeros((w_out.shape[0], w_out.shape[1] * fsdp_count), jnp.float32)
    gate_total = jnp.zeros((w_gate.shape[0] * fsdp_count, w_gate.shape[1]), jnp.float32)
    up_total = jnp.zeros((w_up.shape[0] * fsdp_count, w_up.shape[1]), jnp.float32)
    down_total = jnp.zeros((w_down.shape[0], w_down.shape[1] * fsdp_count), jnp.float32)
    attn_gain_total = jnp.zeros((gain_attn.shape[0] * fsdp_count,), jnp.float32)
    mlp_gain_total = jnp.zeros((gain_mlp.shape[0] * fsdp_count,), jnp.float32)
    key_grads = jnp.zeros((total_rows, groups_here, HEAD_DIM), jnp.float32)
    value_grads = jnp.zeros((total_rows, groups_here, HEAD_DIM), jnp.float32)
    input_parts = [None] * micro_count
    for batch_index in reversed(range(micro_count)):
        current = fetch()
        (
            query_weight,
            key_weight,
            value_weight,
            out_weight,
            gate_weight,
            up_weight,
            down_weight,
            attn_gain,
            mlp_gain,
        ) = current
        (
            stream,
            attn_factor,
            normed_all,
            grouped,
            log_total,
            mixed,
            middle,
            mlp_factor,
            second_all,
            gate,
            up_proj,
            hidden,
            valid,
        ) = saved[batch_index]
        start_row = batch_index * query_rows
        stop_row = start_row + query_rows
        cos_part = cosines[start_row:stop_row]
        sin_part = sines[start_row:stop_row]
        upstream = valid * cotangent[0, batch_index].astype(jnp.float32)
        branch_grad = gather_rows((RESIDUAL * upstream).astype(jnp.bfloat16))
        down_total = down_total + jnp.einsum(
            "qf,qd->fd", hidden, branch_grad, preferred_element_type=jnp.float32
        )
        hidden_grad = jnp.einsum(
            "qd,fd->qf", branch_grad, down_weight, preferred_element_type=jnp.float32
        )
        sigma = jax.nn.sigmoid(gate)
        gate_back = (hidden_grad * up_proj * sigma * (1.0 + gate * (1.0 - sigma))).astype(
            jnp.bfloat16
        )
        up_back = (hidden_grad * gate * sigma).astype(jnp.bfloat16)
        gate_total = gate_total + jnp.einsum(
            "qd,qf->df", second_all, gate_back, preferred_element_type=jnp.float32
        )
        up_total = up_total + jnp.einsum(
            "qd,qf->df", second_all, up_back, preferred_element_type=jnp.float32
        )
        second_part = jnp.einsum(
            "qf,df->qd", gate_back, gate_weight, preferred_element_type=jnp.float32
        )
        second_part = second_part + jnp.einsum(
            "qf,df->qd", up_back, up_weight, preferred_element_type=jnp.float32
        )
        second_grad = scatter_rows(second_part)
        back_mlp, mlp_gain_part = norm_back(
            middle, mlp_factor, mlp_gain.astype(jnp.float32), second_grad
        )
        middle_grad = upstream + back_mlp
        attn_grad = gather_rows((RESIDUAL * middle_grad).astype(jnp.bfloat16))
        out_total = out_total + jnp.einsum(
            "qe,qd->ed", mixed, attn_grad, preferred_element_type=jnp.float32
        )
        mixed_grad = jnp.einsum(
            "qd,ed->qe", attn_grad, out_weight, preferred_element_type=jnp.float32
        )
        mixed_grad = mixed_grad.astype(jnp.bfloat16).reshape(
            query_rows, groups_here, repeat, HEAD_DIM
        )
        keys_seen = jnp.concatenate(key_parts[: batch_index + 1], 0)
        values_seen = jnp.concatenate(value_parts[: batch_index + 1], 0)
        probs = jnp.exp(masked_scores(grouped, keys_seen, batch_index) - log_total)
        prob_grad = jnp.einsum(
            "qgrd,kgd->grqk", mixed_grad, values_seen, preferred_element_type=jnp.float32
        )
        score_grad = (probs * (prob_grad - jnp.sum(probs * prob_grad, -1, keepdims=True))).astype(
            jnp.bfloat16
        )
        query_grad = MULT * jnp.einsum(
            "grqk,kgd->qgrd", score_grad, keys_seen, preferred_element_type=jnp.float32
        )
        key_grads = key_grads.at[:stop_row].add(
            MULT
            * jnp.einsum("grqk,qgrd->kgd", score_grad, grouped, preferred_element_type=jnp.float32)
        )
        value_grads = value_grads.at[:stop_row].add(
            jnp.einsum(
                "grqk,qgrd->kgd",
                probs.astype(jnp.bfloat16),
                mixed_grad,
                preferred_element_type=jnp.float32,
            )
        )
        query_back = unrotate(
            query_grad.reshape(query_rows, heads_here, HEAD_DIM), cos_part, sin_part
        )
        query_back = query_back.reshape(query_rows, heads_here * HEAD_DIM).astype(jnp.bfloat16)
        key_back = unrotate(key_grads[start_row:stop_row], cos_part, sin_part)
        key_back = key_back.reshape(query_rows, groups_here * HEAD_DIM).astype(jnp.bfloat16)
        value_back = (
            value_grads[start_row:stop_row]
            .reshape(query_rows, groups_here * HEAD_DIM)
            .astype(jnp.bfloat16)
        )
        query_total = query_total + jnp.einsum(
            "qd,qe->de", normed_all, query_back, preferred_element_type=jnp.float32
        )
        key_total = key_total + jnp.einsum(
            "qd,qe->de", normed_all, key_back, preferred_element_type=jnp.float32
        )
        value_total = value_total + jnp.einsum(
            "qd,qe->de", normed_all, value_back, preferred_element_type=jnp.float32
        )
        normed_part = jnp.einsum(
            "qe,de->qd", query_back, query_weight, preferred_element_type=jnp.float32
        )
        normed_part = normed_part + jnp.einsum(
            "qe,de->qd", key_back, key_weight, preferred_element_type=jnp.float32
        )
        normed_part = normed_part + jnp.einsum(
            "qe,de->qd", value_back, value_weight, preferred_element_type=jnp.float32
        )
        normed_grad = scatter_rows(normed_part)
        back_attn, attn_gain_part = norm_back(
            stream, attn_factor, attn_gain.astype(jnp.float32), normed_grad
        )
        input_parts[batch_index] = middle_grad + back_attn
        attn_gain_total = attn_gain_total + attn_gain_part
        mlp_gain_total = mlp_gain_total + mlp_gain_part
    grads = (
        lax.psum_scatter(
            query_total.astype(jnp.bfloat16), "fsdp", scatter_dimension=0, tiled=True
        ).astype(jnp.float32),
        lax.psum_scatter(
            key_total.astype(jnp.bfloat16), "fsdp", scatter_dimension=0, tiled=True
        ).astype(jnp.float32),
        lax.psum_scatter(
            value_total.astype(jnp.bfloat16), "fsdp", scatter_dimension=0, tiled=True
        ).astype(jnp.float32),
        lax.psum_scatter(
            out_total.astype(jnp.bfloat16), "fsdp", scatter_dimension=1, tiled=True
        ).astype(jnp.float32),
        lax.psum_scatter(
            gate_total.astype(jnp.bfloat16), "fsdp", scatter_dimension=0, tiled=True
        ).astype(jnp.float32),
        lax.psum_scatter(
            up_total.astype(jnp.bfloat16), "fsdp", scatter_dimension=0, tiled=True
        ).astype(jnp.float32),
        lax.psum_scatter(
            down_total.astype(jnp.bfloat16), "fsdp", scatter_dimension=1, tiled=True
        ).astype(jnp.float32),
    )
    gain_grads = (
        lax.psum_scatter(attn_gain_total, ("fsdp", "tensor"), scatter_dimension=0, tiled=True),
        lax.psum_scatter(mlp_gain_total, ("fsdp", "tensor"), scatter_dimension=0, tiled=True),
    )
    output = jnp.stack(outputs, 0)[None]
    input_grad = jnp.stack(input_parts, 0)[None]
    return (
        output,
        input_grad,
        grads[0],
        grads[1],
        grads[2],
        grads[3],
        grads[4],
        grads[5],
        grads[6],
        gain_grads[0],
        gain_grads[1],
    )


def solution(mesh):
    return jax.shard_map(
        shards,
        mesh=mesh,
        in_specs=(
            P("fsdp", None, "tensor", None),
            P("fsdp"),
            P("fsdp", "tensor"),
            P("fsdp", "tensor"),
            P("fsdp", "tensor"),
            P("tensor", "fsdp"),
            P("fsdp", "tensor"),
            P("fsdp", "tensor"),
            P("tensor", "fsdp"),
            P("fsdp"),
            P("fsdp"),
            P("fsdp", None, "tensor", None),
        ),
        out_specs=(
            P("fsdp", None, "tensor", None),
            P("fsdp", None, "tensor", None),
            P("fsdp", "tensor"),
            P("fsdp", "tensor"),
            P("fsdp", "tensor"),
            P("tensor", "fsdp"),
            P("fsdp", "tensor"),
            P("fsdp", "tensor"),
            P("tensor", "fsdp"),
            P(("fsdp", "tensor")),
            P(("fsdp", "tensor")),
        ),
        check_vma=False,
    )
```

profile of v0, /device:TPU:1, one launch (start us, length us, event | category | flops | bytes accessed | tf_op | source)
XLA Modules:
  0.0 1944.8 jit_solution(13511770948125263623)
XLA Ops:
  9.4 17.9 all-gather
  34.0 25.5 %all_gather.37 = bf16[2048,128]{1,0:T(8,128)(2,1)S(1)} all-gather(bf16[256,128]{1,0:T(8,128)(2,1)S(1)} %copy-done.79), channel_id=1, replica_groups=mesh['fsdp'=8,'tensor'=4] {'fsdp'}, dimensions={0}, use_global_device_ids=true | all-gather | bytes 589824 | tf_op jit(solution)/shard_map/all_gather | solution.py:79
  59.5 26.1 %all_gather.36 = bf16[2048,128]{1,0:T(8,128)(2,1)S(1)} all-gather(bf16[256,128]{1,0:T(8,128)(2,1)S(1)} %copy-done.80), channel_id=1, replica_groups=mesh['fsdp'=8,'tensor'=4] {'fsdp'}, dimensions={0}, use_global_device_ids=true | all-gather | bytes 589824 | tf_op jit(solution)/shard_map/all_gather | solution.py:80
  92.0 16.0 all-gather.18.cloned.1.call-done
  117.6 42.8 %all-gather.20.cloned.1.call-done = bf16[512,2048]{1,0:T(8,128)(2,1)} async-done(((bf16[512,256]{1,0:T(8,128)(2,1)}), bf16[512,2048]{1,0:T(8,128)(2,1)}) %all-gather.20.cloned.1.call-update) | async-done | bytes 2097168 | tf_op jit(solution)/shard_map/all_gather | solution.py:81
  160.4 4.9 fusion.88
  166.9 17.4 all-gather.30.cloned.1.call-done
  191.0 8.4 fusion.85
  199.4 8.1 fusion.3
  207.5 7.6 fusion.30
  215.9 3.3 fusion.94
  220.0 16.7 all-gather.1
  236.8 41.1 %reduce-scatter.20.cloned.1.call-done = f32[128,2048]{1,0:T(8,128)} async-done(((f32[512,2048]{1,0:T(8,128)}), f32[128,2048]{1,0:T(8,128)}) %reduce-scatter.20.cloned.1.call-update) | async-done | bytes 1048592 | tf_op jit(solution)/shard_map/reduce_scatter | solution.py:93
  285.1 119.4 %all-gather.26.cloned.1.call-done = bf16[2048,2048]{1,0:T(8,128)(2,1)} async-done(((bf16[256,2048]{1,0:T(8,128)(2,1)}), bf16[2048,2048]{1,0:T(8,128)(2,1)}) %all-gather.26.cloned.1.call-update) | async-done | bytes 8388624 | tf_op jit(solution)/shard_map/all_gather | solution.py:83
  404.5 23.8 %all-gather.22.cloned.1.call-done = bf16[512,2048]{1,0:T(8,128)(2,1)} async-done(((bf16[128,2048]{1,0:T(8,128)(2,1)}), bf16[512,2048]{1,0:T(8,128)(2,1)}) %all-gather.22.cloned.1.call-update) | async-done | bytes 2097168 | tf_op jit(solution)/shard_map/all_gather | solution.py:90
  428.3 10.5 fusion.90
  438.8 115.8 %all-gather.24.cloned.1.call-done = bf16[2048,2048]{1,0:T(8,128)(2,1)} async-done(((bf16[256,2048]{1,0:T(8,128)(2,1)}), bf16[2048,2048]{1,0:T(8,128)(2,1)}) %all-gather.24.cloned.1.call-update) | async-done | bytes 8388624 | tf_op jit(solution)/shard_map/all_gather | solution.py:82
  554.6 10.5 fusion.89
  565.0 13.1 all-gather.34.cloned.1.call-done
  578.2 126.6 %all-gather.28.cloned.1.call-done = bf16[2048,2048]{1,0:T(8,128)(2,1)} async-done(((bf16[2048,256]{1,0:T(8,128)(2,1)}), bf16[2048,2048]{1,0:T(8,128)(2,1)}) %all-gather.28.cloned.1.call-update) | async-done | bytes 8388624 | tf_op jit(solution)/shard_map/all_gather | solution.py:84
  704.8 12.3 multiply_convert_fusion.2
  717.1 4.5 fusion.98
  721.7 9.5 convolution_add_fusion.1
  731.3 43.2 %reduce-scatter.24.cloned.1.call-done = f32[128,2048]{1,0:T(8,128)} async-done(((f32[512,2048]{1,0:T(8,128)}), f32[128,2048]{1,0:T(8,128)}) %reduce-scatter.24.cloned.1.call-update) | async-done | bytes 1048592 | tf_op jit(solution)/shard_map/reduce_scatter | solution.py:93
  774.5 3.0 multiply_reduce_fusion
  778.3 22.3 %all-gather.32.cloned.1.call-done = bf16[512,2048]{1,0:T(8,128)(2,1)} async-done(((bf16[128,2048]{1,0:T(8,128)(2,1)}), bf16[512,2048]{1,0:T(8,128)(2,1)}) %all-gather.32.cloned.1.call-update) | async-done | bytes 2097168 | tf_op jit(solution)/shard_map/all_gather | solution.py:90
  800.6 10.7 fusion.96
  811.3 9.4 fusion.95
  820.7 4.7 all-gather.38.cloned.1.call-done
  825.3 11.8 multiply_convert_fusion
  837.1 8.5 fusion.100
  845.6 9.6 convolution_add_fusion
  855.5 10.5 fusion.91
  866.1 10.6 fusion.97
  876.8 22.7 %reduce-scatter.26.cloned.1.call-done = f32[128,2048]{1,0:T(8,128)} async-done(((f32[512,2048]{1,0:T(8,128)}), f32[128,2048]{1,0:T(8,128)}) %reduce-scatter.26.cloned.1.call-update) | async-done | bytes 1048592 | tf_op jit(solution)/shard_map/reduce_scatter | solution.py:93
  901.6 44.7 %reduce-scatter.18.cloned.1.call-done = f32[128,2048]{1,0:T(8,128)} async-done(((f32[512,2048]{1,0:T(8,128)}), f32[128,2048]{1,0:T(8,128)}) %reduce-scatter.18.cloned.1.call-update) | async-done | bytes 1048592 | tf_op jit(solution)/shard_map/reduce_scatter | solution.py:93
  946.4 47.1 %reduce-scatter.22.cloned.1.call-done = f32[128,2048]{1,0:T(8,128)} async-done(((f32[512,2048]{1,0:T(8,128)}), f32[128,2048]{1,0:T(8,128)}) %reduce-scatter.22.cloned.1.call-update) | async-done | bytes 1048592 | tf_op jit(solution)/shard_map/reduce_scatter | solution.py:93
  993.4 5.5 multiply_convert_fusion.7
  1000.8 21.3 %all-gather.40.cloned.1.call-done = bf16[512,2048]{1,0:T(8,128)(2,1)} async-done(((bf16[128,2048]{1,0:T(8,128)(2,1)}), bf16[512,2048]{1,0:T(8,128)(2,1)}) %all-gather.40.cloned.1.call-update) | async-done | bytes 2097168 | tf_op jit(solution)/shard_map/all_gather | solution.py:90
  1022.1 3.5 convolution_convert_fusion
  1025.6 7.6 fusion.31
  1033.3 13.6 all-gather.36.cloned.1.call-done
  1046.8 3.0 convolution_convert_fusion.1
  1049.9 4.9 fusion.45
  1054.9 9.0 fusion.7
  1063.9 7.5 fusion
  1075.0 12.2 fusion.2
  1101.2 3.0 fusion.107
  1107.0 3.0 convolution_multiply_fusion.1
  1110.3 5.2 convolution_multiply_fusion
  1120.5 12.8 fusion.110
  1133.3 10.3 add_convert_fusion
  1143.7 12.8 fusion.109
  1156.5 10.4 add_convert_fusion.1
  1167.3 12.8 fusion.108
  1180.1 10.3 add_convert_fusion.2
  1208.9 61.7 %reduce-scatter.38.cloned.1.call-done = bf16[512,256]{1,0:T(8,128)(2,1)} async-done(((bf16[512,2048]{1,0:T(8,128)(2,1)}), bf16[512,256]{1,0:T(8,128)(2,1)}) %reduce-scatter.38.cloned.1.call-update) | async-done | bytes 262160 | tf_op jit(solution)/shard_map/reduce_scatter | solution.py:338
  1272.5 69.0 %reduce-scatter.32.cloned.1.call-done = bf16[256,512]{1,0:T(8,128)(2,1)} async-done(((bf16[2048,512]{1,0:T(8,128)(2,1)}), bf16[256,512]{1,0:T(8,128)(2,1)}) %reduce-scatter.32.cloned.1.call-update) | async-done | bytes 262160 | tf_op jit(solution)/shard_map/reduce_scatter | solution.py:329
  1343.3 152.0 %reduce-scatter.44.cloned.1.call-done = bf16[2048,256]{1,0:T(8,128)(2,1)} async-done(((bf16[2048,2048]{1,0:T(8,128)(2,1)}), bf16[2048,256]{1,0:T(8,128)(2,1)}) %reduce-scatter.44.cloned.1.call-update) | async-done | bytes 1048592 | tf_op jit(solution)/shard_map/reduce_scatter | solution.py:347
  1498.0 149.4 %reduce-scatter.42.cloned.1.call-done = bf16[256,2048]{1,0:T(8,128)(2,1)} async-done(((bf16[2048,2048]{1,0:T(8,128)(2,1)}), bf16[256,2048]{1,0:T(8,128)(2,1)}) %reduce-scatter.42.cloned.1.call-update) | async-done | bytes 1048592 | tf_op jit(solution)/shard_map/reduce_scatter | solution.py:344
  1650.2 148.7 %reduce-scatter.40.cloned.1.call-done = bf16[256,2048]{1,0:T(8,128)(2,1)} async-done(((bf16[2048,2048]{1,0:T(8,128)(2,1)}), bf16[256,2048]{1,0:T(8,128)(2,1)}) %reduce-scatter.40.cloned.1.call-update) | async-done | bytes 1048592 | tf_op jit(solution)/shard_map/reduce_scatter | solution.py:341
  1801.7 43.2 %reduce-scatter.28.cloned.1.call-done = f32[128,2048]{1,0:T(8,128)} async-done(((f32[512,2048]{1,0:T(8,128)}), f32[128,2048]{1,0:T(8,128)}) %reduce-scatter.28.cloned.1.call-update) | async-done | bytes 1048592 | tf_op jit(solution)/shard_map/reduce_scatter | solution.py:93
  1844.9 47.1 %reduce-scatter.30.cloned.1.call-done = f32[128,2048]{1,0:T(8,128)} async-done(((f32[512,2048]{1,0:T(8,128)}), f32[128,2048]{1,0:T(8,128)}) %reduce-scatter.30.cloned.1.call-update) | async-done | bytes 1048592 | tf_op jit(solution)/shard_map/reduce_scatter | solution.py:93
  1894.2 38.7 %all-reduce.2 = (f32[2048]{0:T(1024)S(1)}, f32[2048]{0:T(1024)S(1)}) all-reduce(f32[2048]{0:T(1024)S(1)} %add.297, f32[2048]{0:T(1024)S(1)} %add.298), channel_id=17, replica_groups=mesh['fsdp'=8,'tensor'=4] {'fsdp','tensor'}, use_global_device_ids=true, to_apply=%region_31.32.clone | all-reduce | flops 4096 | bytes 32768
  (362 shorter events, 109.1 us)
Async XLA Ops:
  7.2 26.8 %copy-start.79 = (bf16[256,128]{1,0:T(8,128)(2,1)S(1)}, bf16[256,128]{1,0:T(8,128)(2,1)}, u32[]{:S(2)}) copy-start(bf16[256,128]{1,0:T(8,128)(2,1)} %param.27) | copy-start | bytes 196612
  7.2 52.3 %copy-start.80 = (bf16[256,128]{1,0:T(8,128)(2,1)S(1)}, bf16[256,128]{1,0:T(8,128)(2,1)}, u32[]{:S(2)}) copy-start(bf16[256,128]{1,0:T(8,128)(2,1)} %param.28) | copy-start | bytes 196612
  7.2 79.0 %all-gather.16.cloned.1.call-start = ((), (), s32[]{:S(2)}) async-start(), calls=%async_computation.15 | async-start | bytes 2621440 | tf_op jit(solution)/shard_map/all_gather | solution.py:90
  30.4 77.6 %all-gather.18.cloned.1.call-start = ((), (), s32[]{:S(2)}) async-start(), calls=%async_computation.16 | async-start | bytes 2359296 | tf_op jit(solution)/shard_map/all_gather | solution.py:78
  31.1 129.3 %all-gather.20.cloned.1.call-start = ((), (), s32[]{:S(2)}) async-start(), calls=%async_computation.17 | async-start | bytes 2359296 | tf_op jit(solution)/shard_map/all_gather | solution.py:81
  31.8 152.4 %all-gather.30.cloned.1.call-start = ((), (), s32[]{:S(2)}) async-start(), calls=%async_computation.24 | async-start | bytes 2621440 | tf_op jit(solution)/shard_map/all_gather | solution.py:90
  32.4 204.3 %reduce-scatter.16.cloned.1.call-start = ((), (), s32[]{:S(2)}) async-start(), calls=%async_computation.18 | async-start | bytes 5242880 | tf_op jit(solution)/shard_map/reduce_scatter | solution.py:93
  59.5 124.7 %copy-start.13 = (bf16[2048,128]{1,0:T(8,128)(2,1)}, bf16[2048,128]{1,0:T(8,128)(2,1)S(1)}, u32[]{:S(2)}) copy-start(bf16[2048,128]{1,0:T(8,128)(2,1)S(1)} %all_gather.37) | copy-start | bytes 1572868
  85.6 101.3 %copy-start.11 = (bf16[2048,128]{1,0:T(8,128)(2,1)}, bf16[2048,128]{1,0:T(8,128)(2,1)S(1)}, u32[]{:S(2)}) copy-start(bf16[2048,128]{1,0:T(8,128)(2,1)S(1)} %all_gather.36) | copy-start | bytes 1572868
  86.2 24.7 %copy-start.37 = (f32[512,32]{0,1:T(8,128)}, f32[512,32]{0,1:T(8,128)S(1)}, u32[]{:S(2)}) copy-start(f32[512,32]{0,1:T(8,128)S(1)} %get-tuple-element.131) | copy-start | bytes 196612
  86.2 24.7 %copy-start.39 = (f32[512,32]{0,1:T(8,128)}, f32[512,32]{0,1:T(8,128)S(1)}, u32[]{:S(2)}) copy-start(f32[512,32]{0,1:T(8,128)S(1)} %get-tuple-element.149) | copy-start | bytes 196612
  86.2 104.6 %copy-start.33 = (f32[512,32]{0,1:T(8,128)}, f32[512,32]{0,1:T(8,128)S(1)}, u32[]{:S(2)}) copy-start(f32[512,32]{0,1:T(8,128)S(1)} %get-tuple-element.132) | copy-start | bytes 196612
  86.2 104.6 %copy-start.35 = (f32[512,32]{0,1:T(8,128)}, f32[512,32]{0,1:T(8,128)S(1)}, u32[]{:S(2)}) copy-start(f32[512,32]{0,1:T(8,128)S(1)} %get-tuple-element.148) | copy-start | bytes 196612
  86.2 21.7 %copy-start.4 = (bf16[512,2048]{1,0:T(8,128)(2,1)S(1)}, bf16[512,2048]{1,0:T(8,128)(2,1)}, u32[]{:S(2)}) copy-start(bf16[512,2048]{1,0:T(8,128)(2,1)} %all-gather.16.cloned.1.call-done) | copy-start | bytes 6291460
  88.8 118.6 %copy-start.41 = (bf16[512,128]{0,1:T(8,128)(2,1)}, bf16[512,128]{0,1:T(8,128)(2,1)S(1)}, u32[]{:S(2)}) copy-start(bf16[512,128]{0,1:T(8,128)(2,1)S(1)} %convolution_convert_fusion.3) | copy-start | bytes 393220
  117.6 47.8 %copy-start.28 = (bf16[2,64,4,512]{3,1,2,0:T(8,128)(2,1)}, bf16[2,64,4,512]{3,1,2,0:T(8,128)(2,1)S(1)}, u32[]{:S(2)}) copy-start(bf16[2,64,4,512]{3,1,2,0:T(8,128)(2,1)S(1)} %fusion.29) | copy-start | bytes 1572868
  165.4 24.0 %copy-start.17 = (bf16[2048,512]{1,0:T(8,128)(2,1)S(1)}, bf16[2048,512]{1,0:T(8,128)(2,1)}, u32[]{:S(2)}) copy-start(bf16[2048,512]{1,0:T(8,128)(2,1)} %all-gather.18.cloned.1.call-done) | copy-start | bytes 6291460
  165.4 112.4 %reduce-scatter.20.cloned.1.call-start = ((), (), s32[]{:S(2)}) async-start(), calls=%async_computation.25 | async-start | bytes 5242880 | tf_op jit(solution)/shard_map/reduce_scatter | solution.py:93
  189.4 18.0 copy-start.63
  219.1 58.7 %copy-start.9 = (bf16[1,2,128,2048]{3,2,1,0:T(8,128)(2,1)S(1)}, bf16[1,2,128,2048]{3,2,1,0:T(8,128)(2,1)}, u32[]{:S(2)}) copy-start(bf16[1,2,128,2048]{3,2,1,0:T(8,128)(2,1)} %param.24) | copy-start | bytes 3145732
  219.1 185.4 %all-gather.26.cloned.1.call-start = ((), (), s32[]{:S(2)}) async-start(), calls=%async_computation.21 | async-start | bytes 9437184 | tf_op jit(solution)/shard_map/all_gather | solution.py:83
  219.9 208.4 %all-gather.22.cloned.1.call-start = ((), (), s32[]{:S(2)}) async-start(), calls=%async_computation.19 | async-start | bytes 2621440 | tf_op jit(solution)/shard_map/all_gather | solution.py:90
  280.8 273.7 %all-gather.24.cloned.1.call-start = ((), (), s32[]{:S(2)}) async-start(), calls=%async_computation.20 | async-start | bytes 9437184 | tf_op jit(solution)/shard_map/all_gather | solution.py:82
  281.5 296.6 %all-gather.34.cloned.1.call-start = ((), (), s32[]{:S(2)}) async-start(), calls=%async_computation.28 | async-start | bytes 2621440 | tf_op jit(solution)/shard_map/all_gather | solution.py:90
  284.1 420.7 %all-gather.28.cloned.1.call-start = ((), (), s32[]{:S(2)}) async-start(), calls=%async_computation.22 | async-start | bytes 9437184 | tf_op jit(solution)/shard_map/all_gather | solution.py:84
  284.8 489.7 %reduce-scatter.24.cloned.1.call-start = ((), (), s32[]{:S(2)}) async-start(), calls=%async_computation.29 | async-start | bytes 5242880 | tf_op jit(solution)/shard_map/reduce_scatter | solution.py:93
  704.8 12.3 copy-start.88
  731.2 69.4 %all-gather.32.cloned.1.call-start = ((), (), s32[]{:S(2)}) async-start(), calls=%async_computation.26 | async-start | bytes 2621440 | tf_op jit(solution)/shard_map/all_gather | solution.py:90
  777.5 47.8 %all-gather.38.cloned.1.call-start = ((), (), s32[]{:S(2)}) async-start(), calls=%async_computation.31 | async-start | bytes 2621440 | tf_op jit(solution)/shard_map/all_gather | solution.py:90
  778.1 121.4 %reduce-scatter.26.cloned.1.call-start = ((), (), s32[]{:S(2)}) async-start(), calls=%async_computation.32 | async-start | bytes 5242880 | tf_op jit(solution)/shard_map/reduce_scatter | solution.py:93
  855.2 91.1 %reduce-scatter.18.cloned.1.call-start = ((), (), s32[]{:S(2)}) async-start(), calls=%async_computation.23 | async-start | bytes 5242880 | tf_op jit(solution)/shard_map/reduce_scatter | solution.py:93
  866.0 127.4 %reduce-scatter.22.cloned.1.call-start = ((), (), s32[]{:S(2)}) async-start(), calls=%async_computation.27 | async-start | bytes 5242880 | tf_op jit(solution)/shard_map/reduce_scatter | solution.py:93
  876.7 116.7 %copy-start.25 = (f32[128,2048]{1,0:T(8,128)S(1)}, f32[128,2048]{1,0:T(8,128)}, u32[]{:S(2)}) copy-start(f32[128,2048]{1,0:T(8,128)} %reduce-scatter.24.cloned.1.call-done) | copy-start | bytes 3145732
  876.7 145.3 %all-gather.40.cloned.1.call-start = ((), (), s32[]{:S(2)}) async-start(), calls=%async_computation.33 | async-start | bytes 2621440 | tf_op jit(solution)/shard_map/all_gather | solution.py:90
  901.6 98.5 %copy-start.76 = (f32[2,4,512]{2,1,0:T(4,128)S(1)}, f32[2,4,512]{2,1,0:T(4,128)}, u32[]{:S(2)}) copy-start(f32[2,4,512]{2,1,0:T(4,128)} %copy-done.75) | copy-start | bytes 49156
  901.6 98.5 %copy-start.78 = (f32[2,4,512]{2,1,0:T(4,128)S(1)}, f32[2,4,512]{2,1,0:T(4,128)}, u32[]{:S(2)}) copy-start(f32[2,4,512]{2,1,0:T(4,128)} %copy-done.77) | copy-start | bytes 49156
  998.9 47.9 %all-gather.36.cloned.1.call-start = ((), (), s32[]{:S(2)}) async-start(), calls=%async_computation.30 | async-start | bytes 2621440 | tf_op jit(solution)/shard_map/all_gather | solution.py:90
  999.7 206.3 %reduce-scatter.36.cloned.1.call-start = ((), (), s32[]{:S(2)}) async-start(), calls=%async_computation.38 | async-start | bytes 589824 | tf_op jit(solution)/shard_map/reduce_scatter | solution.py:335
  1025.6 21.3 %copy-start.16 = (bf16[512,2048]{1,0:T(8,128)(2,1)S(1)}, bf16[512,2048]{1,0:T(8,128)(2,1)}, u32[]{:S(2)}) copy-start(bf16[512,2048]{1,0:T(8,128)(2,1)} %all-gather.20.cloned.1.call-done) | copy-start | bytes 6291460
  1046.8 17.1 slice-start
  1049.9 14.0 slice-start.1
  1074.7 132.8 %reduce-scatter.34.cloned.1.call-start = ((), (), s32[]{:S(2)}) async-start(), calls=%async_computation.37 | async-start | bytes 589824 | tf_op jit(solution)/shard_map/reduce_scatter | solution.py:332
  1074.9 16.5 slice-start.4
  1074.9 16.5 slice-start.6
  1074.9 17.5 slice-start.5
  1074.9 18.7 slice-start.7
  1101.1 169.6 %reduce-scatter.38.cloned.1.call-start = ((), (), s32[]{:S(2)}) async-start(), calls=%async_computation.39 | async-start | bytes 2359296 | tf_op jit(solution)/shard_map/reduce_scatter | solution.py:338
  1106.9 234.6 %reduce-scatter.32.cloned.1.call-start = ((), (), s32[]{:S(2)}) async-start(), calls=%async_computation.36 | async-start | bytes 2359296 | tf_op jit(solution)/shard_map/reduce_scatter | solution.py:329
  1120.2 13.1 copy-start.90
  1120.2 375.1 %reduce-scatter.44.cloned.1.call-start = ((), (), s32[]{:S(2)}) async-start(), calls=%async_computation.42 | async-start | bytes 9437184 | tf_op jit(solution)/shard_map/reduce_scatter | solution.py:347
  1120.5 12.8 copy-start.99
  1143.6 12.8 copy-start.89
  1143.6 503.7 %reduce-scatter.42.cloned.1.call-start = ((), (), s32[]{:S(2)}) async-start(), calls=%async_computation.41 | async-start | bytes 9437184 | tf_op jit(solution)/shard_map/reduce_scatter | solution.py:344
  1143.7 12.8 copy-start.98
  1166.9 632.0 %reduce-scatter.40.cloned.1.call-start = ((), (), s32[]{:S(2)}) async-start(), calls=%async_computation.40 | async-start | bytes 9437184 | tf_op jit(solution)/shard_map/reduce_scatter | solution.py:341
  1167.3 12.8 copy-start.96
  1190.5 654.4 %reduce-scatter.28.cloned.1.call-start = ((), (), s32[]{:S(2)}) async-start(), calls=%async_computation.34 | async-start | bytes 5242880 | tf_op jit(solution)/shard_map/reduce_scatter | solution.py:93
  1196.8 695.1 %reduce-scatter.30.cloned.1.call-start = ((), (), s32[]{:S(2)}) async-start(), calls=%async_computation.35 | async-start | bytes 5242880 | tf_op jit(solution)/shard_map/reduce_scatter | solution.py:93
  1343.3 548.7 %copy-start.10 = (bf16[1,2,128,2048]{3,2,1,0:T(8,128)(2,1)S(1)}, bf16[1,2,128,2048]{3,2,1,0:T(8,128)(2,1)}, u32[]{:S(2)}) copy-start(bf16[1,2,128,2048]{3,2,1,0:T(8,128)(2,1)} %param.24) | copy-start | bytes 3145732
  1343.3 548.7 %copy-start.74 = (f32[8,1,256]{2,1,0:T(1,128)S(1)}, f32[8,1,256]{2,1,0:T(1,128)}, u32[]{:S(2)}) copy-start(f32[8,1,256]{2,1,0:T(1,128)} %copy-done.73) | copy-start | bytes 24580
  1343.3 548.7 %copy-start.85 = (f32[128]{0:T(128)S(1)}, f32[128]{0:T(128)}, u32[]{:S(2)}) copy-start(f32[128]{0:T(128)} %copy-done.84) | copy-start | bytes 1540
  1343.3 548.7 %copy-start.87 = (f32[128]{0:T(128)S(1)}, f32[128]{0:T(128)}, u32[]{:S(2)}) copy-start(f32[128]{0:T(128)} %copy-done.86) | copy-start | bytes 1540
  1498.0 436.1 %copy-start.23 = (f32[128,2048]{1,0:T(8,128)S(1)}, f32[128,2048]{1,0:T(8,128)}, u32[]{:S(2)}) copy-start(f32[128,2048]{1,0:T(8,128)} %get-tuple-element.90) | copy-start | bytes 3145732
  1498.0 436.1 %copy-start.24 = (f32[128,2048]{1,0:T(8,128)S(1)}, f32[128,2048]{1,0:T(8,128)}, u32[]{:S(2)}) copy-start(f32[128,2048]{1,0:T(8,128)} %get-tuple-element.114) | copy-start | bytes 3145732
  (72 other events, 264.7 us)
Sparse Core Ops, SparseCore 0:
  30.5 24.0 all-gather.15
  56.7 51.2 all-gather.17
  110.0 50.4 all-gather.19
  162.4 21.7 all-gather.29
  186.6 44.0 reduce-scatter.15
  233.3 44.5 reduce-scatter.19
  280.0 124.4 all-gather.25
  406.6 21.5 all-gather.21
  430.4 124.1 all-gather.23
  556.5 21.5 all-gather.33
  580.2 124.5 all-gather.27
  731.3 43.1 reduce-scatter.23
  777.6 22.9 all-gather.31
  802.7 22.5 all-gather.37
  855.3 44.0 reduce-scatter.25
  901.9 44.4 reduce-scatter.17
  948.9 44.4 reduce-scatter.21
  999.0 22.9 all-gather.39
  1024.2 22.5 all-gather.35
  1074.8 59.6 reduce-scatter.35
  1138.2 60.8 reduce-scatter.33
  1203.2 67.3 reduce-scatter.37
  1274.8 66.6 reduce-scatter.31
  1345.0 150.2 reduce-scatter.43
  1499.4 147.9 reduce-scatter.41
  1650.9 147.9 reduce-scatter.39
  1801.4 43.4 reduce-scatter.27
  1847.4 44.5 reduce-scatter.29
where the time goes:
time: 1950 us; the launch traced here: 1940 us
  waiting for transfers between devices  1410 us (72%)
  matrix products  301 us (15%)
  blocking collectives  125 us (6%)
  other arithmetic  70.8 us (4%)
    reduce_scatter x8, waiting for transfers between devices, scatter_rows(): return lax.psum_scatter(values, 'tensor', scatter_dimension=0, tiled=True)  289 us
    reduce_scatter x1, waiting for transfers between devices, shards(): lax.psum_scatter(down_total.astype(jnp.bfloat16), 'fsdp', scatter_dimensi...  152 us
    reduce_scatter x1, waiting for transfers between devices, shards(): lax.psum_scatter(up_total.astype(jnp.bfloat16), 'fsdp', scatter_dimension...  149 us
    reduce_scatter x1, waiting for transfers between devices, shards(): lax.psum_scatter(gate_total.astype(jnp.bfloat16), 'fsdp', scatter_dimensi...  149 us
    all_gather x1, waiting for transfers between devices, fetch(): lax.all_gather(w_down, 'fsdp', axis=1, tiled=True)  127 us
    all_gather x1, waiting for transfers between devices, fetch(): lax.all_gather(w_up, 'fsdp', axis=0, tiled=True)  119 us
    all_gather x8, waiting for transfers between devices, gather_rows(): return lax.all_gather(values, 'tensor', axis=0, tiled=True)  116 us
    all_gather x1, waiting for transfers between devices, fetch(): lax.all_gather(w_gate, 'fsdp', axis=0, tiled=True)  116 us
  transfers between devices with their start and end apart: 28, of which 24 were waited for; matrix products, arithmetic and copies ran while one was open for 14% of the time, Pallas kernels for 0%

commit v1 on v0

v1 whole, which is shorter than its diff:
```python
import functools

import jax
import jax.numpy as jnp
from jax import lax
from jax.experimental import pallas as pl
from jax.experimental.pallas import tpu as pltpu
from jax.sharding import Mesh, PartitionSpec as P

HEAD_DIM = 64
EPS = 1e-05
MULT = 0.015625
RESIDUAL = 0.22
THETA = 10000000.0
NEGATIVE = -1e30
F32 = jnp.float32
BF16 = jnp.bfloat16
BLOCK = 256
VMEM_LIMIT = 56 * 1024 * 1024
SMEM = pltpu.SMEM


def nn(a, b):
    return lax.dot_general(a, b, (((1,), (0,)), ((), ())), preferred_element_type=F32)


def nt(a, b):
    return lax.dot_general(a, b, (((1,), (1,)), ((), ())), preferred_element_type=F32)


def tn(a, b):
    return lax.dot_general(a, b, (((0,), (0,)), ((), ())), preferred_element_type=F32)


def params():
    return pltpu.CompilerParams(vmem_limit_bytes=VMEM_LIMIT)


def hops(sources, place):
    pairs = []
    for x in range(2):
        for y in range(2):
            for c in range(2):
                if sources != ("same" if x == c else "other"):
                    continue
                px, py, pc = place(x, y, c)
                pairs.append((x * 4 + y * 2 + c, px * 4 + py * 2 + pc))
    return pairs


def over_x(x, y, c):
    return 1 - x, y, c


def over_y(x, y, c):
    return x, 1 - y, c


def over_core(x, y, c):
    return x, y, 1 - c


def flip(pairs):
    return [pair[::-1] for pair in pairs]


FIRST = hops("other", lambda x, y, c: (c, y, x)) + hops("same", over_y)
SECOND = hops("same", over_x) + hops("other", lambda x, y, c: (x, 1 - y, 1 - c))
THIRD = hops("other", over_core)
PASS_Y = hops("other", over_y)
PASS_X = hops("same", over_x)


def send(values, pairs):
    return lax.ppermute(values, ("lo", "y", "core"), pairs)


def trade(values):
    received = send(values, hops("other", lambda x, y, c: (c, y, x)))
    return jnp.where(is_same(), values, received)


def is_same():
    return lax.axis_index("lo") == lax.axis_index("core")


def after(value, anchor):
    return lax.optimization_barrier((value, anchor))[0]


def send_rows(piece):
    first = send(piece, FIRST)
    second = send(piece, SECOND)
    third = send(piece, THIRD)
    return [first, second, third, send(first, PASS_Y), piece, send(first, PASS_X)]


def assemble_kernel(starts, *refs):
    pieces, out, sems = refs[:6], refs[6], refs[7]
    rows = pieces[0].shape[0]

    def copy(piece, k):
        start = pl.multiple_of(starts[k], rows)
        return pltpu.make_async_copy(pieces[piece], out.at[pl.ds(start, rows)], sems.at[k])

    copy(0, 0).start()
    copy(1, 1).start()

    @pl.when(starts[4] == 1)
    def _():
        copy(2, 2).start()
        copy(4, 3).start()

    @pl.when(starts[4] != 1)
    def _():
        copy(3, 2).start()
        copy(5, 3).start()

    for k in range(4):
        copy(k, k).wait()


def join_rows(pieces, starts):
    rows, width = pieces[0].shape
    return pl.pallas_call(
        assemble_kernel,
        out_shape=jax.ShapeDtypeStruct((4 * rows, width), pieces[0].dtype),
        in_specs=[pl.BlockSpec(memory_space=SMEM)] + [pl.BlockSpec(memory_space=pl.ANY)] * 6,
        out_specs=pl.BlockSpec(memory_space=pltpu.VMEM),
        scratch_shapes=[pltpu.SemaphoreType.DMA((4,))],
        compiler_params=params(),
        name="assemble",
    )(starts, *pieces)


def send_sums(parts):
    across_y = send(parts[2], flip(PASS_Y))
    across_x = send(parts[3], flip(PASS_X))
    second = send(parts[1], flip(SECOND))
    third = send(parts[2], flip(THIRD))
    passed = jnp.where(is_same(), across_x, across_y).astype(F32)
    first = send((parts[0].astype(F32) + passed).astype(BF16), flip(FIRST))
    return [first, second, jnp.where(is_same(), parts[3], third)]


def add_sums(parts):
    return sum(part.astype(F32) for part in parts)


def swap_z(values, step, count):
    return lax.ppermute(values, "hi", [(i, i ^ step) for i in range(count)])


class Order:

    def __init__(self):
        self.last = None

    def __call__(self, step, first, *rest):
        if self.last is not None:
            first = after(first, self.last)
        found = step(first, *rest)
        self.last = jax.tree.leaves(found)[0]
        return found


def project_kernel(pairs, rows, starts, *refs):
    lhs, rhs = refs[:pairs], refs[pairs : 2 * pairs]
    outs, total = refs[2 * pairs : -1], refs[-1]
    value = None
    for a, b in zip(lhs, rhs):
        term = nt(a[...], b[...])
        value = term if value is None else value + term
    total[...] = value
    for k, out in enumerate(outs):
        start = pl.multiple_of(starts[k], rows)
        out[...] = total[pl.ds(start, rows), :].astype(BF16)


def project(starts, lhs, rhs, places):
    tall = lhs[0].shape[0]
    count = 4
    rows = tall // count
    wide = rhs[0].shape[0]
    step = min(512, wide)

    def still(j):
        return (0, 0)

    def columns(size, place):
        return pl.BlockSpec((step, size), lambda j: (j, place))

    return pl.pallas_call(
        functools.partial(project_kernel, len(lhs), rows),
        grid=(wide // step,),
        out_shape=(jax.ShapeDtypeStruct((rows, wide), BF16),) * count,
        in_specs=[pl.BlockSpec(memory_space=SMEM)]
        + [pl.BlockSpec(a.shape, still) for a in lhs]
        + [columns(a.shape[1], place) for a, place in zip(lhs, places)],
        out_specs=(pl.BlockSpec((rows, step), lambda j: (0, j)),) * count,
        scratch_shapes=[pltpu.VMEM((tall, step), F32)],
        compiler_params=params(),
        name="project",
    )(starts, *lhs, *rhs)


def mlp_kernel(count, *refs):
    seconds, branch_grads = refs[:count], refs[count : 2 * count]
    w_gate, w_up, w_down = refs[2 * count : 2 * count + 3]
    outs = refs[2 * count + 3 :]
    for m in range(count):
        hidden, gate_back, up_back = outs[3 * m : 3 * m + 3]
        seen = seconds[m][...]
        gate = nn(seen, w_gate[...])
        up = nn(seen, w_up[...])
        grad = nn(branch_grads[m][...], w_down[...])
        sigma = 1.0 / (1.0 + jnp.exp(-gate))
        silu = gate * sigma
        hidden[...] = (silu * up).astype(BF16)
        up_back[...] = (grad * silu).astype(BF16)
        gate_back[...] = (grad * up * (sigma + silu * (1.0 - sigma))).astype(BF16)


def mlp(seconds, branch_grads, weight):
    count = len(seconds)
    tall, width = seconds[0].shape
    units = weight.shape[1] // 3
    step = min(256, units)
    steps = units // step
    whole = pl.BlockSpec((tall, width), lambda j: (0, 0), pipeline_mode=pl.Buffered(1))
    part = pl.BlockSpec((tall, step), lambda j: (0, j))
    shape = jax.ShapeDtypeStruct((tall, units), BF16)
    return pl.pallas_call(
        functools.partial(mlp_kernel, count),
        grid=(steps,),
        out_shape=(shape,) * (3 * count),
        in_specs=[whole] * (2 * count)
        + [
            pl.BlockSpec((width, step), lambda j, k=k: (0, k * steps + j)) for k in range(3)
        ],
        out_specs=(part,) * (3 * count),
        compiler_params=params(),
        name="mlp",
    )(*seconds, *branch_grads, weight, weight, weight)


def grads_kernel(plan, *refs):
    out = refs[-1]
    start = 0
    for pairs in plan:
        value = None
        for a, b in pairs:
            term = tn(refs[a][...], refs[b][...])
            value = term if value is None else value + term
        value = value.astype(BF16).reshape(out.shape[0], out.shape[1], value.shape[1])
        out[:, :, start : start + value.shape[2]] = value
        start += value.shape[2]


def weight_grads(products, count):
    arrays = []
    specs = []
    plan = []
    side = 0
    slab = products[0][0][0].shape[1] // count
    step = max(slab, 256)

    def place(array, cut):
        for i, known in enumerate(arrays):
            if known is array:
                return i
        tall, wide = array.shape
        if cut:
            specs.append(pl.BlockSpec((tall, step), lambda j: (0, j)))
        else:
            specs.append(
                pl.BlockSpec((tall, wide), lambda j: (0, 0), pipeline_mode=pl.Buffered(1))
            )
        arrays.append(array)
        return len(arrays) - 1

    for lhs, rhs in products:
        plan.append([(place(a, True), place(b, False)) for a, b in zip(lhs, rhs)])
        side += rhs[0].shape[1]
    return pl.pallas_call(
        functools.partial(grads_kernel, plan),
        grid=(count * slab // step,),
        out_shape=jax.ShapeDtypeStruct((count, slab, side), BF16),
        in_specs=specs,
        out_specs=pl.BlockSpec((step // slab, slab, side), lambda j: (j, 0, 0)),
        compiler_params=params(),
        name="grads",
    )(*arrays)


def turn(values, cosines, sines):
    lane = lax.broadcasted_iota(jnp.int32, values.shape, 1)
    other = jnp.where(
        lane % HEAD_DIM < HEAD_DIM // 2,
        pltpu.roll(values, 128 - HEAD_DIM // 2, 1),
        pltpu.roll(values, HEAD_DIM // 2, 1),
    )
    return values * cosines + other * sines


def head_block(values, head, high):
    tile = values[:, (head // 2) * 128 : (head // 2 + 1) * 128]
    if (head % 2 == 1) != high:
        tile = pltpu.roll(tile, HEAD_DIM, 1)
    lane = lax.broadcasted_iota(jnp.int32, tile.shape, 1)
    inside = (lane >= HEAD_DIM) if high else (lane < HEAD_DIM)
    return jnp.where(inside, tile, 0.0)


def bias_of(m, rows, j, length):
    seen = m * rows + (j + 1) * BLOCK
    first = m * rows if m else seen - BLOCK
    key = first + lax.broadcasted_iota(jnp.int32, (seen - first, BLOCK), 0)
    query = m * rows + j * BLOCK + lax.broadcasted_iota(jnp.int32, (seen - first, BLOCK), 1)
    return first, seen, jnp.where((key <= query) & (key < length), 0.0, NEGATIVE)


def scores_of(keys, query, bias, first, seen):
    scores = nt(keys[:seen], query)
    if first == 0:
        return scores + bias
    return jnp.concatenate([scores[:first], scores[first:] + bias], 0)


def forward_kernel(m, heads, lengths, *refs):
    tokens, weight, cos_q, sin_q, cos_k, sin_k = refs[:6]
    refs = refs[6:]
    if m:
        before, refs = refs[0], refs[1:]
    queries, pairs, log_total, mixed, factors, flipped = refs
    rows = tokens.shape[0]
    length = lengths[0]
    wide = tokens[...].astype(F32)
    factor = lax.rsqrt(jnp.mean(wide * wide, -1, keepdims=True) + EPS)
    factors[...] = jnp.broadcast_to(factor, (rows, 128))
    qkv = nn(tokens[...], weight[...]) * factor
    parts = []
    for i in range(heads // 2):
        parts.append(turn(qkv[:, i * 128 : (i + 1) * 128], cos_q[...], sin_q[...]))
    query = jnp.concatenate(parts, 1).astype(BF16).astype(F32) * MULT
    queries[...] = query.astype(BF16)
    pair = turn(qkv[:, heads * HEAD_DIM :], cos_k[...], sin_k[...]).astype(BF16)
    pairs[...] = pair
    if m:
        pair = jnp.concatenate([before[...], pair], 0)
    upright = jnp.transpose(pair.astype(F32)).astype(BF16)[HEAD_DIM:]
    for j in range(rows // BLOCK):
        first, seen, bias = bias_of(m, rows, j, length)
        here = slice(j * BLOCK, (j + 1) * BLOCK)
        for h in range(heads):
            q = head_block(query[here], h, False).astype(BF16)
            scores = scores_of(pair, q, bias, first, seen)
            top = jnp.max(scores, 0, keepdims=True)
            expd = jnp.exp(scores - top)
            total = jnp.sum(expd, 0, keepdims=True)
            log_total[0, h : h + 1, here] = top + jnp.log(total)
            out = nn(upright[:, :seen], expd.astype(BF16)) / total
            flipped[h * HEAD_DIM : (h + 1) * HEAD_DIM, here] = out
    mixed[...] = jnp.transpose(flipped[...]).astype(BF16)


def attend(m, heads, lengths, tokens, weight, tables, before):
    rows, width = tokens.shape
    q_width = heads * HEAD_DIM
    groups = weight.shape[1] // (2 * q_width + 128)

    def block(lanes):
        return pl.BlockSpec((rows, lanes), lambda g: (0, g))

    def whole(lanes, place=0):
        return pl.BlockSpec((rows, lanes), lambda g: (place, 0))

    return pl.pallas_call(
        functools.partial(forward_kernel, m, heads),
        grid=(groups,),
        out_shape=(
            jax.ShapeDtypeStruct((rows, groups * q_width), BF16),
            jax.ShapeDtypeStruct((rows, groups * 128), BF16),
            jax.ShapeDtypeStruct((groups, heads, rows), F32),
            jax.ShapeDtypeStruct((rows, groups * q_width), BF16),
            jax.ShapeDtypeStruct((rows, 128), F32),
        ),
        in_specs=[
            pl.BlockSpec(memory_space=SMEM),
            whole(width),
            pl.BlockSpec((width, q_width + 128), lambda g: (0, g)),
        ]
        + [whole(128, m)] * 4
        + ([block(128)] if m else []),
        out_specs=(
            block(q_width),
            block(128),
            pl.BlockSpec((1, heads, rows), lambda g: (g, 0, 0)),
            block(q_width),
            whole(128),
        ),
        scratch_shapes=[pltpu.VMEM((q_width, rows), F32)],
        compiler_params=params(),
        name="attend",
    )(lengths, tokens, weight, *tables, *([before] if m else []))


def backward_kernel(m, heads, last, lengths, *refs):
    grad, w_out, queries, pairs, log_total, factors = refs[:6]
    cos_q, sin_q, cos_k, sin_k = refs[6:10]
    refs = refs[10:]
    if m:
        before, refs = refs[0], refs[1:]
    if not last:
        later, refs = refs[0], refs[1:]
    back, scaled_back, refs = refs[0], refs[1], refs[2:]
    if m:
        earlier, refs = refs[0], refs[1:]
    flipped, pair_grad = refs
    rows = grad.shape[0]
    q_width = heads * HEAD_DIM
    length = lengths[0]
    mixed_grad = nn(grad[...], w_out[...]).astype(BF16).astype(F32)
    query = queries[...].astype(F32)
    pair = pairs[...]
    if m:
        pair = jnp.concatenate([before[...], pair], 0)
    upright = jnp.transpose(pair.astype(F32)).astype(BF16)[:HEAD_DIM]
    pair_grad[...] = jnp.zeros_like(pair_grad)
    if not last:
        pair_grad[m * rows :, :] = later[...]
    for j in range(rows // BLOCK):
        first, seen, bias = bias_of(m, rows, j, length)
        here = slice(j * BLOCK, (j + 1) * BLOCK)
        for h in range(heads):
            q = head_block(query[here], h, False).astype(BF16)
            g = head_block(mixed_grad[here], h, True).astype(BF16)
            scores = scores_of(pair, q, bias, first, seen)
            probs = jnp.exp(scores - log_total[0, h : h + 1, here])
            prob_grad = nt(pair[:seen], g)
            inner = jnp.sum(probs * prob_grad, 0, keepdims=True)
            score_grad = (probs * (prob_grad - inner)).astype(BF16)
            pair_grad[:seen, :] += nn(score_grad, q) + nn(probs.astype(BF16), g)
            flipped[h * HEAD_DIM : (h + 1) * HEAD_DIM, here] = nn(upright[:, :seen], score_grad)
    query_grad = jnp.transpose(flipped[...]) * MULT
    parts = []
    for i in range(heads // 2):
        parts.append(turn(query_grad[:, i * 128 : (i + 1) * 128], cos_q[...], -sin_q[...]))
    parts.append(turn(pair_grad[m * rows :, :], cos_k[...], -sin_k[...]))
    found = jnp.concatenate(parts, 1).astype(BF16)
    back[...] = found
    scaled_back[...] = (found.astype(F32) * factors[:, :1]).astype(BF16)
    if m:
        earlier[...] = pair_grad[: m * rows, :]


def attend_back(m, heads, last, lengths, grad, weight, kept, tables, before, later):
    rows, width = grad.shape
    q_width = heads * HEAD_DIM
    side = q_width + 128
    queries, pairs, log_total, factors = kept
    groups = queries.shape[1] // q_width
    first = groups * side // q_width

    def block(lanes):
        return pl.BlockSpec((rows, lanes), lambda g: (0, g))

    def whole(lanes, place=0):
        return pl.BlockSpec((rows, lanes), lambda g: (place, 0))

    back = jax.ShapeDtypeStruct((rows, groups * side), BF16)
    earlier = (jax.ShapeDtypeStruct((rows, groups * 128), F32),) if m else ()
    return pl.pallas_call(
        functools.partial(backward_kernel, m, heads, last),
        grid=(groups,),
        out_shape=(back, back) + earlier,
        in_specs=[
            pl.BlockSpec(memory_space=SMEM),
            whole(width),
            pl.BlockSpec((width, q_width), lambda g: (0, first + g)),
            block(q_width),
            block(128),
            pl.BlockSpec((1, heads, rows), lambda g: (g, 0, 0)),
            whole(128),
        ]
        + [whole(128, m)] * 4
        + ([block(128)] if m else [])
        + ([] if last else [block(128)]),
        out_specs=(block(side),) * 2 + ((block(128),) if m else ()),
        scratch_shapes=[
            pltpu.VMEM((q_width, rows), F32),
            pltpu.VMEM(((m + 1) * rows, 128), F32),
        ],
        compiler_params=params(),
        name="attend_back",
    )(
        lengths,
        grad,
        weight,
        queries,
        pairs,
        log_total,
        factors,
        *tables,
        *([before] if m else []),
        *([] if last else [later]),
    )


def norm_back(values, factor, weighted):
    scaled = values * factor
    product = weighted * scaled
    back = factor * (weighted - scaled * jnp.mean(product, -1, keepdims=True))
    return back, jnp.sum(product, 0)


def shards(
    tokens,
    lengths,
    w_query,
    w_key,
    w_value,
    w_out,
    w_gate,
    w_up,
    w_down,
    gain_attn,
    gain_mlp,
    cotangent,
):
    hi_count = lax.axis_size("hi")
    slabs = hi_count * 2
    z = lax.axis_index("hi")
    x = lax.axis_index("lo")
    y = lax.axis_index("y")
    c = lax.axis_index("core")
    t = y * 2 + c
    micro_count = tokens.shape[1]
    rows = tokens.shape[2]
    query_rows = rows * 4
    total_rows = micro_count * query_rows
    depth = w_query.shape[0]
    width = depth * slabs
    groups = w_key.shape[1] // HEAD_DIM
    heads = w_query.shape[1] // HEAD_DIM // groups
    q_width = heads * HEAD_DIM
    side = q_width + 128
    attn_column = gain_attn.astype(F32)[:, None]
    mlp_column = gain_mlp.astype(F32)[:, None]

    near = [y * 2 + x, y * 2 + 1 - x]
    far = [(1 - y) * 2 + x, (1 - y) * 2 + 1 - x]
    same = (x == c).astype(jnp.int32)
    starts = jnp.where(
        x == c,
        jnp.stack([far[0], far[1], near[1], near[0]]),
        jnp.stack([near[0], near[1], far[0], far[1]]),
    )
    starts = jnp.append(starts * rows, same).astype(jnp.int32)
    length = lengths[0]
    work_length = trade(lengths)

    order = Order()

    def gather_z(piece):
        return lax.all_gather(piece, ("hi", "core"), axis=0, tiled=True)

    def collect_z(products):
        lhs, rhs = products[0]

        def run(first):
            return weight_grads([(lhs, [first] + list(rhs[1:]))] + products[1:], slabs)

        total = order(run, rhs[0])
        return lax.psum_scatter(total, ("hi", "core"), scatter_dimension=0, tiled=False)

    def scaled(weight, column):
        return (weight.astype(F32) * column).astype(BF16)

    out_turned = jnp.transpose(w_out)
    down_turned = jnp.transpose(w_down)

    def attention_columns():
        parts = []
        for g in range(groups):
            parts.append(w_query[:, g * q_width : (g + 1) * q_width])
            parts.append(w_key[:, g * HEAD_DIM : (g + 1) * HEAD_DIM])
            parts.append(w_value[:, g * HEAD_DIM : (g + 1) * HEAD_DIM])
        return jnp.concatenate([scaled(jnp.concatenate(parts, 1), attn_column), out_turned], 1)

    def unit_columns(h):
        n = w_gate.shape[1] // 2
        here = slice(h * n, (h + 1) * n)
        return jnp.concatenate(
            [
                scaled(w_gate[:, here], mlp_column),
                scaled(w_up[:, here], mlp_column),
                down_turned[:, here],
            ],
            1,
        )

    half_dim = HEAD_DIM // 2
    freqs = jnp.exp(-jnp.log(THETA) * jnp.arange(half_dim).astype(F32) / half_dim)
    angles = jnp.arange(total_rows).astype(F32)[:, None] * freqs[None, :]
    cosines, sines = jnp.cos(angles), jnp.sin(angles)
    cos_head = jnp.concatenate([cosines, cosines], 1)
    sin_head = jnp.concatenate([-sines, sines], 1)
    tables = (
        jnp.concatenate([cos_head, cos_head], 1),
        jnp.concatenate([sin_head, sin_head], 1),
        jnp.concatenate([cos_head, jnp.ones_like(cos_head)], 1),
        jnp.concatenate([sin_head, jnp.zeros_like(sin_head)], 1),
    )

    valids = []
    upstreams = []
    streams = []
    attn_factors = []
    for m in range(micro_count):
        place = m * query_rows + t * rows + jnp.arange(rows)
        valid = (place < length).astype(F32)[:, None]
        valids.append(valid)
        upstreams.append(valid * cotangent[0, m].astype(F32))
        stream = tokens[0, m].astype(F32)
        streams.append(stream)
        attn_factors.append(lax.rsqrt(jnp.mean(stream * stream, -1, keepdims=True) + EPS))

    attn_piece = trade(after(attention_columns(), work_length))
    attn_weight = gather_z(attn_piece)
    here = [send_rows(after(tokens[0, 0], attn_piece))]
    units_piece = [trade(after(unit_columns(0), attn_piece))]
    tokens_all = [order(join_rows, here[0], starts)]
    here.append(send_rows(after(tokens[0, 1], attn_piece)))
    units_weight = [gather_z(order(lambda a: a, units_piece[0]))]

    def forward(m, rows_all):
        return attend(
            m, heads, work_length, rows_all, attn_weight, tables, found[0][1] if m else None
        )

    out_columns = attn_weight[:, groups * side :]

    def out_project(mixed):
        return project(starts, [mixed], [out_columns], [0])

    def enter(m, parts):
        middle = streams[m] + RESIDUAL * add_sums(parts)
        factor = lax.rsqrt(jnp.mean(middle * middle, -1, keepdims=True) + EPS)
        return (middle * factor).astype(BF16), middle, factor

    found = [order(lambda a: forward(0, a), tokens_all[0])]
    sums = [send_sums(order(out_project, found[0][3]))]
    tokens_all.append(order(join_rows, here[1], starts))
    branch_rows = [(RESIDUAL * upstreams[m]).astype(BF16) for m in range(micro_count)]
    branch = [send_rows(after(branch_rows[0], tokens_all[0]))]
    branch.append(send_rows(after(branch_rows[1], found[0][0])))
    branch_grads = [order(join_rows, branch[0], starts)]
    units_piece.append(trade(after(unit_columns(1), found[0][0])))
    found.append(order(lambda a: forward(1, a), tokens_all[1]))
    sums.append(send_sums(order(out_project, found[1][3])))
    entered = [order(lambda a: enter(0, a), sums[0])]
    here = [send_rows(entered[0][0])]
    branch_grads.append(order(join_rows, branch[1], starts))
    units_weight.append(gather_z(order(lambda a: a, units_piece[1])))
    second_all = [order(join_rows, here[0], starts)]
    entered.append(order(lambda a: enter(1, a), sums[1]))
    here.append(send_rows(entered[1][0]))
    second_all.append(order(join_rows, here[1], starts))
    middles = [e[1] for e in entered]
    mlp_factors = [e[2] for e in entered]

    hiddens, gate_backs, up_backs, unit_grads = [], [], [], []
    def back_project(m):
        def run(first):
            return project(
                starts,
                [first, up_backs[0][m], gate_backs[1][m], up_backs[1][m]],
                [units_weight[0], units_weight[0], units_weight[1], units_weight[1]],
                [0, 1, 0, 1],
            )

        return order(run, gate_backs[0][m])

    def branch_project(m):
        def run(first):
            return project(starts, [first, hiddens[1][m]], units_weight, [2, 2])

        return order(run, hiddens[0][m])

    def leave(m, parts):
        back, gain_part = norm_back(middles[m], mlp_factors[m], add_sums(parts))
        middle_grad = upstreams[m] + back
        return (RESIDUAL * middle_grad).astype(BF16), middle_grad, gain_part

    def unit_step(h):
        made = order(lambda a: mlp(a, branch_grads, units_weight[h]), second_all)
        hiddens.append(made[0::3])
        gate_backs.append(made[1::3])
        up_backs.append(made[2::3])
        return [
            (second_all, gate_backs[h]),
            (second_all, up_backs[h]),
            (branch_grads, hiddens[h]),
        ]

    products = unit_step(0)
    unit_grads.append(collect_z(products))
    unit_grads.append(collect_z(unit_step(1)))
    sums = [None, send_sums(back_project(1))]
    sums[0] = send_sums(back_project(0))
    left = [None, order(lambda a: leave(1, a), sums[1])]
    here = [None, send_rows(left[1][0])]
    left[0] = order(lambda a: leave(0, a), sums[0])
    here[0] = send_rows(left[0][0])
    attn_grads = [None, order(join_rows, here[1], starts)]

    def back_attend(m, grad, later):
        queries, pairs, log_total, _, factors = found[m]
        return attend_back(
            m,
            heads,
            m == micro_count - 1,
            work_length,
            grad,
            attn_weight,
            (queries, pairs, log_total, factors),
            tables,
            found[0][1] if m else None,
            later,
        )

    def normed_project(back):
        return project(starts, [back], [attn_weight], [0])

    def end(m, parts):
        back, gain_part = norm_back(streams[m], attn_factors[m], add_sums(parts))
        return left[m][1] + back, gain_part

    def finish(m, parts):
        return valids[m] * (middles[m] + RESIDUAL * add_sums(parts))

    back1, scaled1, later = order(lambda a: back_attend(1, a, None), attn_grads[1])
    sums[1] = send_sums(order(normed_project, back1))
    attn_grads[0] = order(join_rows, here[0], starts)
    unit_parts = [trade(order(lambda a: a, unit_grads[0]))]
    back0, scaled0 = order(lambda a: back_attend(0, a, later), attn_grads[0])
    sums[0] = send_sums(order(normed_project, back0))
    unit_parts[0] = order(lambda a: a, unit_parts[0])
    branch = [None, send_sums(branch_project(1))]
    branch[0] = send_sums(branch_project(0))
    grad_attn = collect_z(
        [(tokens_all, [scaled0, scaled1]), (attn_grads, [found[0][3], found[1][3]])]
    )
    ended = [None, order(lambda a: end(1, a), sums[1])]
    ended[0] = order(lambda a: end(0, a), sums[0])
    attn_gain_total = ended[0][1] + ended[1][1]
    mlp_gain_total = left[0][2] + left[1][2]
    input_parts = [ended[0][0], ended[1][0]]
    both = jnp.stack([attn_gain_total, mlp_gain_total], 0)

    def halve(both, bit, swap):
        n = both.shape[1] // 2
        keep = lax.dynamic_slice_in_dim(both, bit * n, n, 1)
        send = lax.dynamic_slice_in_dim(both, (1 - bit) * n, n, 1)
        return order(lambda a: keep + a, swap(send))

    step = hi_count // 2
    while step >= 1:
        both = halve(both, (z // step) % 2, lambda v, s=step: swap_z(v, s, hi_count))
        step //= 2
    for bit, axis in ((x, "lo"), (y, "y"), (c, "core")):
        both = halve(both, bit, lambda v, a=axis: lax.ppermute(v, a, [(0, 1), (1, 0)]))
    n = both.shape[1]
    gains_here = jnp.stack([gain_attn, gain_mlp], 0).astype(F32)

    both = order(lambda a: a / lax.dynamic_slice_in_dim(gains_here, t * n, n, 1), both)
    outputs = [None, order(lambda a: finish(1, a), branch[1])]
    outputs[0] = order(lambda a: finish(0, a), branch[0])

    unit_parts.append(trade(order(lambda a: a, unit_grads[1])))
    u = unit_parts[0].shape[1] // 3

    def units(k):
        return jnp.concatenate([part[:, k * u : (k + 1) * u] for part in unit_parts], 1).astype(F32)

    unit_outs = order(
        lambda a: (units(0) * a, units(1) * a, jnp.transpose(units(2))), mlp_column
    )
    attn_part = trade(order(lambda a: a, grad_attn)).astype(F32)
    qkv_part = attn_part[:, : groups * side] * attn_column

    def columns(first, last):
        return jnp.concatenate(
            [qkv_part[:, g * side + first : g * side + last] for g in range(groups)], 1
        )

    return (
        jnp.stack(outputs, 0)[None],
        jnp.stack(input_parts, 0)[None],
        columns(0, q_width),
        columns(q_width, q_width + HEAD_DIM),
        columns(q_width + HEAD_DIM, side),
        jnp.transpose(attn_part[:, groups * side :]),
        *unit_outs,
        both[0],
        both[1],
    )


def solution(mesh):
    fsdp_count, tensor_count = mesh.shape["fsdp"], mesh.shape["tensor"]
    split = Mesh(
        mesh.devices.reshape(fsdp_count // 2, 2, tensor_count // 2, 2),
        ("hi", "lo", "y", "core"),
    )
    fsdp = ("hi", "lo")
    tensor = ("y", "core")
    rows = P(fsdp, None, tensor, None)
    inward = P(fsdp, tensor)
    outward = P(tensor, fsdp)
    whole = P(("hi", "lo", "y", "core"))
    weights = (inward, inward, inward, outward, inward, inward, outward)
    return jax.shard_map(
        shards,
        mesh=split,
        in_specs=(rows, P(fsdp)) + weights + (P(fsdp), P(fsdp), rows),
        out_specs=(rows, rows) + weights + (whole, whole),
        check_vma=False,
    )
```

time: 1950 us -> 717 us (0.37)
  waiting for transfers between devices: 1410 us -> 185 us
  matrix products: 301 us -> 0 us
  Pallas kernels: 0 us -> 249 us
  starting transfers between devices: 3.27 us -> 178 us
  blocking collectives: 125 us -> 0 us
    reduce_scatter x15 -> x3, waiting for transfers between devices: 870 us -> 0.02 us  [collect_z(): lax.psum_scatter(total, ('hi', 'core'), scatter_dimension=0, tiled=False)]
    all_gather x13 -> x3, waiting for transfers between devices: 537 us -> 0.04 us  [gather_z(): return lax.all_gather(piece, ('hi', 'core'), axis=0, tiled=True)]
    dot_general x54 -> x0, matrix products: 301 us -> none  [the longest x2 24.1 us: shards(): jnp.einsum('qd,fd->qf', branch_grad, down_weight, preferred_element_type=...]
    pallas_call x0 -> x25, Pallas kernels: none -> 249 us  [the longest x8 67.8 us: project(): pl.pallas_call(functools.partial(project_kernel, len(lhs), rows), grid=(w...]
    ppermute x0 -> x92, waiting for transfers between devices: none -> 185 us  [the longest x87 181 us: send(): return lax.ppermute(values, ('lo', 'y', 'core'), pairs)]
    ppermute x0 -> x92, starting transfers between devices: none -> 178 us  [the longest x87 173 us: send(): return lax.ppermute(values, ('lo', 'y', 'core'), pairs)]
    all_gather x4 -> x0, blocking collectives: 86.2 us -> none  [the longest x1 26.1 us: fetch(): lax.all_gather(w_value, 'fsdp', axis=0, tiled=True)]
    unnamed x1 -> x0, blocking collectives: 38.7 us -> none
  transfers between devices with their start and end apart: 28 -> 98, of which waited for: 24 -> 35; matrix products, arithmetic and copies ran while one was open for 14% -> 9% of each run, Pallas kernels for 0% -> 35%
where the time goes in v1:
time: 717 us; the launch traced here: 705 us
  Pallas kernels  249 us (35%)
  waiting for transfers between devices  185 us (26%)
  starting transfers between devices  178 us (25%)
  other arithmetic  55.8 us (8%)
  local copies, waits for them, and re-layouts  19.3 us (3%)
  between operations  17.8 us (2%)
    ppermute x87, waiting for transfers between devices, send(): return lax.ppermute(values, ('lo', 'y', 'core'), pairs)  181 us
    ppermute x87, starting transfers between devices, send(): return lax.ppermute(values, ('lo', 'y', 'core'), pairs)  173 us
    pallas_call x8, Pallas kernels, project(): pl.pallas_call(functools.partial(project_kernel, len(lhs), rows), grid=(w...  67.8 us
    pallas_call x3, Pallas kernels, weight_grads(): pl.pallas_call(functools.partial(grads_kernel, plan), grid=(count * slab...  50.8 us
    pallas_call x2, Pallas kernels, mlp(): pl.pallas_call(functools.partial(mlp_kernel, count), grid=(steps,), out_s...  39.9 us
    pallas_call x2, Pallas kernels, attend_back(): pl.pallas_call(functools.partial(backward_kernel, m, heads, last), grid=(...  33.1 us
    pallas_call x2, Pallas kernels, attend(): pl.pallas_call(functools.partial(forward_kernel, m, heads), grid=(groups,...  28.7 us
    pallas_call x8, Pallas kernels, join_rows(): pl.pallas_call(assemble_kernel, out_shape=jax.ShapeDtypeStruct((4 * rows,...  28.5 us
  transfers between devices with their start and end apart: 98, of which 35 were waited for; matrix products, arithmetic and copies ran while one was open for 9% of the time, Pallas kernels for 35%

profile of v1, /device:TPU:1, one launch (start us, length us, event | category | flops | bytes accessed | tf_op | source)
XLA Modules:
  0.0 705.5 jit_solution(5938247895761003366)
XLA Ops:
  7.2 4.5 collective-permute-start
  19.2 10.4 %collective-permute-done.1 = bf16[256,1280]{1,0:T(8,128)(2,1)S(1)} collective-permute-done((bf16[256,1280]{1,0:T(8,128)(2,1)S(1)}, bf16[256,1280]{1,0:T(8,128)(2,1)S(1)}, u32[]{:S(2)}, u32[]{:S(2)}) %collective-permute-start.1) | collective-permute-done | bytes 655392 | tf_op jit(solution)/shard_map/ppermute | solution.py:75
  39.8 3.1 collective-permute-start.4
  42.9 25.5 %collective-permute-done.2.refs_0_ = bf16[128,2048]{1,0:T(8,128)(2,1)} collective-permute-done((bf16[128,2048]{1,0:T(8,128)(2,1)}, bf16[128,2048]{1,0:T(8,128)(2,1)}, u32[]{:S(2)}, u32[]{:S(2)}) %collective-permute-start.2) | collective-permute-done | bytes 524320 | tf_op jit(solution)/shard_map/ppermute | solution.py:75
  68.5 3.1 collective-permute-start.5
  73.6 5.4 collective-permute-done.5.refs_3_
  79.0 3.2 collective-permute-done.6.refs_5_
  82.2 3.5 assemble.8.refs_0_
  92.1 3.9 collective-permute-start.15
  96.0 7.2 %collective-permute-done.13.refs_0_ = bf16[128,2048]{1,0:T(8,128)(2,1)} collective-permute-done((bf16[128,2048]{1,0:T(8,128)(2,1)}, bf16[128,2048]{1,0:T(8,128)(2,1)}, u32[]{:S(2)}, u32[]{:S(2)}) %collective-permute-start.13) | collective-permute-done | bytes 524320 | tf_op jit(solution)/shard_map/ppermute | solution.py:75
  107.6 3.2 collective-permute-start.19
  115.1 12.2 %attend.2 = (bf16[512,512]{1,0:T(8,128)(2,1)}, bf16[512,256]{1,0:T(8,128)(2,1)}, f32[2,4,512]{2,1,0:T(4,128)}, bf16[512,512]{1,0:T(8,128)(2,1)}, f32[512,128]{1,0:T(8,128)}) custom-call(s32[1]{0:T(128)S(6)} %select_n.165.lengths, bf16[512,2048]{1,0:T(8,128)(2,1)} %assemble.8.refs_0_, bf16[2048,1280]{1,0:T(8,128)(2,1)} %all-gather.4.cloned.1.call-done.refs_1_, ...), custom_call_target="tpu_custom_call" | custom-call | tf_op jit(solution)/shard_map/attend/pallas_call | solution.py:378
  130.4 5.0 project.8
  148.7 3.5 collective-permute-start.28
  160.4 3.6 assemble.9.refs_0_.refs_2_
  163.9 3.6 assemble.10.refs_2_.refs_6_
  167.5 16.5 %attend.3 = (bf16[512,512]{1,0:T(8,128)(2,1)}, bf16[512,256]{1,0:T(8,128)(2,1)}, f32[2,4,512]{2,1,0:T(4,128)}, bf16[512,512]{1,0:T(8,128)(2,1)}, f32[512,128]{1,0:T(8,128)}) custom-call(s32[1]{0:T(128)S(6)} %select_n.165.lengths, bf16[512,2048]{1,0:T(8,128)(2,1)} %assemble.9.refs_0_.refs_2_, bf16[2048,1280]{1,0:T(8,128)(2,1)} %all-gather.4.cloned.1.call-done.refs_1_, ...), custom_call_target="tpu_custom_call" | custom-call | tf_op jit(solution)/shard_map/attend/pallas_call | solution.py:378
  184.0 4.9 project.9
  198.3 3.8 collective-permute-done.32.refs_3_
  204.8 3.5 assemble.11.refs_3_.refs_8_
  220.2 4.0 collective-permute-start.25
  224.2 8.8 %collective-permute-done.23.refs_0_ = bf16[128,2048]{1,0:T(8,128)(2,1)S(1)} collective-permute-done((bf16[128,2048]{1,0:T(8,128)(2,1)S(1)}, bf16[128,2048]{1,0:T(8,128)(2,1)S(1)}, u32[]{:S(2)}, u32[]{:S(2)}) %collective-permute-start.23) | collective-permute-done | bytes 524320 | tf_op jit(solution)/shard_map/ppermute | solution.py:75
  240.8 4.5 collective-permute-done.26.refs_3_
  246.1 3.8 collective-permute-done.27.refs_5_
  249.9 3.5 assemble.12.refs_0_
  253.5 4.0 collective-permute-done.36
  258.7 3.6 collective-permute-start.41
  262.3 10.4 %collective-permute-done.39.refs_0_ = bf16[128,2048]{1,0:T(8,128)(2,1)S(1)} collective-permute-done((bf16[128,2048]{1,0:T(8,128)(2,1)S(1)}, bf16[128,2048]{1,0:T(8,128)(2,1)S(1)}, u32[]{:S(2)}, u32[]{:S(2)}) %collective-permute-start.39) | collective-permute-done | bytes 524320 | tf_op jit(solution)/shard_map/ppermute | solution.py:75
  276.9 6.2 collective-permute-done.42.refs_3_
  286.3 3.6 assemble.13.refs_1_.refs_2_
  289.9 19.9 %mlp.2 = (bf16[512,1024]{1,0:T(8,128)(2,1)}, bf16[512,1024]{1,0:T(8,128)(2,1)}, bf16[512,1024]{1,0:T(8,128)(2,1)}, bf16[512,1024]{1,0:T(8,128)(2,1)}, bf16[512,1...) custom-call(bf16[512,2048]{1,0:T(8,128)(2,1)} %assemble.12.refs_0_, bf16[512,2048]{1,0:T(8,128)(2,1)} %assemble.13.refs_1_.refs_2_, ...), custom_call_target="tpu_custom_call" | custom-call | tf_op jit(solution)/shard_map/mlp/pallas_call | solution.py:233
  309.9 19.3 %grads.3 = bf16[8,256,3072]{2,1,0:T(8,128)(2,1)} custom-call(bf16[512,2048]{1,0:T(8,128)(2,1)} %assemble.12.refs_0_, bf16[512,1024]{1,0:T(8,128)(2,1)} %get-tuple-element.254.refs_1_.refs_0_, bf16[512,2048]{1,0:T(8,128)(2,1)} %assemble.13.refs_1_.refs_2_, bf16[512,1024]{1,0:T(8,128)(2,1)} %get-tuple-element.252.refs_3_.refs_0_, ...), custom_call_target="tpu_custom_call" | custom-call | tf_op jit(solution)/shard_map/grads/pallas_call | solution.py:285
  329.3 20.0 %mlp.3 = (bf16[512,1024]{1,0:T(8,128)(2,1)}, bf16[512,1024]{1,0:T(8,128)(2,1)}, bf16[512,1024]{1,0:T(8,128)(2,1)}, bf16[512,1024]{1,0:T(8,128)(2,1)}, bf16[512,1...) custom-call(bf16[512,2048]{1,0:T(8,128)(2,1)} %assemble.12.refs_0_, bf16[512,2048]{1,0:T(8,128)(2,1)} %assemble.13.refs_1_.refs_2_, ...), custom_call_target="tpu_custom_call" | custom-call | tf_op jit(solution)/shard_map/mlp/pallas_call | solution.py:233
  349.2 19.4 %grads.4 = bf16[8,256,3072]{2,1,0:T(8,128)(2,1)} custom-call(bf16[512,2048]{1,0:T(8,128)(2,1)} %assemble.12.refs_0_, bf16[512,1024]{1,0:T(8,128)(2,1)} %get-tuple-element.247.refs_1_.refs_2_, bf16[512,2048]{1,0:T(8,128)(2,1)} %assemble.13.refs_1_.refs_2_, bf16[512,1024]{1,0:T(8,128)(2,1)} %get-tuple-element.248.refs_3_.refs_2_, ...), custom_call_target="tpu_custom_call" | custom-call | tf_op jit(solution)/shard_map/grads/pallas_call | solution.py:285
  368.9 14.5 %project.10 = (bf16[128,2048]{1,0:T(8,128)(2,1)}, bf16[128,2048]{1,0:T(8,128)(2,1)}, bf16[128,2048]{1,0:T(8,128)(2,1)}, bf16[128,2048]{1,0:T(8,128)(2,1)}) custom-call(s32[5]{0:T(128)} %pad_add_fusion.starts, bf16[512,1024]{1,0:T(8,128)(2,1)} %get-tuple-element.252.refs_3_.refs_0_, bf16[512,1024]{1,0:T(8,128)(2,1)} %get-tuple-element.242.refs_5_.refs_1_, ...), custom_call_target="tpu_custom_call" | custom-call | tf_op jit(solution)/shard_map/project/pallas_call | solution.py:193
  383.3 14.5 %project.11 = (bf16[128,2048]{1,0:T(8,128)(2,1)}, bf16[128,2048]{1,0:T(8,128)(2,1)}, bf16[128,2048]{1,0:T(8,128)(2,1)}, bf16[128,2048]{1,0:T(8,128)(2,1)}) custom-call(s32[5]{0:T(128)} %pad_add_fusion.starts, bf16[512,1024]{1,0:T(8,128)(2,1)} %get-tuple-element.254.refs_1_.refs_0_, bf16[512,1024]{1,0:T(8,128)(2,1)} %get-tuple-element.241.refs_4_.refs_1_, ...), custom_call_target="tpu_custom_call" | custom-call | tf_op jit(solution)/shard_map/project/pallas_call | solution.py:193
  397.9 3.2 collective-permute-start.44
  401.1 3.1 collective-permute-start.45
  415.5 3.6 collective-permute-done.50
  421.4 7.1 %collective-permute-done.52 = bf16[128,2048]{1,0:T(8,128)(2,1)S(1)} collective-permute-done((bf16[128,2048]{1,0:T(8,128)(2,1)S(1)}, bf16[128,2048]{1,0:T(8,128)(2,1)S(1)}, u32[]{:S(2)}, u32[]{:S(2)}) %collective-permute-start.52) | collective-permute-done | bytes 524320 | tf_op jit(solution)/shard_map/ppermute | solution.py:75
  428.5 9.1 %collective-permute-done.51 = bf16[128,2048]{1,0:T(8,128)(2,1)S(1)} collective-permute-done((bf16[128,2048]{1,0:T(8,128)(2,1)S(1)}, bf16[128,2048]{1,0:T(8,128)(2,1)S(1)}, u32[]{:S(2)}, u32[]{:S(2)}) %collective-permute-start.51) | collective-permute-done | bytes 524320 | tf_op jit(solution)/shard_map/ppermute | solution.py:75
  443.3 3.8 collective-permute-start.60
  449.2 3.1 collective-permute-start.62
  453.6 6.8 collective-permute-done.54.refs_0_
  460.4 5.1 collective-permute-start.55
  472.6 3.5 assemble.14.refs_0_.refs_6_
  476.2 19.8 %attend_back.2 = (bf16[512,768]{1,0:T(8,128)(2,1)}, bf16[512,768]{1,0:T(8,128)(2,1)}, f32[512,256]{1,0:T(8,128)}) custom-call(s32[1]{0:T(128)S(6)} %select_n.165.lengths, bf16[512,2048]{1,0:T(8,128)(2,1)} %assemble.14.refs_0_.refs_6_, bf16[2048,1280]{1,0:T(8,128)(2,1)} %all-gather.4.cloned.1.call-done.refs_1_, bf16[512,512]{1,0:T(8,128)(2,1)} %get-tuple-element.201.refs_2_, ...), custom_call_target="tpu_custom_call" | custom-call | tf_op jit(solution)/shard_map/attend_back/pallas_call | solution.py:473
  495.9 5.6 project.12
  501.5 5.5 collective-permute-start.80
  510.9 3.6 assemble.15.refs_0_.refs_4_
  518.2 13.4 %attend_back.3 = (bf16[512,768]{1,0:T(8,128)(2,1)}, bf16[512,768]{1,0:T(8,128)(2,1)}) custom-call(s32[1]{0:T(128)S(6)} %select_n.165.lengths, bf16[512,2048]{1,0:T(8,128)(2,1)} %assemble.15.refs_0_.refs_4_, bf16[2048,1280]{1,0:T(8,128)(2,1)} %all-gather.4.cloned.1.call-done.refs_1_, bf16[512,512]{1,0:T(8,128)(2,1)} %get-tuple-element.178.refs_2_, ...), custom_call_target="tpu_custom_call" | custom-call | tf_op jit(solution)/shard_map/attend_back/pallas_call | solution.py:473
  531.5 5.6 project.13
  537.2 3.2 collective-permute-start.75
  549.9 6.4 collective-permute-done.76
  559.5 8.8 %project.14 = (bf16[128,2048]{1,0:T(8,128)(2,1)}, bf16[128,2048]{1,0:T(8,128)(2,1)}, bf16[128,2048]{1,0:T(8,128)(2,1)}, bf16[128,2048]{1,0:T(8,128)(2,1)}) custom-call(s32[5]{0:T(128)} %pad_add_fusion.starts, bf16[512,1024]{1,0:T(8,128)(2,1)} %get-tuple-element.294.refs_9_.refs_0_, bf16[512,1024]{1,0:T(8,128)(2,1)} %get-tuple-element.251.refs_9_.refs_1_, ...), custom_call_target="tpu_custom_call" | custom-call | tf_op jit(solution)/shard_map/project/pallas_call | solution.py:193
  568.3 8.9 %project.15 = (bf16[128,2048]{1,0:T(8,128)(2,1)}, bf16[128,2048]{1,0:T(8,128)(2,1)}, bf16[128,2048]{1,0:T(8,128)(2,1)}, bf16[128,2048]{1,0:T(8,128)(2,1)}) custom-call(s32[5]{0:T(128)} %pad_add_fusion.starts, bf16[512,1024]{1,0:T(8,128)(2,1)} %get-tuple-element.296.refs_7_.refs_0_, bf16[512,1024]{1,0:T(8,128)(2,1)} %get-tuple-element.246.refs_7_.refs_1_, ...), custom_call_target="tpu_custom_call" | custom-call | tf_op jit(solution)/shard_map/project/pallas_call | solution.py:193
  577.2 12.1 %grads.5 = bf16[8,256,1280]{2,1,0:T(8,128)(2,1)} custom-call(bf16[512,2048]{1,0:T(8,128)(2,1)} %assemble.8.refs_0_, bf16[512,768]{1,0:T(8,128)(2,1)} %get-tuple-element.311.refs_1_, bf16[512,2048]{1,0:T(8,128)(2,1)} %assemble.9.refs_0_.refs_2_, bf16[512,768]{1,0:T(8,128)(2,1)} %get-tuple-element.312.refs_3_, bf16[512,2048]{1,0:T(8,128)(2,1)} %assemble.15.refs_0_.refs_4_, ...), custom_call_target="tpu_custom_call" | custom-call | tf_op jit(solution)/shard_map/grads/pallas_call | solution.py:285
  608.3 3.3 collective-permute-start.70
  616.2 6.7 collective-permute-start.65
  631.5 4.3 collective-permute-done.66
  639.0 9.5 %collective-permute-done.72 = bf16[128,2048]{1,0:T(8,128)(2,1)S(1)} collective-permute-done((bf16[128,2048]{1,0:T(8,128)(2,1)S(1)}, bf16[128,2048]{1,0:T(8,128)(2,1)S(1)}, u32[]{:S(2)}, u32[]{:S(2)}) %collective-permute-start.72) | collective-permute-done | bytes 524320 | tf_op jit(solution)/shard_map/ppermute | solution.py:75
  649.8 4.3 collective-permute-done.67
  659.2 18.3 %collective-permute-done.90 = bf16[256,3072]{1,0:T(8,128)(2,1)S(1)} collective-permute-done((bf16[256,3072]{1,0:T(8,128)(2,1)}, bf16[256,3072]{1,0:T(8,128)(2,1)S(1)}, u32[]{:S(2)}, u32[]{:S(2)}) %collective-permute-start.90) | collective-permute-done | bytes 1572896 | tf_op jit(solution)/shard_map/ppermute | solution.py:75
  686.9 6.2 collective-permute-done.91
  (402 shorter events, 203.9 us)
Async XLA Ops:
  7.2 107.9 %all-gather.4.cloned.1.call-start = ((), (), s32[]{:S(2)}) async-start(), calls=%async_computation.3 | async-start | bytes 5898240 | tf_op jit(solution)/shard_map/all_gather | solution.py:566
  30.6 259.4 %all-gather.6.cloned.1.call-start = ((), (), s32[]{:S(2)}) async-start(), calls=%async_computation.4 | async-start | bytes 14155776 | tf_op jit(solution)/shard_map/all_gather | solution.py:566
  35.0 50.7 %collective-permute-start.7 = (bf16[256,3072]{1,0:T(8,128)(2,1)S(1)}, bf16[256,3072]{1,0:T(8,128)(2,1)}, u32[]{:S(2)}, u32[]{:S(2)}) collective-permute-start(bf16[256,3072]{1,0:T(8,128)(2,1)S(1)} %pad_maximum_fusion), channel_id=1, source_target_pairs={{1,4},{3,6},{4,1},{6,3},{9,12},{11,14},{12,9},{14,11},{17,20},{19,... | collective-permute-start | bytes 4718600 | tf_op jit(solution)/shard_map/ppermute | solution.py:75
  38.1 30.4 %collective-permute-start.2 = (bf16[128,2048]{1,0:T(8,128)(2,1)}, bf16[128,2048]{1,0:T(8,128)(2,1)}, u32[]{:S(2)}, u32[]{:S(2)}) collective-permute-start(bf16[128,2048]{1,0:T(8,128)(2,1)} %get-tuple-element.173.refs_4_), channel_id=1, source_target_pairs={{1,4},{3,6},{4,1},{6,3},{0,2},{2,0},{5,7},{7,5},{9,12},{11,14},{12... | collective-permute-start | bytes 1572872 | tf_op jit(solution)/shard_map/ppermute | solution.py:75
  39.8 33.8 %collective-permute-start.3 = (bf16[128,2048]{1,0:T(8,128)(2,1)}, bf16[128,2048]{1,0:T(8,128)(2,1)}, u32[]{:S(2)}, u32[]{:S(2)}) collective-permute-start(bf16[128,2048]{1,0:T(8,128)(2,1)} %get-tuple-element.173.refs_4_), channel_id=1, source_target_pairs={{0,4},{2,6},{5,1},{7,3},{1,2},{3,0},{4,7},{6,5},{8,12},{10,14},{13... | collective-permute-start | bytes 1572872 | tf_op jit(solution)/shard_map/ppermute | solution.py:75
  39.8 33.8 %collective-permute-start.4 = (bf16[128,2048]{1,0:T(8,128)(2,1)}, bf16[128,2048]{1,0:T(8,128)(2,1)}, u32[]{:S(2)}, u32[]{:S(2)}) collective-permute-start(bf16[128,2048]{1,0:T(8,128)(2,1)} %get-tuple-element.173.refs_4_), channel_id=1, source_target_pairs={{1,0},{3,2},{4,5},{6,7},{9,8},{11,10},{12,13},{14,15},{17,16},{19,... | collective-permute-start | bytes 1572872 | tf_op jit(solution)/shard_map/ppermute | solution.py:75
  88.5 240.7 %all-gather.8.cloned.1.call-start = ((), (), s32[]{:S(2)}) async-start(), calls=%async_computation.6 | async-start | bytes 14155776 | tf_op jit(solution)/shard_map/all_gather | solution.py:566
  88.6 14.6 %collective-permute-start.13 = (bf16[128,2048]{1,0:T(8,128)(2,1)}, bf16[128,2048]{1,0:T(8,128)(2,1)}, u32[]{:S(2)}, u32[]{:S(2)}) collective-permute-start(bf16[128,2048]{1,0:T(8,128)(2,1)} %get-tuple-element.189.refs_4_), channel_id=1, source_target_pairs={{1,4},{3,6},{4,1},{6,3},{0,2},{2,0},{5,7},{7,5},{9,12},{11,14},{12... | collective-permute-start | bytes 1572872 | tf_op jit(solution)/shard_map/ppermute | solution.py:75
  89.6 17.2 %collective-permute-start.14 = (bf16[128,2048]{1,0:T(8,128)(2,1)}, bf16[128,2048]{1,0:T(8,128)(2,1)S(1)}, u32[]{:S(2)}, u32[]{:S(2)}) collective-permute-start(bf16[128,2048]{1,0:T(8,128)(2,1)} %get-tuple-element.189.refs_4_), channel_id=1, source_target_pairs={{0,4},{2,6},{5,1},{7,3},{1,2},{3,0},{4,7},{6,5},{8,12},{10,14},{13... | collective-permute-start | bytes 1572872 | tf_op jit(solution)/shard_map/ppermute | solution.py:75
  92.1 43.3 %collective-permute-start.15 = (bf16[128,2048]{1,0:T(8,128)(2,1)}, bf16[128,2048]{1,0:T(8,128)(2,1)}, u32[]{:S(2)}, u32[]{:S(2)}) collective-permute-start(bf16[128,2048]{1,0:T(8,128)(2,1)} %get-tuple-element.189.refs_4_), channel_id=1, source_target_pairs={{1,0},{3,2},{4,5},{6,7},{9,8},{11,10},{12,13},{14,15},{17,16},{19,... | collective-permute-start | bytes 1572872 | tf_op jit(solution)/shard_map/ppermute | solution.py:75
  103.2 35.0 %collective-permute-start.16 = (bf16[128,2048]{1,0:T(8,128)(2,1)}, bf16[128,2048]{1,0:T(8,128)(2,1)}, u32[]{:S(2)}, u32[]{:S(2)}) collective-permute-start(bf16[128,2048]{1,0:T(8,128)(2,1)} %collective-permute-done.13.refs_0_), channel_id=1, source_target_pairs={{1,3},{3,1},{4,6},{6,4},{9,11},{11,9},{12,14},{14,12},{17,19},{19,... | collective-permute-start | bytes 1572872 | tf_op jit(solution)/shard_map/ppermute | solution.py:75
  105.4 35.0 %collective-permute-start.17 = (bf16[128,2048]{1,0:T(8,128)(2,1)}, bf16[128,2048]{1,0:T(8,128)(2,1)}, u32[]{:S(2)}, u32[]{:S(2)}) collective-permute-start(bf16[128,2048]{1,0:T(8,128)(2,1)} %collective-permute-done.13.refs_0_), channel_id=1, source_target_pairs={{0,4},{2,6},{5,1},{7,3},{8,12},{10,14},{13,9},{15,11},{16,20},{18,... | collective-permute-start | bytes 1572872 | tf_op jit(solution)/shard_map/ppermute | solution.py:75
  106.7 35.0 %collective-permute-start.18 = (bf16[128,2048]{1,0:T(8,128)(2,1)}, bf16[128,2048]{1,0:T(8,128)(2,1)}, u32[]{:S(2)}, u32[]{:S(2)}) collective-permute-start(bf16[128,2048]{1,0:T(8,128)(2,1)} %get-tuple-element.196.refs_4_), channel_id=1, source_target_pairs={{1,4},{3,6},{4,1},{6,3},{0,2},{2,0},{5,7},{7,5},{9,12},{11,14},{12... | collective-permute-start | bytes 1572872 | tf_op jit(solution)/shard_map/ppermute | solution.py:75
  107.6 37.2 %collective-permute-start.19 = (bf16[128,2048]{1,0:T(8,128)(2,1)}, bf16[128,2048]{1,0:T(8,128)(2,1)}, u32[]{:S(2)}, u32[]{:S(2)}) collective-permute-start(bf16[128,2048]{1,0:T(8,128)(2,1)} %get-tuple-element.196.refs_4_), channel_id=1, source_target_pairs={{0,4},{2,6},{5,1},{7,3},{1,2},{3,0},{4,7},{6,5},{8,12},{10,14},{13... | collective-permute-start | bytes 1572872 | tf_op jit(solution)/shard_map/ppermute | solution.py:75
  146.2 42.7 %collective-permute-start.12 = (bf16[128,2048]{1,0:T(8,128)(2,1)}, bf16[128,2048]{1,0:T(8,128)(2,1)S(1)}, u32[]{:S(2)}, u32[]{:S(2)}) collective-permute-start(bf16[128,2048]{1,0:T(8,128)(2,1)} %get-tuple-element.182), channel_id=1, source_target_pairs={{0,1},{2,3},{5,4},{7,6},{8,9},{10,11},{13,12},{15,14},{16,17},{18,... | collective-permute-start | bytes 1572872 | tf_op jit(solution)/shard_map/ppermute | solution.py:75
  148.7 59.7 %collective-permute-start.28 = (bf16[256,3072]{1,0:T(8,128)(2,1)S(1)}, bf16[256,3072]{1,0:T(8,128)(2,1)S(1)}, u32[]{:S(2)}, u32[]{:S(2)}) collective-permute-start(bf16[256,3072]{1,0:T(8,128)(2,1)S(1)} %pad_maximum_fusion.1), channel_id=1, source_target_pairs={{1,4},{3,6},{4,1},{6,3},{9,12},{11,14},{12,9},{14,11},{17,20},{19,... | collective-permute-start | bytes 4718600 | tf_op jit(solution)/shard_map/ppermute | solution.py:75
  152.5 36.6 %collective-permute-start.11 = (bf16[128,2048]{1,0:T(8,128)(2,1)}, bf16[128,2048]{1,0:T(8,128)(2,1)S(1)}, u32[]{:S(2)}, u32[]{:S(2)}) collective-permute-start(bf16[128,2048]{1,0:T(8,128)(2,1)} %get-tuple-element.183), channel_id=1, source_target_pairs={{4,0},{6,2},{1,5},{3,7},{2,1},{0,3},{7,4},{5,6},{12,8},{14,10},{9,... | collective-permute-start | bytes 1572872 | tf_op jit(solution)/shard_map/ppermute | solution.py:75
  154.3 37.1 %collective-permute-start.29 = (bf16[128,2048]{1,0:T(8,128)(2,1)S(1)}, bf16[128,2048]{1,0:T(8,128)(2,1)}, u32[]{:S(2)}, u32[]{:S(2)}) collective-permute-start(bf16[128,2048]{1,0:T(8,128)(2,1)S(1)} %copy-done.14), channel_id=1, source_target_pairs={{1,4},{3,6},{4,1},{6,3},{0,2},{2,0},{5,7},{7,5},{9,12},{11,14},{12... | collective-permute-start | bytes 1572872 | tf_op jit(solution)/shard_map/ppermute | solution.py:75
  157.4 36.4 %collective-permute-start.10 = (bf16[128,2048]{1,0:T(8,128)(2,1)S(1)}, bf16[128,2048]{1,0:T(8,128)(2,1)S(1)}, u32[]{:S(2)}, u32[]{:S(2)}) collective-permute-start(bf16[128,2048]{1,0:T(8,128)(2,1)S(1)} %add_convert_fusion.7), channel_id=1, source_target_pairs={{4,1},{6,3},{1,4},{3,6},{2,0},{0,2},{7,5},{5,7},{12,9},{14,11},{9,... | collective-permute-start | bytes 1572872 | tf_op jit(solution)/shard_map/ppermute | solution.py:75
  209.7 304.9 %reduce-scatter.4.cloned.1.call-start = ((), (), s32[]{:S(2)}) async-start(), calls=%async_computation.5 | async-start | bytes 14155776 | tf_op jit(solution)/shard_map/reduce_scatter | solution.py:575
  211.5 21.5 %collective-permute-start.23 = (bf16[128,2048]{1,0:T(8,128)(2,1)S(1)}, bf16[128,2048]{1,0:T(8,128)(2,1)S(1)}, u32[]{:S(2)}, u32[]{:S(2)}) collective-permute-start(bf16[128,2048]{1,0:T(8,128)(2,1)S(1)} %multiply_convert_fusion.7.refs_4_), channel_id=1, source_target_pairs={{1,4},{3,6},{4,1},{6,3},{0,2},{2,0},{5,7},{7,5},{9,12},{11,14},{12... | collective-permute-start | bytes 1572872 | tf_op jit(solution)/shard_map/ppermute | solution.py:75
  214.5 21.5 %collective-permute-start.35 = (bf16[128,2048]{1,0:T(8,128)(2,1)}, bf16[128,2048]{1,0:T(8,128)(2,1)S(1)}, u32[]{:S(2)}, u32[]{:S(2)}) collective-permute-start(bf16[128,2048]{1,0:T(8,128)(2,1)} %get-tuple-element.223), channel_id=1, source_target_pairs={{3,1},{1,3},{6,4},{4,6},{11,9},{9,11},{14,12},{12,14},{19,17},{17,... | collective-permute-start | bytes 1572872 | tf_op jit(solution)/shard_map/ppermute | solution.py:75
  217.4 20.2 %collective-permute-start.38 = (bf16[128,2048]{1,0:T(8,128)(2,1)}, bf16[128,2048]{1,0:T(8,128)(2,1)S(1)}, u32[]{:S(2)}, u32[]{:S(2)}) collective-permute-start(bf16[128,2048]{1,0:T(8,128)(2,1)} %get-tuple-element.223), channel_id=1, source_target_pairs={{0,1},{2,3},{5,4},{7,6},{8,9},{10,11},{13,12},{15,14},{16,17},{18,... | collective-permute-start | bytes 1572872 | tf_op jit(solution)/shard_map/ppermute | solution.py:75
  218.7 21.8 %collective-permute-start.24 = (bf16[128,2048]{1,0:T(8,128)(2,1)S(1)}, bf16[128,2048]{1,0:T(8,128)(2,1)S(1)}, u32[]{:S(2)}, u32[]{:S(2)}) collective-permute-start(bf16[128,2048]{1,0:T(8,128)(2,1)S(1)} %multiply_convert_fusion.7.refs_4_), channel_id=1, source_target_pairs={{0,4},{2,6},{5,1},{7,3},{1,2},{3,0},{4,7},{6,5},{8,12},{10,14},{13... | collective-permute-start | bytes 1572872 | tf_op jit(solution)/shard_map/ppermute | solution.py:75
  220.2 20.6 %collective-permute-start.25 = (bf16[128,2048]{1,0:T(8,128)(2,1)S(1)}, bf16[128,2048]{1,0:T(8,128)(2,1)S(1)}, u32[]{:S(2)}, u32[]{:S(2)}) collective-permute-start(bf16[128,2048]{1,0:T(8,128)(2,1)S(1)} %multiply_convert_fusion.7.refs_4_), channel_id=1, source_target_pairs={{1,0},{3,2},{4,5},{6,7},{9,8},{11,10},{12,13},{14,15},{17,16},{19,... | collective-permute-start | bytes 1572872 | tf_op jit(solution)/shard_map/ppermute | solution.py:75
  236.0 14.0 %collective-permute-start.27 = (bf16[128,2048]{1,0:T(8,128)(2,1)S(1)}, bf16[128,2048]{1,0:T(8,128)(2,1)}, u32[]{:S(2)}, u32[]{:S(2)}) collective-permute-start(bf16[128,2048]{1,0:T(8,128)(2,1)S(1)} %collective-permute-done.23.refs_0_), channel_id=1, source_target_pairs={{0,4},{2,6},{5,1},{7,3},{8,12},{10,14},{13,9},{15,11},{16,20},{18,... | collective-permute-start | bytes 1572872 | tf_op jit(solution)/shard_map/ppermute | solution.py:75
  237.5 15.9 %collective-permute-start.37 = (bf16[128,2048]{1,0:T(8,128)(2,1)}, bf16[128,2048]{1,0:T(8,128)(2,1)S(1)}, u32[]{:S(2)}, u32[]{:S(2)}) collective-permute-start(bf16[128,2048]{1,0:T(8,128)(2,1)} %get-tuple-element.224), channel_id=1, source_target_pairs={{4,0},{6,2},{1,5},{3,7},{2,1},{0,3},{7,4},{5,6},{12,8},{14,10},{9,... | collective-permute-start | bytes 1572872 | tf_op jit(solution)/shard_map/ppermute | solution.py:75
  240.5 17.1 %collective-permute-start.36 = (bf16[128,2048]{1,0:T(8,128)(2,1)S(1)}, bf16[128,2048]{1,0:T(8,128)(2,1)S(1)}, u32[]{:S(2)}, u32[]{:S(2)}) collective-permute-start(bf16[128,2048]{1,0:T(8,128)(2,1)S(1)} %add_convert_fusion.6), channel_id=1, source_target_pairs={{4,1},{6,3},{1,4},{3,6},{2,0},{0,2},{7,5},{5,7},{12,9},{14,11},{9,... | collective-permute-start | bytes 1572872 | tf_op jit(solution)/shard_map/ppermute | solution.py:75
  258.2 14.6 %collective-permute-start.39 = (bf16[128,2048]{1,0:T(8,128)(2,1)S(1)}, bf16[128,2048]{1,0:T(8,128)(2,1)S(1)}, u32[]{:S(2)}, u32[]{:S(2)}) collective-permute-start(bf16[128,2048]{1,0:T(8,128)(2,1)S(1)} %multiply_convert_fusion.6.refs_4_), channel_id=1, source_target_pairs={{1,4},{3,6},{4,1},{6,3},{0,2},{2,0},{5,7},{7,5},{9,12},{11,14},{12... | collective-permute-start | bytes 1572872 | tf_op jit(solution)/shard_map/ppermute | solution.py:75
  258.7 18.1 %collective-permute-start.40 = (bf16[128,2048]{1,0:T(8,128)(2,1)S(1)}, bf16[128,2048]{1,0:T(8,128)(2,1)S(1)}, u32[]{:S(2)}, u32[]{:S(2)}) collective-permute-start(bf16[128,2048]{1,0:T(8,128)(2,1)S(1)} %multiply_convert_fusion.6.refs_4_), channel_id=1, source_target_pairs={{0,4},{2,6},{5,1},{7,3},{1,2},{3,0},{4,7},{6,5},{8,12},{10,14},{13... | collective-permute-start | bytes 1572872 | tf_op jit(solution)/shard_map/ppermute | solution.py:75
  258.7 18.2 %collective-permute-start.41 = (bf16[128,2048]{1,0:T(8,128)(2,1)S(1)}, bf16[128,2048]{1,0:T(8,128)(2,1)S(1)}, u32[]{:S(2)}, u32[]{:S(2)}) collective-permute-start(bf16[128,2048]{1,0:T(8,128)(2,1)S(1)} %multiply_convert_fusion.6.refs_4_), channel_id=1, source_target_pairs={{1,0},{3,2},{4,5},{6,7},{9,8},{11,10},{12,13},{14,15},{17,16},{19,... | collective-permute-start | bytes 1572872 | tf_op jit(solution)/shard_map/ppermute | solution.py:75
  329.2 326.2 %reduce-scatter.8.cloned.1.call-start = ((), (), s32[]{:S(2)}) async-start(), calls=%async_computation.8 | async-start | bytes 14155776 | tf_op jit(solution)/shard_map/reduce_scatter | solution.py:575
  368.6 312.3 %reduce-scatter.6.cloned.1.call-start = ((), (), s32[]{:S(2)}) async-start(), calls=%async_computation.7 | async-start | bytes 5898240 | tf_op jit(solution)/shard_map/reduce_scatter | solution.py:575
  405.6 13.6 %collective-permute-start.50 = (bf16[128,2048]{1,0:T(8,128)(2,1)S(1)}, bf16[128,2048]{1,0:T(8,128)(2,1)S(1)}, u32[]{:S(2)}, u32[]{:S(2)}) collective-permute-start(bf16[128,2048]{1,0:T(8,128)(2,1)S(1)} %copy-done.64), channel_id=1, source_target_pairs={{3,1},{1,3},{6,4},{4,6},{11,9},{9,11},{14,12},{12,14},{19,17},{17,... | collective-permute-start | bytes 1572872 | tf_op jit(solution)/shard_map/ppermute | solution.py:75
  407.7 13.4 %collective-permute-start.48 = (bf16[128,2048]{1,0:T(8,128)(2,1)}, bf16[128,2048]{1,0:T(8,128)(2,1)S(1)}, u32[]{:S(2)}, u32[]{:S(2)}) collective-permute-start(bf16[128,2048]{1,0:T(8,128)(2,1)} %get-tuple-element.257), channel_id=1, source_target_pairs={{0,1},{2,3},{5,4},{7,6},{8,9},{10,11},{13,12},{15,14},{16,17},{18,... | collective-permute-start | bytes 1572872 | tf_op jit(solution)/shard_map/ppermute | solution.py:75
  411.6 28.3 %collective-permute-start.47 = (bf16[128,2048]{1,0:T(8,128)(2,1)}, bf16[128,2048]{1,0:T(8,128)(2,1)S(1)}, u32[]{:S(2)}, u32[]{:S(2)}) collective-permute-start(bf16[128,2048]{1,0:T(8,128)(2,1)} %get-tuple-element.258), channel_id=1, source_target_pairs={{4,0},{6,2},{1,5},{3,7},{2,1},{0,3},{7,4},{5,6},{12,8},{14,10},{9,... | collective-permute-start | bytes 1572872 | tf_op jit(solution)/shard_map/ppermute | solution.py:75
  413.7 14.8 %collective-permute-start.52 = (bf16[128,2048]{1,0:T(8,128)(2,1)S(1)}, bf16[128,2048]{1,0:T(8,128)(2,1)S(1)}, u32[]{:S(2)}, u32[]{:S(2)}) collective-permute-start(bf16[128,2048]{1,0:T(8,128)(2,1)S(1)} %copy-done.63), channel_id=1, source_target_pairs={{4,0},{6,2},{1,5},{3,7},{2,1},{0,3},{7,4},{5,6},{12,8},{14,10},{9,... | collective-permute-start | bytes 1572872 | tf_op jit(solution)/shard_map/ppermute | solution.py:75
  419.2 20.7 %collective-permute-start.46 = (bf16[128,2048]{1,0:T(8,128)(2,1)S(1)}, bf16[128,2048]{1,0:T(8,128)(2,1)S(1)}, u32[]{:S(2)}, u32[]{:S(2)}) collective-permute-start(bf16[128,2048]{1,0:T(8,128)(2,1)S(1)} %add_convert_fusion.5), channel_id=1, source_target_pairs={{4,1},{6,3},{1,4},{3,6},{2,0},{0,2},{7,5},{5,7},{12,9},{14,11},{9,... | collective-permute-start | bytes 1572872 | tf_op jit(solution)/shard_map/ppermute | solution.py:75
  421.1 16.4 %collective-permute-start.51 = (bf16[128,2048]{1,0:T(8,128)(2,1)S(1)}, bf16[128,2048]{1,0:T(8,128)(2,1)S(1)}, u32[]{:S(2)}, u32[]{:S(2)}) collective-permute-start(bf16[128,2048]{1,0:T(8,128)(2,1)S(1)} %add_convert_fusion.4), channel_id=1, source_target_pairs={{4,1},{6,3},{1,4},{3,6},{2,0},{0,2},{7,5},{5,7},{12,9},{14,11},{9,... | collective-permute-start | bytes 1572872 | tf_op jit(solution)/shard_map/ppermute | solution.py:75
  442.0 18.5 %collective-permute-start.54 = (bf16[128,2048]{1,0:T(8,128)(2,1)}, bf16[128,2048]{1,0:T(8,128)(2,1)}, u32[]{:S(2)}, u32[]{:S(2)}) collective-permute-start(bf16[128,2048]{1,0:T(8,128)(2,1)} %get-tuple-element.284.refs_4_), channel_id=1, source_target_pairs={{1,4},{3,6},{4,1},{6,3},{0,2},{2,0},{5,7},{7,5},{9,12},{11,14},{12... | collective-permute-start | bytes 1572872 | tf_op jit(solution)/shard_map/ppermute | solution.py:75
  443.3 22.2 %collective-permute-start.60 = (bf16[128,2048]{1,0:T(8,128)(2,1)S(1)}, bf16[128,2048]{1,0:T(8,128)(2,1)S(1)}, u32[]{:S(2)}, u32[]{:S(2)}) collective-permute-start(bf16[128,2048]{1,0:T(8,128)(2,1)S(1)} %get-tuple-element.272.refs_4_), channel_id=1, source_target_pairs={{0,4},{2,6},{5,1},{7,3},{1,2},{3,0},{4,7},{6,5},{8,12},{10,14},{13... | collective-permute-start | bytes 1572872 | tf_op jit(solution)/shard_map/ppermute | solution.py:75
  447.1 20.5 %collective-permute-start.61 = (bf16[128,2048]{1,0:T(8,128)(2,1)S(1)}, bf16[128,2048]{1,0:T(8,128)(2,1)S(1)}, u32[]{:S(2)}, u32[]{:S(2)}) collective-permute-start(bf16[128,2048]{1,0:T(8,128)(2,1)S(1)} %get-tuple-element.272.refs_4_), channel_id=1, source_target_pairs={{1,0},{3,2},{4,5},{6,7},{9,8},{11,10},{12,13},{14,15},{17,16},{19,... | collective-permute-start | bytes 1572872 | tf_op jit(solution)/shard_map/ppermute | solution.py:75
  449.2 21.1 %collective-permute-start.62 = (bf16[128,2048]{1,0:T(8,128)(2,1)S(1)}, bf16[128,2048]{1,0:T(8,128)(2,1)S(1)}, u32[]{:S(2)}, u32[]{:S(2)}) collective-permute-start(bf16[128,2048]{1,0:T(8,128)(2,1)S(1)} %collective-permute-done.59.refs_0_), channel_id=1, source_target_pairs={{1,3},{3,1},{4,6},{6,4},{9,11},{11,9},{12,14},{14,12},{17,19},{19,... | collective-permute-start | bytes 1572872 | tf_op jit(solution)/shard_map/ppermute | solution.py:75
  452.3 19.5 %collective-permute-start.63 = (bf16[128,2048]{1,0:T(8,128)(2,1)S(1)}, bf16[128,2048]{1,0:T(8,128)(2,1)S(1)}, u32[]{:S(2)}, u32[]{:S(2)}) collective-permute-start(bf16[128,2048]{1,0:T(8,128)(2,1)S(1)} %collective-permute-done.59.refs_0_), channel_id=1, source_target_pairs={{0,4},{2,6},{5,1},{7,3},{8,12},{10,14},{13,9},{15,11},{16,20},{18,... | collective-permute-start | bytes 1572872 | tf_op jit(solution)/shard_map/ppermute | solution.py:75
  460.4 46.5 %collective-permute-start.55 = (bf16[128,2048]{1,0:T(8,128)(2,1)}, bf16[128,2048]{1,0:T(8,128)(2,1)}, u32[]{:S(2)}, u32[]{:S(2)}) collective-permute-start(bf16[128,2048]{1,0:T(8,128)(2,1)} %get-tuple-element.284.refs_4_), channel_id=1, source_target_pairs={{0,4},{2,6},{5,1},{7,3},{1,2},{3,0},{4,7},{6,5},{8,12},{10,14},{13... | collective-permute-start | bytes 1572872 | tf_op jit(solution)/shard_map/ppermute | solution.py:75
  465.5 44.1 %collective-permute-start.56 = (bf16[128,2048]{1,0:T(8,128)(2,1)}, bf16[128,2048]{1,0:T(8,128)(2,1)}, u32[]{:S(2)}, u32[]{:S(2)}) collective-permute-start(bf16[128,2048]{1,0:T(8,128)(2,1)} %get-tuple-element.284.refs_4_), channel_id=1, source_target_pairs={{1,0},{3,2},{4,5},{6,7},{9,8},{11,10},{12,13},{14,15},{17,16},{19,... | collective-permute-start | bytes 1572872 | tf_op jit(solution)/shard_map/ppermute | solution.py:75
  467.6 43.3 %collective-permute-start.57 = (bf16[128,2048]{1,0:T(8,128)(2,1)}, bf16[128,2048]{1,0:T(8,128)(2,1)}, u32[]{:S(2)}, u32[]{:S(2)}) collective-permute-start(bf16[128,2048]{1,0:T(8,128)(2,1)} %collective-permute-done.54.refs_0_), channel_id=1, source_target_pairs={{1,3},{3,1},{4,6},{6,4},{9,11},{11,9},{12,14},{14,12},{17,19},{19,... | collective-permute-start | bytes 1572872 | tf_op jit(solution)/shard_map/ppermute | solution.py:75
  470.3 40.7 %collective-permute-start.58 = (bf16[128,2048]{1,0:T(8,128)(2,1)}, bf16[128,2048]{1,0:T(8,128)(2,1)}, u32[]{:S(2)}, u32[]{:S(2)}) collective-permute-start(bf16[128,2048]{1,0:T(8,128)(2,1)} %collective-permute-done.54.refs_0_), channel_id=1, source_target_pairs={{0,4},{2,6},{5,1},{7,3},{8,12},{10,14},{13,9},{15,11},{16,20},{18,... | collective-permute-start | bytes 1572872 | tf_op jit(solution)/shard_map/ppermute | solution.py:75
  501.5 35.7 %collective-permute-start.80 = (bf16[128,2048]{1,0:T(8,128)(2,1)}, bf16[128,2048]{1,0:T(8,128)(2,1)}, u32[]{:S(2)}, u32[]{:S(2)}) collective-permute-start(bf16[128,2048]{1,0:T(8,128)(2,1)} %get-tuple-element.307), channel_id=1, source_target_pairs={{4,0},{6,2},{1,5},{3,7},{12,8},{14,10},{9,13},{11,15},{20,16},{22,... | collective-permute-start | bytes 1572872 | tf_op jit(solution)/shard_map/ppermute | solution.py:75
  506.9 33.5 %collective-permute-start.81 = (bf16[128,2048]{1,0:T(8,128)(2,1)}, bf16[128,2048]{1,0:T(8,128)(2,1)}, u32[]{:S(2)}, u32[]{:S(2)}) collective-permute-start(bf16[128,2048]{1,0:T(8,128)(2,1)} %get-tuple-element.308), channel_id=1, source_target_pairs={{3,1},{1,3},{6,4},{4,6},{11,9},{9,11},{14,12},{12,14},{19,17},{17,... | collective-permute-start | bytes 1572872 | tf_op jit(solution)/shard_map/ppermute | solution.py:75
  509.6 35.6 %collective-permute-start.84 = (bf16[128,2048]{1,0:T(8,128)(2,1)}, bf16[128,2048]{1,0:T(8,128)(2,1)}, u32[]{:S(2)}, u32[]{:S(2)}) collective-permute-start(bf16[128,2048]{1,0:T(8,128)(2,1)} %get-tuple-element.308), channel_id=1, source_target_pairs={{0,1},{2,3},{5,4},{7,6},{8,9},{10,11},{13,12},{15,14},{16,17},{18,... | collective-permute-start | bytes 1572872 | tf_op jit(solution)/shard_map/ppermute | solution.py:75
  514.6 42.8 %collective-permute-start.64 = (bf16[256,3072]{1,0:T(8,128)(2,1)}, bf16[256,3072]{1,0:T(8,128)(2,1)S(1)}, u32[]{:S(2)}, u32[]{:S(2)}) collective-permute-start(bf16[256,3072]{1,0:T(8,128)(2,1)} %bitcast.76), channel_id=1, source_target_pairs={{1,4},{3,6},{4,1},{6,3},{9,12},{11,14},{12,9},{14,11},{17,20},{19,... | collective-permute-start | bytes 4718600 | tf_op jit(solution)/shard_map/ppermute | solution.py:75
  517.5 73.1 %collective-permute-start.83 = (bf16[128,2048]{1,0:T(8,128)(2,1)}, bf16[128,2048]{1,0:T(8,128)(2,1)}, u32[]{:S(2)}, u32[]{:S(2)}) collective-permute-start(bf16[128,2048]{1,0:T(8,128)(2,1)} %get-tuple-element.309), channel_id=1, source_target_pairs={{4,0},{6,2},{1,5},{3,7},{2,1},{0,3},{7,4},{5,6},{12,8},{14,10},{9,... | collective-permute-start | bytes 1572872 | tf_op jit(solution)/shard_map/ppermute | solution.py:75
  540.5 15.9 %collective-permute-start.76 = (bf16[128,2048]{1,0:T(8,128)(2,1)}, bf16[128,2048]{1,0:T(8,128)(2,1)S(1)}, u32[]{:S(2)}, u32[]{:S(2)}) collective-permute-start(bf16[128,2048]{1,0:T(8,128)(2,1)} %get-tuple-element.305), channel_id=1, source_target_pairs={{3,1},{1,3},{6,4},{4,6},{11,9},{9,11},{14,12},{12,14},{19,17},{17,... | collective-permute-start | bytes 1572872 | tf_op jit(solution)/shard_map/ppermute | solution.py:75
  545.2 45.3 %collective-permute-start.82 = (bf16[128,2048]{1,0:T(8,128)(2,1)}, bf16[128,2048]{1,0:T(8,128)(2,1)}, u32[]{:S(2)}, u32[]{:S(2)}) collective-permute-start(bf16[128,2048]{1,0:T(8,128)(2,1)} %add_convert_fusion), channel_id=1, source_target_pairs={{4,1},{6,3},{1,4},{3,6},{2,0},{0,2},{7,5},{5,7},{12,9},{14,11},{9,... | collective-permute-start | bytes 1572872 | tf_op jit(solution)/shard_map/ppermute | solution.py:75
  548.6 40.7 %collective-permute-start.79 = (bf16[128,2048]{1,0:T(8,128)(2,1)}, bf16[128,2048]{1,0:T(8,128)(2,1)}, u32[]{:S(2)}, u32[]{:S(2)}) collective-permute-start(bf16[128,2048]{1,0:T(8,128)(2,1)} %get-tuple-element.305), channel_id=1, source_target_pairs={{0,1},{2,3},{5,4},{7,6},{8,9},{10,11},{13,12},{15,14},{16,17},{18,... | collective-permute-start | bytes 1572872 | tf_op jit(solution)/shard_map/ppermute | solution.py:75
  556.3 38.8 %collective-permute-start.78 = (bf16[128,2048]{1,0:T(8,128)(2,1)}, bf16[128,2048]{1,0:T(8,128)(2,1)}, u32[]{:S(2)}, u32[]{:S(2)}) collective-permute-start(bf16[128,2048]{1,0:T(8,128)(2,1)} %get-tuple-element.306), channel_id=1, source_target_pairs={{4,0},{6,2},{1,5},{3,7},{2,1},{0,3},{7,4},{5,6},{12,8},{14,10},{9,... | collective-permute-start | bytes 1572872 | tf_op jit(solution)/shard_map/ppermute | solution.py:75
  557.4 37.7 %collective-permute-start.77 = (bf16[128,2048]{1,0:T(8,128)(2,1)}, bf16[128,2048]{1,0:T(8,128)(2,1)}, u32[]{:S(2)}, u32[]{:S(2)}) collective-permute-start(bf16[128,2048]{1,0:T(8,128)(2,1)} %add_convert_fusion.1), channel_id=1, source_target_pairs={{4,1},{6,3},{1,4},{3,6},{2,0},{0,2},{7,5},{5,7},{12,9},{14,11},{9,... | collective-permute-start | bytes 1572872 | tf_op jit(solution)/shard_map/ppermute | solution.py:75
  608.3 17.2 %collective-permute-start.70 = (bf16[128,2048]{1,0:T(8,128)(2,1)}, bf16[128,2048]{1,0:T(8,128)(2,1)S(1)}, u32[]{:S(2)}, u32[]{:S(2)}) collective-permute-start(bf16[128,2048]{1,0:T(8,128)(2,1)} %get-tuple-element.301), channel_id=1, source_target_pairs={{4,0},{6,2},{1,5},{3,7},{12,8},{14,10},{9,13},{11,15},{20,16},{22,... | collective-permute-start | bytes 1572872 | tf_op jit(solution)/shard_map/ppermute | solution.py:75
  611.6 15.5 %collective-permute-start.71 = (bf16[128,2048]{1,0:T(8,128)(2,1)}, bf16[128,2048]{1,0:T(8,128)(2,1)}, u32[]{:S(2)}, u32[]{:S(2)}) collective-permute-start(bf16[128,2048]{1,0:T(8,128)(2,1)} %get-tuple-element.302), channel_id=1, source_target_pairs={{3,1},{1,3},{6,4},{4,6},{11,9},{9,11},{14,12},{12,14},{19,17},{17,... | collective-permute-start | bytes 1572872 | tf_op jit(solution)/shard_map/ppermute | solution.py:75
  614.7 21.3 %collective-permute-start.74 = (bf16[128,2048]{1,0:T(8,128)(2,1)}, bf16[128,2048]{1,0:T(8,128)(2,1)S(1)}, u32[]{:S(2)}, u32[]{:S(2)}) collective-permute-start(bf16[128,2048]{1,0:T(8,128)(2,1)} %get-tuple-element.302), channel_id=1, source_target_pairs={{0,1},{2,3},{5,4},{7,6},{8,9},{10,11},{13,12},{15,14},{16,17},{18,... | collective-permute-start | bytes 1572872 | tf_op jit(solution)/shard_map/ppermute | solution.py:75
  629.3 20.6 %collective-permute-start.68 = (bf16[128,2048]{1,0:T(8,128)(2,1)S(1)}, bf16[128,2048]{1,0:T(8,128)(2,1)S(1)}, u32[]{:S(2)}, u32[]{:S(2)}) collective-permute-start(bf16[128,2048]{1,0:T(8,128)(2,1)S(1)} %copy-done.62), channel_id=1, source_target_pairs={{4,0},{6,2},{1,5},{3,7},{2,1},{0,3},{7,4},{5,6},{12,8},{14,10},{9,... | collective-permute-start | bytes 1572872 | tf_op jit(solution)/shard_map/ppermute | solution.py:75
  636.0 18.1 %collective-permute-start.67 = (bf16[128,2048]{1,0:T(8,128)(2,1)S(1)}, bf16[128,2048]{1,0:T(8,128)(2,1)S(1)}, u32[]{:S(2)}, u32[]{:S(2)}) collective-permute-start(bf16[128,2048]{1,0:T(8,128)(2,1)S(1)} %add_convert_fusion.3), channel_id=1, source_target_pairs={{4,1},{6,3},{1,4},{3,6},{2,0},{0,2},{7,5},{5,7},{12,9},{14,11},{9,... | collective-permute-start | bytes 1572872 | tf_op jit(solution)/shard_map/ppermute | solution.py:75
  655.4 22.1 %collective-permute-start.90 = (bf16[256,3072]{1,0:T(8,128)(2,1)}, bf16[256,3072]{1,0:T(8,128)(2,1)S(1)}, u32[]{:S(2)}, u32[]{:S(2)}) collective-permute-start(bf16[256,3072]{1,0:T(8,128)(2,1)} %bitcast.74), channel_id=1, source_target_pairs={{1,4},{3,6},{4,1},{6,3},{9,12},{11,14},{12,9},{14,11},{17,20},{19,... | collective-permute-start | bytes 4718600 | tf_op jit(solution)/shard_map/ppermute | solution.py:75
  (102 other events, 1037.0 us)
Sparse Core Ops, SparseCore 0:
  30.7 56.2 all-gather.3
  88.6 116.5 all-gather.5
  209.9 119.3 all-gather.7
  331.4 124.8 reduce-scatter.3
  458.4 127.5 reduce-scatter.7
  589.4 57.3 reduce-scatter.5

commit v2 on v1

--- a/solution.py
+++ b/solution.py
@@ -709,6 +709,8 @@
     unit_grads.append(collect_z(unit_step(1)))
     sums = [None, send_sums(back_project(1))]
     sums[0] = send_sums(back_project(0))
+    branch = [None, send_sums(branch_project(1))]
+    branch[0] = send_sums(branch_project(0))
     left = [None, order(lambda a: leave(1, a), sums[1])]
     here = [None, send_rows(left[1][0])]
     left[0] = order(lambda a: leave(0, a), sums[0])
@@ -743,17 +745,19 @@
     back1, scaled1, later = order(lambda a: back_attend(1, a, None), attn_grads[1])
     sums[1] = send_sums(order(normed_project, back1))
     attn_grads[0] = order(join_rows, here[0], starts)
+    outputs = [None, order(lambda a: finish(1, a), branch[1])]
     unit_parts = [trade(order(lambda a: a, unit_grads[0]))]
     back0, scaled0 = order(lambda a: back_attend(0, a, later), attn_grads[0])
     sums[0] = send_sums(order(normed_project, back0))
+    outputs[0] = order(lambda a: finish(0, a), branch[0])
     unit_parts[0] = order(lambda a: a, unit_parts[0])
-    branch = [None, send_sums(branch_project(1))]
-    branch[0] = send_sums(branch_project(0))
     grad_attn = collect_z(
         [(tokens_all, [scaled0, scaled1]), (attn_grads, [found[0][3], found[1][3]])]
     )
+    unit_parts.append(trade(order(lambda a: a, unit_grads[1])))
     ended = [None, order(lambda a: end(1, a), sums[1])]
     ended[0] = order(lambda a: end(0, a), sums[0])
+    unit_parts[1] = order(lambda a: a, unit_parts[1])
     attn_gain_total = ended[0][1] + ended[1][1]
     mlp_gain_total = left[0][2] + left[1][2]
     input_parts = [ended[0][0], ended[1][0]]
@@ -775,10 +779,7 @@
     gains_here = jnp.stack([gain_attn, gain_mlp], 0).astype(F32)
 
     both = order(lambda a: a / lax.dynamic_slice_in_dim(gains_here, t * n, n, 1), both)
-    outputs = [None, order(lambda a: finish(1, a), branch[1])]
-    outputs[0] = order(lambda a: finish(0, a), branch[0])
-
-    unit_parts.append(trade(order(lambda a: a, unit_grads[1])))
+
     u = unit_parts[0].shape[1] // 3
 
     def units(k):

time: 717 us -> 693 us (0.967)
  starting transfers between devices: 178 us -> 166 us
  waiting for transfers between devices: 185 us -> 175 us
    ppermute x87, waiting for transfers between devices: 181 us -> 160 us  [send(): return lax.ppermute(values, ('lo', 'y', 'core'), pairs)]
    ppermute x87, starting transfers between devices: 173 us -> 161 us  [send(): return lax.ppermute(values, ('lo', 'y', 'core'), pairs)]
    all_gather x3, waiting for transfers between devices: 0.04 us -> 9.82 us  [gather_z(): return lax.all_gather(piece, ('hi', 'core'), axis=0, tiled=True)]
  transfers between devices with their start and end apart: 98 -> 98, of which waited for: 35 -> 38; matrix products, arithmetic and copies ran while one was open for 9% -> 9% of each run, Pallas kernels for 35% -> 37%
where the time goes in v2:
time: 693 us; the launch traced here: 682 us
  Pallas kernels  249 us (36%)
  waiting for transfers between devices  175 us (25%)
  starting transfers between devices  166 us (24%)
  other arithmetic  52.2 us (8%)
  local copies, waits for them, and re-layouts  20.8 us (3%)
  between operations  17.8 us (3%)
    ppermute x87, starting transfers between devices, send(): return lax.ppermute(values, ('lo', 'y', 'core'), pairs)  161 us
    ppermute x87, waiting for transfers between devices, send(): return lax.ppermute(values, ('lo', 'y', 'core'), pairs)  160 us
    pallas_call x8, Pallas kernels, project(): pl.pallas_call(functools.partial(project_kernel, len(lhs), rows), grid=(w...  68 us
    pallas_call x3, Pallas kernels, weight_grads(): pl.pallas_call(functools.partial(grads_kernel, plan), grid=(count * slab...  50.7 us
    pallas_call x2, Pallas kernels, mlp(): pl.pallas_call(functools.partial(mlp_kernel, count), grid=(steps,), out_s...  39.8 us
    pallas_call x2, Pallas kernels, attend_back(): pl.pallas_call(functools.partial(backward_kernel, m, heads, last), grid=(...  33.4 us
    pallas_call x2, Pallas kernels, attend(): pl.pallas_call(functools.partial(forward_kernel, m, heads), grid=(groups,...  28.8 us
    pallas_call x8, Pallas kernels, join_rows(): pl.pallas_call(assemble_kernel, out_shape=jax.ShapeDtypeStruct((4 * rows,...  28.5 us
  transfers between devices with their start and end apart: 98, of which 38 were waited for; matrix products, arithmetic and copies ran while one was open for 9% of the time, Pallas kernels for 37%

profile of v2, /device:TPU:1, one launch (start us, length us, event | category | flops | bytes accessed | tf_op | source)
XLA Modules:
  0.0 681.5 jit_solution(8893262471092981126)
XLA Ops:
  7.2 4.5 collective-permute-start
  19.1 10.4 %collective-permute-done.1 = bf16[256,1280]{1,0:T(8,128)(2,1)S(1)} collective-permute-done((bf16[256,1280]{1,0:T(8,128)(2,1)S(1)}, bf16[256,1280]{1,0:T(8,128)(2,1)S(1)}, u32[]{:S(2)}, u32[]{:S(2)}) %collective-permute-start.1) | collective-permute-done | bytes 655392 | tf_op jit(solution)/shard_map/ppermute | solution.py:75
  42.1 26.5 %collective-permute-done.2.refs_0_ = bf16[128,2048]{1,0:T(8,128)(2,1)} collective-permute-done((bf16[128,2048]{1,0:T(8,128)(2,1)}, bf16[128,2048]{1,0:T(8,128)(2,1)}, u32[]{:S(2)}, u32[]{:S(2)}) %collective-permute-start.2) | collective-permute-done | bytes 524320 | tf_op jit(solution)/shard_map/ppermute | solution.py:75
  69.9 3.1 collective-permute-start.5
  73.8 5.4 collective-permute-done.6.refs_5_
  80.5 3.6 assemble.8.refs_0_
  91.3 9.3 %collective-permute-done.13.refs_0_ = bf16[128,2048]{1,0:T(8,128)(2,1)S(1)} collective-permute-done((bf16[128,2048]{1,0:T(8,128)(2,1)}, bf16[128,2048]{1,0:T(8,128)(2,1)S(1)}, u32[]{:S(2)}, u32[]{:S(2)}) %collective-permute-start.13) | collective-permute-done | bytes 524320 | tf_op jit(solution)/shard_map/ppermute | solution.py:75
  101.9 3.1 collective-permute-start.16
  113.7 12.2 %attend.2 = (bf16[512,512]{1,0:T(8,128)(2,1)}, bf16[512,256]{1,0:T(8,128)(2,1)}, f32[2,4,512]{2,1,0:T(4,128)}, bf16[512,512]{1,0:T(8,128)(2,1)}, f32[512,128]{1,0:T(8,128)}) custom-call(s32[1]{0:T(128)S(6)} %select_n.165.lengths, bf16[512,2048]{1,0:T(8,128)(2,1)} %assemble.8.refs_0_, bf16[2048,1280]{1,0:T(8,128)(2,1)} %all-gather.4.cloned.1.call-done.refs_1_, ...), custom_call_target="tpu_custom_call" | custom-call | tf_op jit(solution)/shard_map/attend/pallas_call | solution.py:378
  128.9 5.0 project.8
  146.1 3.3 collective-permute-start.28
  151.6 6.3 collective-permute-done.22.refs_5_
  162.1 3.6 assemble.9.refs_0_.refs_2_
  165.6 3.5 assemble.10.refs_2_.refs_6_
  169.2 16.6 %attend.3 = (bf16[512,512]{1,0:T(8,128)(2,1)}, bf16[512,256]{1,0:T(8,128)(2,1)}, f32[2,4,512]{2,1,0:T(4,128)}, bf16[512,512]{1,0:T(8,128)(2,1)}, f32[512,128]{1,0:T(8,128)}) custom-call(s32[1]{0:T(128)S(6)} %select_n.165.lengths, bf16[512,2048]{1,0:T(8,128)(2,1)} %assemble.9.refs_0_.refs_2_, bf16[2048,1280]{1,0:T(8,128)(2,1)} %all-gather.4.cloned.1.call-done.refs_1_, ...), custom_call_target="tpu_custom_call" | custom-call | tf_op jit(solution)/shard_map/attend/pallas_call | solution.py:378
  185.8 5.0 project.9
  197.1 3.6 collective-permute-done.30.refs_1_
  200.7 5.2 collective-permute-done.33.refs_5_
  207.5 3.5 assemble.11.refs_3_.refs_8_
  215.5 3.3 collective-permute-start.35
  220.1 3.1 collective-permute-start.25
  224.4 6.4 collective-permute-done.23.refs_0_
  232.1 4.6 collective-permute-start.26
  237.2 6.3 collective-permute-done.27.refs_5_
  247.3 3.6 assemble.12.refs_0_
  253.2 6.3 collective-permute-start.41
  263.3 7.3 %collective-permute-start.42 = (bf16[128,2048]{1,0:T(8,128)(2,1)S(1)}, bf16[128,2048]{1,0:T(8,128)(2,1)S(1)}, u32[]{:S(2)}, u32[]{:S(2)}) collective-permute-start(bf16[128,2048]{1,0:T(8,128)(2,1)S(1)} %collective-permute-done.39.refs_0_), channel_id=1, source_target_pairs={{1,3},{3,1},{4,6},{6,4},{9,11},{11,9},{12,14},{14,12},{17,19},{19,... | collective-permute-start | bytes 1572872 | tf_op jit(solution)/shard_map/ppermute | solution.py:75
  270.6 3.8 collective-permute-done.43.refs_5_
  278.0 3.6 assemble.13.refs_1_.refs_2_
  281.6 19.9 %mlp.2 = (bf16[512,1024]{1,0:T(8,128)(2,1)}, bf16[512,1024]{1,0:T(8,128)(2,1)}, bf16[512,1024]{1,0:T(8,128)(2,1)}, bf16[512,1024]{1,0:T(8,128)(2,1)}, bf16[512,1...) custom-call(bf16[512,2048]{1,0:T(8,128)(2,1)} %assemble.12.refs_0_, bf16[512,2048]{1,0:T(8,128)(2,1)} %assemble.13.refs_1_.refs_2_, ...), custom_call_target="tpu_custom_call" | custom-call | tf_op jit(solution)/shard_map/mlp/pallas_call | solution.py:233
  301.5 19.3 %grads.3 = bf16[8,256,3072]{2,1,0:T(8,128)(2,1)} custom-call(bf16[512,2048]{1,0:T(8,128)(2,1)} %assemble.12.refs_0_, bf16[512,1024]{1,0:T(8,128)(2,1)} %get-tuple-element.255.refs_1_.refs_0_, bf16[512,2048]{1,0:T(8,128)(2,1)} %assemble.13.refs_1_.refs_2_, bf16[512,1024]{1,0:T(8,128)(2,1)} %get-tuple-element.253.refs_3_.refs_0_, ...), custom_call_target="tpu_custom_call" | custom-call | tf_op jit(solution)/shard_map/grads/pallas_call | solution.py:285
  320.9 9.8 %all-gather.8.cloned.1.call-done.refs_4_.refs_5_.refs_6_.refs_7_.refs_3_ = bf16[2048,3072]{1,0:T(8,128)(2,1)} async-done(((bf16[256,3072]{1,0:T(8,128)(2,1)}), bf16[2048,3072]{1,0:T(8,128)(2,1)}) %all-gather.8.cloned.1.call-update) | async-done | bytes 12582928 | tf_op jit(solution)/shard_map/all_gather | solution.py:566
  330.7 19.9 %mlp.3 = (bf16[512,1024]{1,0:T(8,128)(2,1)}, bf16[512,1024]{1,0:T(8,128)(2,1)}, bf16[512,1024]{1,0:T(8,128)(2,1)}, bf16[512,1024]{1,0:T(8,128)(2,1)}, bf16[512,1...) custom-call(bf16[512,2048]{1,0:T(8,128)(2,1)} %assemble.12.refs_0_, bf16[512,2048]{1,0:T(8,128)(2,1)} %assemble.13.refs_1_.refs_2_, ...), custom_call_target="tpu_custom_call" | custom-call | tf_op jit(solution)/shard_map/mlp/pallas_call | solution.py:233
  350.6 19.3 %grads.4 = bf16[8,256,3072]{2,1,0:T(8,128)(2,1)} custom-call(bf16[512,2048]{1,0:T(8,128)(2,1)} %assemble.12.refs_0_, bf16[512,1024]{1,0:T(8,128)(2,1)} %get-tuple-element.248.refs_1_.refs_2_, bf16[512,2048]{1,0:T(8,128)(2,1)} %assemble.13.refs_1_.refs_2_, bf16[512,1024]{1,0:T(8,128)(2,1)} %get-tuple-element.249.refs_3_.refs_2_, ...), custom_call_target="tpu_custom_call" | custom-call | tf_op jit(solution)/shard_map/grads/pallas_call | solution.py:285
  370.0 14.5 %project.10 = (bf16[128,2048]{1,0:T(8,128)(2,1)}, bf16[128,2048]{1,0:T(8,128)(2,1)}, bf16[128,2048]{1,0:T(8,128)(2,1)}, bf16[128,2048]{1,0:T(8,128)(2,1)}) custom-call(s32[5]{0:T(128)} %pad_add_fusion.starts, bf16[512,1024]{1,0:T(8,128)(2,1)} %get-tuple-element.253.refs_3_.refs_0_, bf16[512,1024]{1,0:T(8,128)(2,1)} %get-tuple-element.243.refs_5_.refs_1_, ...), custom_call_target="tpu_custom_call" | custom-call | tf_op jit(solution)/shard_map/project/pallas_call | solution.py:193
  384.6 3.1 collective-permute-start.54
  387.7 3.3 collective-permute-start.55
  391.0 14.6 %project.11 = (bf16[128,2048]{1,0:T(8,128)(2,1)}, bf16[128,2048]{1,0:T(8,128)(2,1)}, bf16[128,2048]{1,0:T(8,128)(2,1)}, bf16[128,2048]{1,0:T(8,128)(2,1)}) custom-call(s32[5]{0:T(128)} %pad_add_fusion.starts, bf16[512,1024]{1,0:T(8,128)(2,1)} %get-tuple-element.255.refs_1_.refs_0_, bf16[512,1024]{1,0:T(8,128)(2,1)} %get-tuple-element.242.refs_4_.refs_1_, ...), custom_call_target="tpu_custom_call" | custom-call | tf_op jit(solution)/shard_map/project/pallas_call | solution.py:193
  410.3 8.8 %project.12 = (bf16[128,2048]{1,0:T(8,128)(2,1)}, bf16[128,2048]{1,0:T(8,128)(2,1)}, bf16[128,2048]{1,0:T(8,128)(2,1)}, bf16[128,2048]{1,0:T(8,128)(2,1)}) custom-call(s32[5]{0:T(128)} %pad_add_fusion.starts, bf16[512,1024]{1,0:T(8,128)(2,1)} %get-tuple-element.257.refs_9_.refs_0_, bf16[512,1024]{1,0:T(8,128)(2,1)} %get-tuple-element.252.refs_9_.refs_1_, ...), custom_call_target="tpu_custom_call" | custom-call | tf_op jit(solution)/shard_map/project/pallas_call | solution.py:193
  419.2 8.9 %project.13 = (bf16[128,2048]{1,0:T(8,128)(2,1)}, bf16[128,2048]{1,0:T(8,128)(2,1)}, bf16[128,2048]{1,0:T(8,128)(2,1)}, bf16[128,2048]{1,0:T(8,128)(2,1)}) custom-call(s32[5]{0:T(128)} %pad_add_fusion.starts, bf16[512,1024]{1,0:T(8,128)(2,1)} %get-tuple-element.259.refs_7_.refs_0_, bf16[512,1024]{1,0:T(8,128)(2,1)} %get-tuple-element.247.refs_7_.refs_1_, ...), custom_call_target="tpu_custom_call" | custom-call | tf_op jit(solution)/shard_map/project/pallas_call | solution.py:193
  429.6 4.9 collective-permute-start.49
  437.1 3.5 collective-permute-done.49
  440.6 3.2 collective-permute-start.70
  448.5 5.4 collective-permute-done.56
  456.2 6.9 %collective-permute-done.52 = bf16[128,2048]{1,0:T(8,128)(2,1)S(1)} collective-permute-done((bf16[128,2048]{1,0:T(8,128)(2,1)S(1)}, bf16[128,2048]{1,0:T(8,128)(2,1)S(1)}, u32[]{:S(2)}, u32[]{:S(2)}) %collective-permute-start.52) | collective-permute-done | bytes 524320 | tf_op jit(solution)/shard_map/ppermute | solution.py:75
  464.6 6.2 collective-permute-done.51
  477.7 3.1 collective-permute-start.67
  480.8 6.7 collective-permute-done.59.refs_0_
  496.1 3.6 assemble.14.refs_0_.refs_6_
  499.7 19.8 %attend_back.2 = (bf16[512,768]{1,0:T(8,128)(2,1)}, bf16[512,768]{1,0:T(8,128)(2,1)}, f32[512,256]{1,0:T(8,128)}) custom-call(s32[1]{0:T(128)S(6)} %select_n.165.lengths, bf16[512,2048]{1,0:T(8,128)(2,1)} %assemble.14.refs_0_.refs_6_, bf16[2048,1280]{1,0:T(8,128)(2,1)} %all-gather.4.cloned.1.call-done.refs_1_, bf16[512,512]{1,0:T(8,128)(2,1)} %get-tuple-element.202.refs_2_, ...), custom_call_target="tpu_custom_call" | custom-call | tf_op jit(solution)/shard_map/attend_back/pallas_call | solution.py:473
  519.5 5.5 project.14
  525.0 3.4 collective-permute-start.44
  530.9 3.5 assemble.15.refs_0_.refs_4_
  535.8 4.5 collective-permute-start.84
  546.3 13.6 %attend_back.3 = (bf16[512,768]{1,0:T(8,128)(2,1)}, bf16[512,768]{1,0:T(8,128)(2,1)}) custom-call(s32[1]{0:T(128)S(6)} %select_n.165.lengths, bf16[512,2048]{1,0:T(8,128)(2,1)} %assemble.15.refs_0_.refs_4_, bf16[2048,1280]{1,0:T(8,128)(2,1)} %all-gather.4.cloned.1.call-done.refs_1_, bf16[512,512]{1,0:T(8,128)(2,1)} %get-tuple-element.179.refs_2_, ...), custom_call_target="tpu_custom_call" | custom-call | tf_op jit(solution)/shard_map/attend_back/pallas_call | solution.py:473
  559.9 5.6 project.15
  565.5 4.8 collective-permute-done.46
  571.7 12.1 %grads.5 = bf16[8,256,1280]{2,1,0:T(8,128)(2,1)} custom-call(bf16[512,2048]{1,0:T(8,128)(2,1)} %assemble.8.refs_0_, bf16[512,768]{1,0:T(8,128)(2,1)} %get-tuple-element.318.refs_1_, bf16[512,2048]{1,0:T(8,128)(2,1)} %assemble.9.refs_0_.refs_2_, bf16[512,768]{1,0:T(8,128)(2,1)} %get-tuple-element.319.refs_3_, bf16[512,2048]{1,0:T(8,128)(2,1)} %assemble.15.refs_0_.refs_4_, ...), custom_call_target="tpu_custom_call" | custom-call | tf_op jit(solution)/shard_map/grads/pallas_call | solution.py:285
  601.3 3.1 collective-permute-start.81
  607.4 3.4 collective-permute-done.75
  627.7 12.1 %collective-permute-done.85 = bf16[256,3072]{1,0:T(8,128)(2,1)S(1)} collective-permute-done((bf16[256,3072]{1,0:T(8,128)(2,1)}, bf16[256,3072]{1,0:T(8,128)(2,1)S(1)}, u32[]{:S(2)}, u32[]{:S(2)}) %collective-permute-start.85) | collective-permute-done | bytes 1572896 | tf_op jit(solution)/shard_map/ppermute | solution.py:75
  641.4 3.1 collective-permute-done.87
  649.9 3.6 collective-permute-start.90
  663.7 5.6 collective-permute-done.91
  (413 shorter events, 193.2 us)
Async XLA Ops:
  7.2 106.5 %all-gather.4.cloned.1.call-start = ((), (), s32[]{:S(2)}) async-start(), calls=%async_computation.3 | async-start | bytes 5898240 | tf_op jit(solution)/shard_map/all_gather | solution.py:566
  30.4 251.2 %all-gather.6.cloned.1.call-start = ((), (), s32[]{:S(2)}) async-start(), calls=%async_computation.4 | async-start | bytes 14155776 | tf_op jit(solution)/shard_map/all_gather | solution.py:566
  35.2 48.9 %collective-permute-start.7 = (bf16[256,3072]{1,0:T(8,128)(2,1)S(1)}, bf16[256,3072]{1,0:T(8,128)(2,1)}, u32[]{:S(2)}, u32[]{:S(2)}) collective-permute-start(bf16[256,3072]{1,0:T(8,128)(2,1)S(1)} %pad_maximum_fusion), channel_id=1, source_target_pairs={{1,4},{3,6},{4,1},{6,3},{9,12},{11,14},{12,9},{14,11},{17,20},{19,... | collective-permute-start | bytes 4718600 | tf_op jit(solution)/shard_map/ppermute | solution.py:75
  38.3 30.4 %collective-permute-start.2 = (bf16[128,2048]{1,0:T(8,128)(2,1)}, bf16[128,2048]{1,0:T(8,128)(2,1)}, u32[]{:S(2)}, u32[]{:S(2)}) collective-permute-start(bf16[128,2048]{1,0:T(8,128)(2,1)} %get-tuple-element.174.refs_4_), channel_id=1, source_target_pairs={{1,4},{3,6},{4,1},{6,3},{0,2},{2,0},{5,7},{7,5},{9,12},{11,14},{12... | collective-permute-start | bytes 1572872 | tf_op jit(solution)/shard_map/ppermute | solution.py:75
  40.0 33.8 %collective-permute-start.4 = (bf16[128,2048]{1,0:T(8,128)(2,1)}, bf16[128,2048]{1,0:T(8,128)(2,1)}, u32[]{:S(2)}, u32[]{:S(2)}) collective-permute-start(bf16[128,2048]{1,0:T(8,128)(2,1)} %get-tuple-element.174.refs_4_), channel_id=1, source_target_pairs={{1,0},{3,2},{4,5},{6,7},{9,8},{11,10},{12,13},{14,15},{17,16},{19,... | collective-permute-start | bytes 1572872 | tf_op jit(solution)/shard_map/ppermute | solution.py:75
  42.1 31.7 %collective-permute-start.3 = (bf16[128,2048]{1,0:T(8,128)(2,1)}, bf16[128,2048]{1,0:T(8,128)(2,1)}, u32[]{:S(2)}, u32[]{:S(2)}) collective-permute-start(bf16[128,2048]{1,0:T(8,128)(2,1)} %get-tuple-element.174.refs_4_), channel_id=1, source_target_pairs={{0,4},{2,6},{5,1},{7,3},{1,2},{3,0},{4,7},{6,5},{8,12},{10,14},{13... | collective-permute-start | bytes 1572872 | tf_op jit(solution)/shard_map/ppermute | solution.py:75
  86.8 243.8 %all-gather.8.cloned.1.call-start = ((), (), s32[]{:S(2)}) async-start(), calls=%async_computation.5 | async-start | bytes 14155776 | tf_op jit(solution)/shard_map/all_gather | solution.py:566
  86.9 20.2 %collective-permute-start.15 = (bf16[128,2048]{1,0:T(8,128)(2,1)}, bf16[128,2048]{1,0:T(8,128)(2,1)S(1)}, u32[]{:S(2)}, u32[]{:S(2)}) collective-permute-start(bf16[128,2048]{1,0:T(8,128)(2,1)} %get-tuple-element.190.refs_4_), channel_id=1, source_target_pairs={{1,0},{3,2},{4,5},{6,7},{9,8},{11,10},{12,13},{14,15},{17,16},{19,... | collective-permute-start | bytes 1572872 | tf_op jit(solution)/shard_map/ppermute | solution.py:75
  91.3 42.6 %collective-permute-start.14 = (bf16[128,2048]{1,0:T(8,128)(2,1)}, bf16[128,2048]{1,0:T(8,128)(2,1)S(1)}, u32[]{:S(2)}, u32[]{:S(2)}) collective-permute-start(bf16[128,2048]{1,0:T(8,128)(2,1)} %get-tuple-element.190.refs_4_), channel_id=1, source_target_pairs={{0,4},{2,6},{5,1},{7,3},{1,2},{3,0},{4,7},{6,5},{8,12},{10,14},{13... | collective-permute-start | bytes 1572872 | tf_op jit(solution)/shard_map/ppermute | solution.py:75
  100.6 34.9 %collective-permute-start.17 = (bf16[128,2048]{1,0:T(8,128)(2,1)S(1)}, bf16[128,2048]{1,0:T(8,128)(2,1)S(1)}, u32[]{:S(2)}, u32[]{:S(2)}) collective-permute-start(bf16[128,2048]{1,0:T(8,128)(2,1)S(1)} %collective-permute-done.13.refs_0_), channel_id=1, source_target_pairs={{0,4},{2,6},{5,1},{7,3},{8,12},{10,14},{13,9},{15,11},{16,20},{18,... | collective-permute-start | bytes 1572872 | tf_op jit(solution)/shard_map/ppermute | solution.py:75
  101.9 36.6 %collective-permute-start.16 = (bf16[128,2048]{1,0:T(8,128)(2,1)S(1)}, bf16[128,2048]{1,0:T(8,128)(2,1)}, u32[]{:S(2)}, u32[]{:S(2)}) collective-permute-start(bf16[128,2048]{1,0:T(8,128)(2,1)S(1)} %collective-permute-done.13.refs_0_), channel_id=1, source_target_pairs={{1,3},{3,1},{4,6},{6,4},{9,11},{11,9},{12,14},{14,12},{17,19},{19,... | collective-permute-start | bytes 1572872 | tf_op jit(solution)/shard_map/ppermute | solution.py:75
  105.1 34.9 %collective-permute-start.20 = (bf16[128,2048]{1,0:T(8,128)(2,1)}, bf16[128,2048]{1,0:T(8,128)(2,1)}, u32[]{:S(2)}, u32[]{:S(2)}) collective-permute-start(bf16[128,2048]{1,0:T(8,128)(2,1)} %get-tuple-element.197.refs_4_), channel_id=1, source_target_pairs={{1,0},{3,2},{4,5},{6,7},{9,8},{11,10},{12,13},{14,15},{17,16},{19,... | collective-permute-start | bytes 1572872 | tf_op jit(solution)/shard_map/ppermute | solution.py:75
  108.0 30.7 %collective-permute-start.18 = (bf16[128,2048]{1,0:T(8,128)(2,1)}, bf16[128,2048]{1,0:T(8,128)(2,1)}, u32[]{:S(2)}, u32[]{:S(2)}) collective-permute-start(bf16[128,2048]{1,0:T(8,128)(2,1)} %get-tuple-element.197.refs_4_), channel_id=1, source_target_pairs={{1,4},{3,6},{4,1},{6,3},{0,2},{2,0},{5,7},{7,5},{9,12},{11,14},{12... | collective-permute-start | bytes 1572872 | tf_op jit(solution)/shard_map/ppermute | solution.py:75
  138.7 19.2 %collective-permute-start.22 = (bf16[128,2048]{1,0:T(8,128)(2,1)}, bf16[128,2048]{1,0:T(8,128)(2,1)S(1)}, u32[]{:S(2)}, u32[]{:S(2)}) collective-permute-start(bf16[128,2048]{1,0:T(8,128)(2,1)} %collective-permute-done.18.refs_0_), channel_id=1, source_target_pairs={{0,4},{2,6},{5,1},{7,3},{8,12},{10,14},{13,9},{15,11},{16,20},{18,... | collective-permute-start | bytes 1572872 | tf_op jit(solution)/shard_map/ppermute | solution.py:75
  140.0 19.3 %collective-permute-start.21 = (bf16[128,2048]{1,0:T(8,128)(2,1)}, bf16[128,2048]{1,0:T(8,128)(2,1)S(1)}, u32[]{:S(2)}, u32[]{:S(2)}) collective-permute-start(bf16[128,2048]{1,0:T(8,128)(2,1)} %collective-permute-done.18.refs_0_), channel_id=1, source_target_pairs={{1,3},{3,1},{4,6},{6,4},{9,11},{11,9},{12,14},{14,12},{17,19},{19,... | collective-permute-start | bytes 1572872 | tf_op jit(solution)/shard_map/ppermute | solution.py:75
  143.3 47.5 %collective-permute-start.12 = (bf16[128,2048]{1,0:T(8,128)(2,1)}, bf16[128,2048]{1,0:T(8,128)(2,1)S(1)}, u32[]{:S(2)}, u32[]{:S(2)}) collective-permute-start(bf16[128,2048]{1,0:T(8,128)(2,1)} %get-tuple-element.183), channel_id=1, source_target_pairs={{0,1},{2,3},{5,4},{7,6},{8,9},{10,11},{13,12},{15,14},{16,17},{18,... | collective-permute-start | bytes 1572872 | tf_op jit(solution)/shard_map/ppermute | solution.py:75
  146.1 65.1 %collective-permute-start.28 = (bf16[256,3072]{1,0:T(8,128)(2,1)S(1)}, bf16[256,3072]{1,0:T(8,128)(2,1)S(1)}, u32[]{:S(2)}, u32[]{:S(2)}) collective-permute-start(bf16[256,3072]{1,0:T(8,128)(2,1)S(1)} %pad_maximum_fusion.1), channel_id=1, source_target_pairs={{1,4},{3,6},{4,1},{6,3},{9,12},{11,14},{12,9},{14,11},{17,20},{19,... | collective-permute-start | bytes 4718600 | tf_op jit(solution)/shard_map/ppermute | solution.py:75
  150.6 41.6 %collective-permute-start.29 = (bf16[128,2048]{1,0:T(8,128)(2,1)S(1)}, bf16[128,2048]{1,0:T(8,128)(2,1)}, u32[]{:S(2)}, u32[]{:S(2)}) collective-permute-start(bf16[128,2048]{1,0:T(8,128)(2,1)S(1)} %copy-done.13), channel_id=1, source_target_pairs={{1,4},{3,6},{4,1},{6,3},{0,2},{2,0},{5,7},{7,5},{9,12},{11,14},{12... | collective-permute-start | bytes 1572872 | tf_op jit(solution)/shard_map/ppermute | solution.py:75
  157.8 34.4 %collective-permute-start.11 = (bf16[128,2048]{1,0:T(8,128)(2,1)}, bf16[128,2048]{1,0:T(8,128)(2,1)S(1)}, u32[]{:S(2)}, u32[]{:S(2)}) collective-permute-start(bf16[128,2048]{1,0:T(8,128)(2,1)} %get-tuple-element.184), channel_id=1, source_target_pairs={{4,0},{6,2},{1,5},{3,7},{2,1},{0,3},{7,4},{5,6},{12,8},{14,10},{9,... | collective-permute-start | bytes 1572872 | tf_op jit(solution)/shard_map/ppermute | solution.py:75
  160.1 33.5 %collective-permute-start.10 = (bf16[128,2048]{1,0:T(8,128)(2,1)S(1)}, bf16[128,2048]{1,0:T(8,128)(2,1)S(1)}, u32[]{:S(2)}, u32[]{:S(2)}) collective-permute-start(bf16[128,2048]{1,0:T(8,128)(2,1)S(1)} %add_convert_fusion.7), channel_id=1, source_target_pairs={{4,1},{6,3},{1,4},{3,6},{2,0},{0,2},{7,5},{5,7},{12,9},{14,11},{9,... | collective-permute-start | bytes 1572872 | tf_op jit(solution)/shard_map/ppermute | solution.py:75
  212.5 323.3 %reduce-scatter.4.cloned.1.call-start = ((), (), s32[]{:S(2)}) async-start(), calls=%async_computation.6 | async-start | bytes 14155776 | tf_op jit(solution)/shard_map/reduce_scatter | solution.py:575
  214.3 16.5 %collective-permute-start.23 = (bf16[128,2048]{1,0:T(8,128)(2,1)S(1)}, bf16[128,2048]{1,0:T(8,128)(2,1)S(1)}, u32[]{:S(2)}, u32[]{:S(2)}) collective-permute-start(bf16[128,2048]{1,0:T(8,128)(2,1)S(1)} %multiply_convert_fusion.7.refs_4_), channel_id=1, source_target_pairs={{1,4},{3,6},{4,1},{6,3},{0,2},{2,0},{5,7},{7,5},{9,12},{11,14},{12... | collective-permute-start | bytes 1572872 | tf_op jit(solution)/shard_map/ppermute | solution.py:75
  215.5 16.6 %collective-permute-start.35 = (bf16[128,2048]{1,0:T(8,128)(2,1)}, bf16[128,2048]{1,0:T(8,128)(2,1)S(1)}, u32[]{:S(2)}, u32[]{:S(2)}) collective-permute-start(bf16[128,2048]{1,0:T(8,128)(2,1)} %get-tuple-element.224), channel_id=1, source_target_pairs={{3,1},{1,3},{6,4},{4,6},{11,9},{9,11},{14,12},{12,14},{19,17},{17,... | collective-permute-start | bytes 1572872 | tf_op jit(solution)/shard_map/ppermute | solution.py:75
  218.8 18.2 %collective-permute-start.38 = (bf16[128,2048]{1,0:T(8,128)(2,1)}, bf16[128,2048]{1,0:T(8,128)(2,1)S(1)}, u32[]{:S(2)}, u32[]{:S(2)}) collective-permute-start(bf16[128,2048]{1,0:T(8,128)(2,1)} %get-tuple-element.224), channel_id=1, source_target_pairs={{0,1},{2,3},{5,4},{7,6},{8,9},{10,11},{13,12},{15,14},{16,17},{18,... | collective-permute-start | bytes 1572872 | tf_op jit(solution)/shard_map/ppermute | solution.py:75
  220.1 17.0 %collective-permute-start.25 = (bf16[128,2048]{1,0:T(8,128)(2,1)S(1)}, bf16[128,2048]{1,0:T(8,128)(2,1)S(1)}, u32[]{:S(2)}, u32[]{:S(2)}) collective-permute-start(bf16[128,2048]{1,0:T(8,128)(2,1)S(1)} %multiply_convert_fusion.7.refs_4_), channel_id=1, source_target_pairs={{1,0},{3,2},{4,5},{6,7},{9,8},{11,10},{12,13},{14,15},{17,16},{19,... | collective-permute-start | bytes 1572872 | tf_op jit(solution)/shard_map/ppermute | solution.py:75
  223.2 14.0 %collective-permute-start.24 = (bf16[128,2048]{1,0:T(8,128)(2,1)S(1)}, bf16[128,2048]{1,0:T(8,128)(2,1)S(1)}, u32[]{:S(2)}, u32[]{:S(2)}) collective-permute-start(bf16[128,2048]{1,0:T(8,128)(2,1)S(1)} %multiply_convert_fusion.7.refs_4_), channel_id=1, source_target_pairs={{0,4},{2,6},{5,1},{7,3},{1,2},{3,0},{4,7},{6,5},{8,12},{10,14},{13... | collective-permute-start | bytes 1572872 | tf_op jit(solution)/shard_map/ppermute | solution.py:75
  232.1 15.2 %collective-permute-start.26 = (bf16[128,2048]{1,0:T(8,128)(2,1)S(1)}, bf16[128,2048]{1,0:T(8,128)(2,1)}, u32[]{:S(2)}, u32[]{:S(2)}) collective-permute-start(bf16[128,2048]{1,0:T(8,128)(2,1)S(1)} %collective-permute-done.23.refs_0_), channel_id=1, source_target_pairs={{1,3},{3,1},{4,6},{6,4},{9,11},{11,9},{12,14},{14,12},{17,19},{19,... | collective-permute-start | bytes 1572872 | tf_op jit(solution)/shard_map/ppermute | solution.py:75
  237.0 13.9 %collective-permute-start.37 = (bf16[128,2048]{1,0:T(8,128)(2,1)}, bf16[128,2048]{1,0:T(8,128)(2,1)S(1)}, u32[]{:S(2)}, u32[]{:S(2)}) collective-permute-start(bf16[128,2048]{1,0:T(8,128)(2,1)} %get-tuple-element.225), channel_id=1, source_target_pairs={{4,0},{6,2},{1,5},{3,7},{2,1},{0,3},{7,4},{5,6},{12,8},{14,10},{9,... | collective-permute-start | bytes 1572872 | tf_op jit(solution)/shard_map/ppermute | solution.py:75
  237.1 15.3 %collective-permute-start.36 = (bf16[128,2048]{1,0:T(8,128)(2,1)S(1)}, bf16[128,2048]{1,0:T(8,128)(2,1)S(1)}, u32[]{:S(2)}, u32[]{:S(2)}) collective-permute-start(bf16[128,2048]{1,0:T(8,128)(2,1)S(1)} %add_convert_fusion.6), channel_id=1, source_target_pairs={{4,1},{6,3},{1,4},{3,6},{2,0},{0,2},{7,5},{5,7},{12,9},{14,11},{9,... | collective-permute-start | bytes 1572872 | tf_op jit(solution)/shard_map/ppermute | solution.py:75
  253.2 17.4 %collective-permute-start.41 = (bf16[128,2048]{1,0:T(8,128)(2,1)S(1)}, bf16[128,2048]{1,0:T(8,128)(2,1)S(1)}, u32[]{:S(2)}, u32[]{:S(2)}) collective-permute-start(bf16[128,2048]{1,0:T(8,128)(2,1)S(1)} %multiply_convert_fusion.6.refs_4_), channel_id=1, source_target_pairs={{1,0},{3,2},{4,5},{6,7},{9,8},{11,10},{12,13},{14,15},{17,16},{19,... | collective-permute-start | bytes 1572872 | tf_op jit(solution)/shard_map/ppermute | solution.py:75
  263.3 13.8 %collective-permute-start.42 = (bf16[128,2048]{1,0:T(8,128)(2,1)S(1)}, bf16[128,2048]{1,0:T(8,128)(2,1)S(1)}, u32[]{:S(2)}, u32[]{:S(2)}) collective-permute-start(bf16[128,2048]{1,0:T(8,128)(2,1)S(1)} %collective-permute-done.39.refs_0_), channel_id=1, source_target_pairs={{1,3},{3,1},{4,6},{6,4},{9,11},{11,9},{12,14},{14,12},{17,19},{19,... | collective-permute-start | bytes 1572872 | tf_op jit(solution)/shard_map/ppermute | solution.py:75
  320.8 293.7 %reduce-scatter.6.cloned.1.call-start = ((), (), s32[]{:S(2)}) async-start(), calls=%async_computation.7 | async-start | bytes 14155776 | tf_op jit(solution)/shard_map/reduce_scatter | solution.py:575
  370.0 287.1 %reduce-scatter.8.cloned.1.call-start = ((), (), s32[]{:S(2)}) async-start(), calls=%async_computation.8 | async-start | bytes 5898240 | tf_op jit(solution)/shard_map/reduce_scatter | solution.py:575
  384.6 43.6 %collective-permute-start.54 = (bf16[128,2048]{1,0:T(8,128)(2,1)}, bf16[128,2048]{1,0:T(8,128)(2,1)S(1)}, u32[]{:S(2)}, u32[]{:S(2)}) collective-permute-start(bf16[128,2048]{1,0:T(8,128)(2,1)} %get-tuple-element.267), channel_id=1, source_target_pairs={{4,0},{6,2},{1,5},{3,7},{12,8},{14,10},{9,13},{11,15},{20,16},{22,... | collective-permute-start | bytes 1572872 | tf_op jit(solution)/shard_map/ppermute | solution.py:75
  387.7 41.9 %collective-permute-start.55 = (bf16[128,2048]{1,0:T(8,128)(2,1)}, bf16[128,2048]{1,0:T(8,128)(2,1)S(1)}, u32[]{:S(2)}, u32[]{:S(2)}) collective-permute-start(bf16[128,2048]{1,0:T(8,128)(2,1)} %get-tuple-element.268), channel_id=1, source_target_pairs={{3,1},{1,3},{6,4},{4,6},{11,9},{9,11},{14,12},{12,14},{19,17},{17,... | collective-permute-start | bytes 1572872 | tf_op jit(solution)/shard_map/ppermute | solution.py:75
  405.6 29.3 %collective-permute-start.53 = (bf16[128,2048]{1,0:T(8,128)(2,1)}, bf16[128,2048]{1,0:T(8,128)(2,1)S(1)}, u32[]{:S(2)}, u32[]{:S(2)}) collective-permute-start(bf16[128,2048]{1,0:T(8,128)(2,1)} %get-tuple-element.265), channel_id=1, source_target_pairs={{0,1},{2,3},{5,4},{7,6},{8,9},{10,11},{13,12},{15,14},{16,17},{18,... | collective-permute-start | bytes 1572872 | tf_op jit(solution)/shard_map/ppermute | solution.py:75
  406.9 36.9 %collective-permute-start.50 = (bf16[128,2048]{1,0:T(8,128)(2,1)}, bf16[128,2048]{1,0:T(8,128)(2,1)S(1)}, u32[]{:S(2)}, u32[]{:S(2)}) collective-permute-start(bf16[128,2048]{1,0:T(8,128)(2,1)} %get-tuple-element.265), channel_id=1, source_target_pairs={{3,1},{1,3},{6,4},{4,6},{11,9},{9,11},{14,12},{12,14},{19,17},{17,... | collective-permute-start | bytes 1572872 | tf_op jit(solution)/shard_map/ppermute | solution.py:75
  409.0 25.9 %collective-permute-start.58 = (bf16[128,2048]{1,0:T(8,128)(2,1)S(1)}, bf16[128,2048]{1,0:T(8,128)(2,1)}, u32[]{:S(2)}, u32[]{:S(2)}) collective-permute-start(bf16[128,2048]{1,0:T(8,128)(2,1)S(1)} %copy-done.70), channel_id=1, source_target_pairs={{0,1},{2,3},{5,4},{7,6},{8,9},{10,11},{13,12},{15,14},{16,17},{18,... | collective-permute-start | bytes 1572872 | tf_op jit(solution)/shard_map/ppermute | solution.py:75
  428.2 46.4 %collective-permute-start.73 = (bf16[128,2048]{1,0:T(8,128)(2,1)}, bf16[128,2048]{1,0:T(8,128)(2,1)S(1)}, u32[]{:S(2)}, u32[]{:S(2)}) collective-permute-start(bf16[128,2048]{1,0:T(8,128)(2,1)} %get-tuple-element.295), channel_id=1, source_target_pairs={{0,1},{2,3},{5,4},{7,6},{8,9},{10,11},{13,12},{15,14},{16,17},{18,... | collective-permute-start | bytes 1572872 | tf_op jit(solution)/shard_map/ppermute | solution.py:75
  435.0 18.9 %collective-permute-start.56 = (bf16[128,2048]{1,0:T(8,128)(2,1)S(1)}, bf16[128,2048]{1,0:T(8,128)(2,1)S(1)}, u32[]{:S(2)}, u32[]{:S(2)}) collective-permute-start(bf16[128,2048]{1,0:T(8,128)(2,1)S(1)} %add_convert_fusion.3), channel_id=1, source_target_pairs={{4,1},{6,3},{1,4},{3,6},{2,0},{0,2},{7,5},{5,7},{12,9},{14,11},{9,... | collective-permute-start | bytes 1572872 | tf_op jit(solution)/shard_map/ppermute | solution.py:75
  440.6 35.2 %collective-permute-start.70 = (bf16[128,2048]{1,0:T(8,128)(2,1)}, bf16[128,2048]{1,0:T(8,128)(2,1)S(1)}, u32[]{:S(2)}, u32[]{:S(2)}) collective-permute-start(bf16[128,2048]{1,0:T(8,128)(2,1)} %get-tuple-element.295), channel_id=1, source_target_pairs={{3,1},{1,3},{6,4},{4,6},{11,9},{9,11},{14,12},{12,14},{19,17},{17,... | collective-permute-start | bytes 1572872 | tf_op jit(solution)/shard_map/ppermute | solution.py:75
  443.8 30.2 %collective-permute-start.69 = (bf16[128,2048]{1,0:T(8,128)(2,1)S(1)}, bf16[128,2048]{1,0:T(8,128)(2,1)S(1)}, u32[]{:S(2)}, u32[]{:S(2)}) collective-permute-start(bf16[128,2048]{1,0:T(8,128)(2,1)S(1)} %copy-done.30), channel_id=1, source_target_pairs={{4,0},{6,2},{1,5},{3,7},{12,8},{14,10},{9,13},{11,15},{20,16},{22,... | collective-permute-start | bytes 1572872 | tf_op jit(solution)/shard_map/ppermute | solution.py:75
  446.2 16.9 %collective-permute-start.52 = (bf16[128,2048]{1,0:T(8,128)(2,1)S(1)}, bf16[128,2048]{1,0:T(8,128)(2,1)S(1)}, u32[]{:S(2)}, u32[]{:S(2)}) collective-permute-start(bf16[128,2048]{1,0:T(8,128)(2,1)S(1)} %copy-done.68), channel_id=1, source_target_pairs={{4,0},{6,2},{1,5},{3,7},{2,1},{0,3},{7,4},{5,6},{12,8},{14,10},{9,... | collective-permute-start | bytes 1572872 | tf_op jit(solution)/shard_map/ppermute | solution.py:75
  453.9 16.9 %collective-permute-start.51 = (bf16[128,2048]{1,0:T(8,128)(2,1)S(1)}, bf16[128,2048]{1,0:T(8,128)(2,1)S(1)}, u32[]{:S(2)}, u32[]{:S(2)}) collective-permute-start(bf16[128,2048]{1,0:T(8,128)(2,1)S(1)} %add_convert_fusion.4), channel_id=1, source_target_pairs={{4,1},{6,3},{1,4},{3,6},{2,0},{0,2},{7,5},{5,7},{12,9},{14,11},{9,... | collective-permute-start | bytes 1572872 | tf_op jit(solution)/shard_map/ppermute | solution.py:75
  476.4 18.0 %collective-permute-start.68 = (bf16[128,2048]{1,0:T(8,128)(2,1)S(1)}, bf16[128,2048]{1,0:T(8,128)(2,1)S(1)}, u32[]{:S(2)}, u32[]{:S(2)}) collective-permute-start(bf16[128,2048]{1,0:T(8,128)(2,1)S(1)} %collective-permute-done.64.refs_0_), channel_id=1, source_target_pairs={{0,4},{2,6},{5,1},{7,3},{8,12},{10,14},{13,9},{15,11},{16,20},{18,... | collective-permute-start | bytes 1572872 | tf_op jit(solution)/shard_map/ppermute | solution.py:75
  477.7 17.5 %collective-permute-start.67 = (bf16[128,2048]{1,0:T(8,128)(2,1)S(1)}, bf16[128,2048]{1,0:T(8,128)(2,1)S(1)}, u32[]{:S(2)}, u32[]{:S(2)}) collective-permute-start(bf16[128,2048]{1,0:T(8,128)(2,1)S(1)} %collective-permute-done.64.refs_0_), channel_id=1, source_target_pairs={{1,3},{3,1},{4,6},{6,4},{9,11},{11,9},{12,14},{14,12},{17,19},{19,... | collective-permute-start | bytes 1572872 | tf_op jit(solution)/shard_map/ppermute | solution.py:75
  487.5 37.5 %collective-permute-start.60 = (bf16[128,2048]{1,0:T(8,128)(2,1)S(1)}, bf16[128,2048]{1,0:T(8,128)(2,1)S(1)}, u32[]{:S(2)}, u32[]{:S(2)}) collective-permute-start(bf16[128,2048]{1,0:T(8,128)(2,1)S(1)} %get-tuple-element.292.refs_4_), channel_id=1, source_target_pairs={{0,4},{2,6},{5,1},{7,3},{1,2},{3,0},{4,7},{6,5},{8,12},{10,14},{13... | collective-permute-start | bytes 1572872 | tf_op jit(solution)/shard_map/ppermute | solution.py:75
  487.5 40.9 %collective-permute-start.63 = (bf16[128,2048]{1,0:T(8,128)(2,1)S(1)}, bf16[128,2048]{1,0:T(8,128)(2,1)}, u32[]{:S(2)}, u32[]{:S(2)}) collective-permute-start(bf16[128,2048]{1,0:T(8,128)(2,1)S(1)} %collective-permute-done.59.refs_0_), channel_id=1, source_target_pairs={{0,4},{2,6},{5,1},{7,3},{8,12},{10,14},{13,9},{15,11},{16,20},{18,... | collective-permute-start | bytes 1572872 | tf_op jit(solution)/shard_map/ppermute | solution.py:75
  488.8 42.1 %collective-permute-start.62 = (bf16[128,2048]{1,0:T(8,128)(2,1)S(1)}, bf16[128,2048]{1,0:T(8,128)(2,1)}, u32[]{:S(2)}, u32[]{:S(2)}) collective-permute-start(bf16[128,2048]{1,0:T(8,128)(2,1)S(1)} %collective-permute-done.59.refs_0_), channel_id=1, source_target_pairs={{1,3},{3,1},{4,6},{6,4},{9,11},{11,9},{12,14},{14,12},{17,19},{19,... | collective-permute-start | bytes 1572872 | tf_op jit(solution)/shard_map/ppermute | solution.py:75
  494.4 40.1 %collective-permute-start.72 = (bf16[128,2048]{1,0:T(8,128)(2,1)}, bf16[128,2048]{1,0:T(8,128)(2,1)S(1)}, u32[]{:S(2)}, u32[]{:S(2)}) collective-permute-start(bf16[128,2048]{1,0:T(8,128)(2,1)} %get-tuple-element.296), channel_id=1, source_target_pairs={{4,0},{6,2},{1,5},{3,7},{2,1},{0,3},{7,4},{5,6},{12,8},{14,10},{9,... | collective-permute-start | bytes 1572872 | tf_op jit(solution)/shard_map/ppermute | solution.py:75
  495.2 39.3 %collective-permute-start.71 = (bf16[128,2048]{1,0:T(8,128)(2,1)S(1)}, bf16[128,2048]{1,0:T(8,128)(2,1)S(1)}, u32[]{:S(2)}, u32[]{:S(2)}) collective-permute-start(bf16[128,2048]{1,0:T(8,128)(2,1)S(1)} %add_convert_fusion.2), channel_id=1, source_target_pairs={{4,1},{6,3},{1,4},{3,6},{2,0},{0,2},{7,5},{5,7},{12,9},{14,11},{9,... | collective-permute-start | bytes 1572872 | tf_op jit(solution)/shard_map/ppermute | solution.py:75
  525.0 17.7 %collective-permute-start.44 = (bf16[128,2048]{1,0:T(8,128)(2,1)}, bf16[128,2048]{1,0:T(8,128)(2,1)}, u32[]{:S(2)}, u32[]{:S(2)}) collective-permute-start(bf16[128,2048]{1,0:T(8,128)(2,1)} %get-tuple-element.261), channel_id=1, source_target_pairs={{4,0},{6,2},{1,5},{3,7},{12,8},{14,10},{9,13},{11,15},{20,16},{22,... | collective-permute-start | bytes 1572872 | tf_op jit(solution)/shard_map/ppermute | solution.py:75
  528.4 14.3 %collective-permute-start.45 = (bf16[128,2048]{1,0:T(8,128)(2,1)}, bf16[128,2048]{1,0:T(8,128)(2,1)}, u32[]{:S(2)}, u32[]{:S(2)}) collective-permute-start(bf16[128,2048]{1,0:T(8,128)(2,1)} %get-tuple-element.262), channel_id=1, source_target_pairs={{3,1},{1,3},{6,4},{4,6},{11,9},{9,11},{14,12},{12,14},{19,17},{17,... | collective-permute-start | bytes 1572872 | tf_op jit(solution)/shard_map/ppermute | solution.py:75
  535.8 35.7 %collective-permute-start.84 = (bf16[256,3072]{1,0:T(8,128)(2,1)}, bf16[256,3072]{1,0:T(8,128)(2,1)S(1)}, u32[]{:S(2)}, u32[]{:S(2)}) collective-permute-start(bf16[256,3072]{1,0:T(8,128)(2,1)} %bitcast.75), channel_id=1, source_target_pairs={{1,4},{3,6},{4,1},{6,3},{9,12},{11,14},{12,9},{14,11},{17,20},{19,... | collective-permute-start | bytes 4718600 | tf_op jit(solution)/shard_map/ppermute | solution.py:75
  541.6 23.9 %collective-permute-start.47 = (bf16[128,2048]{1,0:T(8,128)(2,1)}, bf16[128,2048]{1,0:T(8,128)(2,1)S(1)}, u32[]{:S(2)}, u32[]{:S(2)}) collective-permute-start(bf16[128,2048]{1,0:T(8,128)(2,1)} %get-tuple-element.263), channel_id=1, source_target_pairs={{4,0},{6,2},{1,5},{3,7},{2,1},{0,3},{7,4},{5,6},{12,8},{14,10},{9,... | collective-permute-start | bytes 1572872 | tf_op jit(solution)/shard_map/ppermute | solution.py:75
  544.2 26.1 %collective-permute-start.46 = (bf16[128,2048]{1,0:T(8,128)(2,1)S(1)}, bf16[128,2048]{1,0:T(8,128)(2,1)S(1)}, u32[]{:S(2)}, u32[]{:S(2)}) collective-permute-start(bf16[128,2048]{1,0:T(8,128)(2,1)S(1)} %add_convert_fusion.5), channel_id=1, source_target_pairs={{4,1},{6,3},{1,4},{3,6},{2,0},{0,2},{7,5},{5,7},{12,9},{14,11},{9,... | collective-permute-start | bytes 1572872 | tf_op jit(solution)/shard_map/ppermute | solution.py:75
  588.4 15.9 %collective-permute-start.83 = (bf16[128,2048]{1,0:T(8,128)(2,1)}, bf16[128,2048]{1,0:T(8,128)(2,1)S(1)}, u32[]{:S(2)}, u32[]{:S(2)}) collective-permute-start(bf16[128,2048]{1,0:T(8,128)(2,1)} %get-tuple-element.314), channel_id=1, source_target_pairs={{0,1},{2,3},{5,4},{7,6},{8,9},{10,11},{13,12},{15,14},{16,17},{18,... | collective-permute-start | bytes 1572872 | tf_op jit(solution)/shard_map/ppermute | solution.py:75
  589.9 26.7 %collective-permute-start.82 = (bf16[128,2048]{1,0:T(8,128)(2,1)}, bf16[128,2048]{1,0:T(8,128)(2,1)}, u32[]{:S(2)}, u32[]{:S(2)}) collective-permute-start(bf16[128,2048]{1,0:T(8,128)(2,1)} %get-tuple-element.315), channel_id=1, source_target_pairs={{4,0},{6,2},{1,5},{3,7},{2,1},{0,3},{7,4},{5,6},{12,8},{14,10},{9,... | collective-permute-start | bytes 1572872 | tf_op jit(solution)/shard_map/ppermute | solution.py:75
  592.3 14.2 %collective-permute-start.74 = (bf16[128,2048]{1,0:T(8,128)(2,1)}, bf16[128,2048]{1,0:T(8,128)(2,1)S(1)}, u32[]{:S(2)}, u32[]{:S(2)}) collective-permute-start(bf16[128,2048]{1,0:T(8,128)(2,1)} %get-tuple-element.310), channel_id=1, source_target_pairs={{4,0},{6,2},{1,5},{3,7},{12,8},{14,10},{9,13},{11,15},{20,16},{22,... | collective-permute-start | bytes 1572872 | tf_op jit(solution)/shard_map/ppermute | solution.py:75
  594.6 16.2 %collective-permute-start.75 = (bf16[128,2048]{1,0:T(8,128)(2,1)}, bf16[128,2048]{1,0:T(8,128)(2,1)S(1)}, u32[]{:S(2)}, u32[]{:S(2)}) collective-permute-start(bf16[128,2048]{1,0:T(8,128)(2,1)} %get-tuple-element.311), channel_id=1, source_target_pairs={{3,1},{1,3},{6,4},{4,6},{11,9},{9,11},{14,12},{12,14},{19,17},{17,... | collective-permute-start | bytes 1572872 | tf_op jit(solution)/shard_map/ppermute | solution.py:75
  601.3 15.3 %collective-permute-start.81 = (bf16[128,2048]{1,0:T(8,128)(2,1)}, bf16[128,2048]{1,0:T(8,128)(2,1)}, u32[]{:S(2)}, u32[]{:S(2)}) collective-permute-start(bf16[128,2048]{1,0:T(8,128)(2,1)} %add_convert_fusion), channel_id=1, source_target_pairs={{4,1},{6,3},{1,4},{3,6},{2,0},{0,2},{7,5},{5,7},{12,9},{14,11},{9,... | collective-permute-start | bytes 1572872 | tf_op jit(solution)/shard_map/ppermute | solution.py:75
  606.5 14.7 %collective-permute-start.77 = (bf16[128,2048]{1,0:T(8,128)(2,1)}, bf16[128,2048]{1,0:T(8,128)(2,1)}, u32[]{:S(2)}, u32[]{:S(2)}) collective-permute-start(bf16[128,2048]{1,0:T(8,128)(2,1)} %get-tuple-element.312), channel_id=1, source_target_pairs={{4,0},{6,2},{1,5},{3,7},{2,1},{0,3},{7,4},{5,6},{12,8},{14,10},{9,... | collective-permute-start | bytes 1572872 | tf_op jit(solution)/shard_map/ppermute | solution.py:75
  614.5 25.4 %collective-permute-start.85 = (bf16[256,3072]{1,0:T(8,128)(2,1)}, bf16[256,3072]{1,0:T(8,128)(2,1)S(1)}, u32[]{:S(2)}, u32[]{:S(2)}) collective-permute-start(bf16[256,3072]{1,0:T(8,128)(2,1)} %bitcast.73), channel_id=1, source_target_pairs={{1,4},{3,6},{4,1},{6,3},{9,12},{11,14},{12,9},{14,11},{17,20},{19,... | collective-permute-start | bytes 4718600 | tf_op jit(solution)/shard_map/ppermute | solution.py:75
  624.8 16.4 %collective-permute-start.86 = (f32[2,1024]{1,0:T(2,128)S(1)}, f32[2,1024]{1,0:T(2,128)S(1)}, u32[]{:S(2)}, u32[]{:S(2)}) collective-permute-start(f32[2,1024]{1,0:T(2,128)S(1)} %fusion.25), channel_id=1, source_target_pairs={{0,16},{8,24},{16,0},{24,8},{1,17},{9,25},{17,1},{25,9},{2,18},{10... | collective-permute-start | bytes 24584 | tf_op jit(solution)/shard_map/ppermute | solution.py:151
  (108 other events, 1111.5 us)
Sparse Core Ops, SparseCore 0:
  30.5 56.2 all-gather.3
  88.4 115.6 all-gather.5
  212.6 117.9 all-gather.7
  332.8 124.8 reduce-scatter.3
  459.9 127.5 reduce-scatter.5
  589.6 58.5 reduce-scatter.7

commit v3 on v2

--- a/solution.py
+++ b/solution.py
@@ -657,12 +657,12 @@
     branch.append(send_rows(after(branch_rows[1], found[0][0])))
     branch_grads = [order(join_rows, branch[0], starts)]
     units_piece.append(trade(after(unit_columns(1), found[0][0])))
+    units_weight.append(gather_z(order(lambda a: a, units_piece[1])))
     found.append(order(lambda a: forward(1, a), tokens_all[1]))
     sums.append(send_sums(order(out_project, found[1][3])))
     entered = [order(lambda a: enter(0, a), sums[0])]
     here = [send_rows(entered[0][0])]
     branch_grads.append(order(join_rows, branch[1], starts))
-    units_weight.append(gather_z(order(lambda a: a, units_piece[1])))
     second_all = [order(join_rows, here[0], starts)]
     entered.append(order(lambda a: enter(1, a), sums[1]))
     here.append(send_rows(entered[1][0]))

time: 693 us -> 689 us (level)
  starting transfers between devices: 166 us -> 176 us
  waiting for transfers between devices: 175 us -> 165 us
    all_gather x3, waiting for transfers between devices: 9.82 us -> 0.04 us  [gather_z(): return lax.all_gather(piece, ('hi', 'core'), axis=0, tiled=True)]
    ppermute x87, starting transfers between devices: 161 us -> 169 us  [send(): return lax.ppermute(values, ('lo', 'y', 'core'), pairs)]
  transfers between devices with their start and end apart: 98 -> 98, of which waited for: 38 -> 33; matrix products, arithmetic and copies ran while one was open for 9% -> 9% of each run, Pallas kernels for 37% -> 37%
where the time goes in v3:
time: 689 us; the launch traced here: 678 us
  Pallas kernels  250 us (36%)
  starting transfers between devices  176 us (26%)
  waiting for transfers between devices  165 us (24%)
  other arithmetic  52.3 us (8%)
  between operations  17.8 us (3%)
  local copies, waits for them, and re-layouts  17.1 us (2%)
    ppermute x87, starting transfers between devices, send(): return lax.ppermute(values, ('lo', 'y', 'core'), pairs)  169 us
    ppermute x87, waiting for transfers between devices, send(): return lax.ppermute(values, ('lo', 'y', 'core'), pairs)  160 us
    pallas_call x8, Pallas kernels, project(): pl.pallas_call(functools.partial(project_kernel, len(lhs), rows), grid=(w...  68 us
    pallas_call x3, Pallas kernels, weight_grads(): pl.pallas_call(functools.partial(grads_kernel, plan), grid=(count * slab...  50.6 us
    pallas_call x2, Pallas kernels, mlp(): pl.pallas_call(functools.partial(mlp_kernel, count), grid=(steps,), out_s...  39.8 us
    pallas_call x2, Pallas kernels, attend_back(): pl.pallas_call(functools.partial(backward_kernel, m, heads, last), grid=(...  33.3 us
    pallas_call x2, Pallas kernels, attend(): pl.pallas_call(functools.partial(forward_kernel, m, heads), grid=(groups,...  29.4 us
    pallas_call x8, Pallas kernels, join_rows(): pl.pallas_call(assemble_kernel, out_shape=jax.ShapeDtypeStruct((4 * rows,...  28.5 us
  transfers between devices with their start and end apart: 98, of which 33 were waited for; matrix products, arithmetic and copies ran while one was open for 9% of the time, Pallas kernels for 37%

profile of v3, /device:TPU:1, one launch (start us, length us, event | category | flops | bytes accessed | tf_op | source)
XLA Modules:
  0.0 677.7 jit_solution(11755041243705105994)
XLA Ops:
  7.2 4.5 collective-permute-start
  19.2 10.4 %collective-permute-done.1 = bf16[256,1280]{1,0:T(8,128)(2,1)S(1)} collective-permute-done((bf16[256,1280]{1,0:T(8,128)(2,1)S(1)}, bf16[256,1280]{1,0:T(8,128)(2,1)S(1)}, u32[]{:S(2)}, u32[]{:S(2)}) %collective-permute-start.1) | collective-permute-done | bytes 655392 | tf_op jit(solution)/shard_map/ppermute | solution.py:75
  41.3 26.6 %collective-permute-done.2.refs_0_ = bf16[128,2048]{1,0:T(8,128)(2,1)} collective-permute-done((bf16[128,2048]{1,0:T(8,128)(2,1)}, bf16[128,2048]{1,0:T(8,128)(2,1)}, u32[]{:S(2)}, u32[]{:S(2)}) %collective-permute-start.2) | collective-permute-done | bytes 524320 | tf_op jit(solution)/shard_map/ppermute | solution.py:75
  69.2 3.1 collective-permute-start.5
  73.1 5.4 collective-permute-done.6.refs_5_
  79.8 3.5 assemble.8.refs_0_
  93.3 12.8 %attend.2 = (bf16[512,512]{1,0:T(8,128)(2,1)}, bf16[512,256]{1,0:T(8,128)(2,1)}, f32[2,4,512]{2,1,0:T(4,128)}, bf16[512,512]{1,0:T(8,128)(2,1)}, f32[512,128]{1,0:T(8,128)}) custom-call(s32[1]{0:T(128)S(6)} %select_n.165.lengths, bf16[512,2048]{1,0:T(8,128)(2,1)} %assemble.8.refs_0_, bf16[2048,1280]{1,0:T(8,128)(2,1)} %all-gather.4.cloned.1.call-done.refs_1_, ...), custom_call_target="tpu_custom_call" | custom-call | tf_op jit(solution)/shard_map/attend/pallas_call | solution.py:378
  111.5 3.1 collective-permute-start.16
  114.7 9.2 %collective-permute-done.14.refs_1_ = bf16[128,2048]{1,0:T(8,128)(2,1)S(1)} collective-permute-done((bf16[128,2048]{1,0:T(8,128)(2,1)}, bf16[128,2048]{1,0:T(8,128)(2,1)S(1)}, u32[]{:S(2)}, u32[]{:S(2)}) %collective-permute-start.14) | collective-permute-done | bytes 524320 | tf_op jit(solution)/shard_map/ppermute | solution.py:75
  125.2 9.9 %collective-permute-done.17.refs_5_ = bf16[128,2048]{1,0:T(8,128)(2,1)S(1)} collective-permute-done((bf16[128,2048]{1,0:T(8,128)(2,1)}, bf16[128,2048]{1,0:T(8,128)(2,1)S(1)}, u32[]{:S(2)}, u32[]{:S(2)}) %collective-permute-start.17) | collective-permute-done | bytes 524320 | tf_op jit(solution)/shard_map/ppermute | solution.py:75
  135.6 15.1 %collective-permute-done.19.refs_0_ = bf16[128,2048]{1,0:T(8,128)(2,1)S(1)} collective-permute-done((bf16[128,2048]{1,0:T(8,128)(2,1)S(1)}, bf16[128,2048]{1,0:T(8,128)(2,1)S(1)}, u32[]{:S(2)}, u32[]{:S(2)}) %collective-permute-start.19) | collective-permute-done | bytes 524320 | tf_op jit(solution)/shard_map/ppermute | solution.py:75
  152.0 3.3 collective-permute-start.22
  155.3 3.1 slice.135.refs_1_
  158.4 5.0 project.8
  163.5 3.5 assemble.9.refs_0_.refs_2_
  168.0 3.6 assemble.10.refs_2_.refs_6_
  173.0 3.2 collective-permute-start.8
  176.2 3.1 collective-permute-start.9
  183.3 5.0 collective-permute-done.9
  189.6 3.3 collective-permute-start.10
  195.7 16.6 %attend.3 = (bf16[512,512]{1,0:T(8,128)(2,1)}, bf16[512,256]{1,0:T(8,128)(2,1)}, f32[2,4,512]{2,1,0:T(4,128)}, bf16[512,512]{1,0:T(8,128)(2,1)}, f32[512,128]{1,0:T(8,128)}) custom-call(s32[1]{0:T(128)S(6)} %select_n.165.lengths, bf16[512,2048]{1,0:T(8,128)(2,1)} %assemble.9.refs_0_.refs_2_, bf16[2048,1280]{1,0:T(8,128)(2,1)} %all-gather.4.cloned.1.call-done.refs_1_, ...), custom_call_target="tpu_custom_call" | custom-call | tf_op jit(solution)/shard_map/attend/pallas_call | solution.py:378
  212.3 5.1 project.9
  217.3 4.0 collective-permute-start.32
  222.7 3.2 collective-permute-start.34
  232.4 5.4 collective-permute-start.25
  239.6 3.4 collective-permute-start.27
  245.0 3.6 assemble.11.refs_3_.refs_8_
  251.5 3.8 collective-permute-done.27.refs_3_
  255.4 3.5 assemble.12.refs_0_
  263.1 3.6 collective-permute-start.41
  266.7 4.3 collective-permute-done.39.refs_0_
  272.4 4.9 collective-permute-start.42
  277.3 6.5 collective-permute-done.43.refs_5_
  285.4 3.6 assemble.13.refs_1_.refs_2_
  289.0 19.9 %mlp.2 = (bf16[512,1024]{1,0:T(8,128)(2,1)}, bf16[512,1024]{1,0:T(8,128)(2,1)}, bf16[512,1024]{1,0:T(8,128)(2,1)}, bf16[512,1024]{1,0:T(8,128)(2,1)}, bf16[512,1...) custom-call(bf16[512,2048]{1,0:T(8,128)(2,1)} %assemble.12.refs_0_, bf16[512,2048]{1,0:T(8,128)(2,1)} %assemble.13.refs_1_.refs_2_, ...), custom_call_target="tpu_custom_call" | custom-call | tf_op jit(solution)/shard_map/mlp/pallas_call | solution.py:233
  308.8 19.3 %grads.3 = bf16[8,256,3072]{2,1,0:T(8,128)(2,1)} custom-call(bf16[512,2048]{1,0:T(8,128)(2,1)} %assemble.12.refs_0_, bf16[512,1024]{1,0:T(8,128)(2,1)} %get-tuple-element.255.refs_1_.refs_0_, bf16[512,2048]{1,0:T(8,128)(2,1)} %assemble.13.refs_1_.refs_2_, bf16[512,1024]{1,0:T(8,128)(2,1)} %get-tuple-element.253.refs_3_.refs_0_, ...), custom_call_target="tpu_custom_call" | custom-call | tf_op jit(solution)/shard_map/grads/pallas_call | solution.py:285
  328.2 20.0 %mlp.3 = (bf16[512,1024]{1,0:T(8,128)(2,1)}, bf16[512,1024]{1,0:T(8,128)(2,1)}, bf16[512,1024]{1,0:T(8,128)(2,1)}, bf16[512,1024]{1,0:T(8,128)(2,1)}, bf16[512,1...) custom-call(bf16[512,2048]{1,0:T(8,128)(2,1)} %assemble.12.refs_0_, bf16[512,2048]{1,0:T(8,128)(2,1)} %assemble.13.refs_1_.refs_2_, ...), custom_call_target="tpu_custom_call" | custom-call | tf_op jit(solution)/shard_map/mlp/pallas_call | solution.py:233
  348.2 19.2 %grads.4 = bf16[8,256,3072]{2,1,0:T(8,128)(2,1)} custom-call(bf16[512,2048]{1,0:T(8,128)(2,1)} %assemble.12.refs_0_, bf16[512,1024]{1,0:T(8,128)(2,1)} %get-tuple-element.248.refs_1_.refs_2_, bf16[512,2048]{1,0:T(8,128)(2,1)} %assemble.13.refs_1_.refs_2_, bf16[512,1024]{1,0:T(8,128)(2,1)} %get-tuple-element.249.refs_3_.refs_2_, ...), custom_call_target="tpu_custom_call" | custom-call | tf_op jit(solution)/shard_map/grads/pallas_call | solution.py:285
  367.5 14.5 %project.10 = (bf16[128,2048]{1,0:T(8,128)(2,1)}, bf16[128,2048]{1,0:T(8,128)(2,1)}, bf16[128,2048]{1,0:T(8,128)(2,1)}, bf16[128,2048]{1,0:T(8,128)(2,1)}) custom-call(s32[5]{0:T(128)} %pad_add_fusion.starts, bf16[512,1024]{1,0:T(8,128)(2,1)} %get-tuple-element.253.refs_3_.refs_0_, bf16[512,1024]{1,0:T(8,128)(2,1)} %get-tuple-element.243.refs_5_.refs_1_, ...), custom_call_target="tpu_custom_call" | custom-call | tf_op jit(solution)/shard_map/project/pallas_call | solution.py:193
  386.2 14.5 %project.11 = (bf16[128,2048]{1,0:T(8,128)(2,1)}, bf16[128,2048]{1,0:T(8,128)(2,1)}, bf16[128,2048]{1,0:T(8,128)(2,1)}, bf16[128,2048]{1,0:T(8,128)(2,1)}) custom-call(s32[5]{0:T(128)} %pad_add_fusion.starts, bf16[512,1024]{1,0:T(8,128)(2,1)} %get-tuple-element.255.refs_1_.refs_0_, bf16[512,1024]{1,0:T(8,128)(2,1)} %get-tuple-element.242.refs_4_.refs_1_, ...), custom_call_target="tpu_custom_call" | custom-call | tf_op jit(solution)/shard_map/project/pallas_call | solution.py:193
  405.9 8.8 %project.12 = (bf16[128,2048]{1,0:T(8,128)(2,1)}, bf16[128,2048]{1,0:T(8,128)(2,1)}, bf16[128,2048]{1,0:T(8,128)(2,1)}, bf16[128,2048]{1,0:T(8,128)(2,1)}) custom-call(s32[5]{0:T(128)} %pad_add_fusion.starts, bf16[512,1024]{1,0:T(8,128)(2,1)} %get-tuple-element.257.refs_9_.refs_0_, bf16[512,1024]{1,0:T(8,128)(2,1)} %get-tuple-element.252.refs_9_.refs_1_, ...), custom_call_target="tpu_custom_call" | custom-call | tf_op jit(solution)/shard_map/project/pallas_call | solution.py:193
  414.7 8.9 %project.13 = (bf16[128,2048]{1,0:T(8,128)(2,1)}, bf16[128,2048]{1,0:T(8,128)(2,1)}, bf16[128,2048]{1,0:T(8,128)(2,1)}, bf16[128,2048]{1,0:T(8,128)(2,1)}) custom-call(s32[5]{0:T(128)} %pad_add_fusion.starts, bf16[512,1024]{1,0:T(8,128)(2,1)} %get-tuple-element.259.refs_7_.refs_0_, bf16[512,1024]{1,0:T(8,128)(2,1)} %get-tuple-element.247.refs_7_.refs_1_, ...), custom_call_target="tpu_custom_call" | custom-call | tf_op jit(solution)/shard_map/project/pallas_call | solution.py:193
  425.1 6.2 collective-permute-start.49
  434.2 3.6 collective-permute-done.49
  437.7 3.5 collective-permute-start.70
  445.6 4.1 collective-permute-done.56
  453.3 6.8 %collective-permute-done.52 = bf16[128,2048]{1,0:T(8,128)(2,1)S(1)} collective-permute-done((bf16[128,2048]{1,0:T(8,128)(2,1)S(1)}, bf16[128,2048]{1,0:T(8,128)(2,1)S(1)}, u32[]{:S(2)}, u32[]{:S(2)}) %collective-permute-start.52) | collective-permute-done | bytes 524320 | tf_op jit(solution)/shard_map/ppermute | solution.py:75
  460.3 6.1 collective-permute-done.51
  474.3 3.5 collective-permute-start.67
  477.8 4.0 collective-permute-done.59.refs_0_
  484.4 3.5 collective-permute-start.62
  491.8 3.5 assemble.14.refs_0_.refs_6_
  495.3 19.8 %attend_back.2 = (bf16[512,768]{1,0:T(8,128)(2,1)}, bf16[512,768]{1,0:T(8,128)(2,1)}, f32[512,256]{1,0:T(8,128)}) custom-call(s32[1]{0:T(128)S(6)} %select_n.165.lengths, bf16[512,2048]{1,0:T(8,128)(2,1)} %assemble.14.refs_0_.refs_6_, bf16[2048,1280]{1,0:T(8,128)(2,1)} %all-gather.4.cloned.1.call-done.refs_1_, bf16[512,512]{1,0:T(8,128)(2,1)} %get-tuple-element.204.refs_2_, ...), custom_call_target="tpu_custom_call" | custom-call | tf_op jit(solution)/shard_map/attend_back/pallas_call | solution.py:473
  515.2 5.5 project.14
  520.7 4.9 collective-permute-start.44
  528.2 3.6 assemble.15.refs_0_.refs_4_
  533.1 3.2 collective-permute-start.84
  542.3 13.5 %attend_back.3 = (bf16[512,768]{1,0:T(8,128)(2,1)}, bf16[512,768]{1,0:T(8,128)(2,1)}) custom-call(s32[1]{0:T(128)S(6)} %select_n.165.lengths, bf16[512,2048]{1,0:T(8,128)(2,1)} %assemble.15.refs_0_.refs_4_, bf16[2048,1280]{1,0:T(8,128)(2,1)} %all-gather.4.cloned.1.call-done.refs_1_, bf16[512,512]{1,0:T(8,128)(2,1)} %get-tuple-element.179.refs_2_, ...), custom_call_target="tpu_custom_call" | custom-call | tf_op jit(solution)/shard_map/attend_back/pallas_call | solution.py:473
  555.8 5.6 project.15
  561.4 5.3 collective-permute-done.46
  568.2 12.1 %grads.5 = bf16[8,256,1280]{2,1,0:T(8,128)(2,1)} custom-call(bf16[512,2048]{1,0:T(8,128)(2,1)} %assemble.8.refs_0_, bf16[512,768]{1,0:T(8,128)(2,1)} %get-tuple-element.318.refs_1_, bf16[512,2048]{1,0:T(8,128)(2,1)} %assemble.9.refs_0_.refs_2_, bf16[512,768]{1,0:T(8,128)(2,1)} %get-tuple-element.319.refs_3_, bf16[512,2048]{1,0:T(8,128)(2,1)} %assemble.15.refs_0_.refs_4_, ...), custom_call_target="tpu_custom_call" | custom-call | tf_op jit(solution)/shard_map/grads/pallas_call | solution.py:285
  603.5 3.4 collective-permute-done.75
  626.1 10.3 %collective-permute-done.85 = bf16[256,3072]{1,0:T(8,128)(2,1)S(1)} collective-permute-done((bf16[256,3072]{1,0:T(8,128)(2,1)}, bf16[256,3072]{1,0:T(8,128)(2,1)S(1)}, u32[]{:S(2)}, u32[]{:S(2)}) %collective-permute-start.85) | collective-permute-done | bytes 1572896 | tf_op jit(solution)/shard_map/ppermute | solution.py:75
  659.9 5.5 collective-permute-done.91
  (405 shorter events, 189.1 us)
Async XLA Ops:
  7.2 86.1 %all-gather.4.cloned.1.call-start = ((), (), s32[]{:S(2)}) async-start(), calls=%async_computation.3 | async-start | bytes 5898240 | tf_op jit(solution)/shard_map/all_gather | solution.py:566
  30.5 258.4 %all-gather.6.cloned.1.call-start = ((), (), s32[]{:S(2)}) async-start(), calls=%async_computation.4 | async-start | bytes 14155776 | tf_op jit(solution)/shard_map/all_gather | solution.py:566
  34.4 48.9 %collective-permute-start.7 = (bf16[256,3072]{1,0:T(8,128)(2,1)S(1)}, bf16[256,3072]{1,0:T(8,128)(2,1)}, u32[]{:S(2)}, u32[]{:S(2)}) collective-permute-start(bf16[256,3072]{1,0:T(8,128)(2,1)S(1)} %pad_maximum_fusion), channel_id=1, source_target_pairs={{1,4},{3,6},{4,1},{6,3},{9,12},{11,14},{12,9},{14,11},{17,20},{19,... | collective-permute-start | bytes 4718600 | tf_op jit(solution)/shard_map/ppermute | solution.py:75
  37.5 30.4 %collective-permute-start.2 = (bf16[128,2048]{1,0:T(8,128)(2,1)}, bf16[128,2048]{1,0:T(8,128)(2,1)}, u32[]{:S(2)}, u32[]{:S(2)}) collective-permute-start(bf16[128,2048]{1,0:T(8,128)(2,1)} %get-tuple-element.174.refs_4_), channel_id=1, source_target_pairs={{1,4},{3,6},{4,1},{6,3},{0,2},{2,0},{5,7},{7,5},{9,12},{11,14},{12... | collective-permute-start | bytes 1572872 | tf_op jit(solution)/shard_map/ppermute | solution.py:75
  39.3 33.8 %collective-permute-start.4 = (bf16[128,2048]{1,0:T(8,128)(2,1)}, bf16[128,2048]{1,0:T(8,128)(2,1)}, u32[]{:S(2)}, u32[]{:S(2)}) collective-permute-start(bf16[128,2048]{1,0:T(8,128)(2,1)} %get-tuple-element.174.refs_4_), channel_id=1, source_target_pairs={{1,0},{3,2},{4,5},{6,7},{9,8},{11,10},{12,13},{14,15},{17,16},{19,... | collective-permute-start | bytes 1572872 | tf_op jit(solution)/shard_map/ppermute | solution.py:75
  41.3 31.7 %collective-permute-start.3 = (bf16[128,2048]{1,0:T(8,128)(2,1)}, bf16[128,2048]{1,0:T(8,128)(2,1)}, u32[]{:S(2)}, u32[]{:S(2)}) collective-permute-start(bf16[128,2048]{1,0:T(8,128)(2,1)} %get-tuple-element.174.refs_4_), channel_id=1, source_target_pairs={{0,4},{2,6},{5,1},{7,3},{1,2},{3,0},{4,7},{6,5},{8,12},{10,14},{13... | collective-permute-start | bytes 1572872 | tf_op jit(solution)/shard_map/ppermute | solution.py:75
  86.1 242.2 %all-gather.8.cloned.1.call-start = ((), (), s32[]{:S(2)}) async-start(), calls=%async_computation.5 | async-start | bytes 14155776 | tf_op jit(solution)/shard_map/all_gather | solution.py:566
  90.6 21.0 %collective-permute-start.15 = (bf16[128,2048]{1,0:T(8,128)(2,1)}, bf16[128,2048]{1,0:T(8,128)(2,1)}, u32[]{:S(2)}, u32[]{:S(2)}) collective-permute-start(bf16[128,2048]{1,0:T(8,128)(2,1)} %get-tuple-element.190.refs_4_), channel_id=1, source_target_pairs={{1,0},{3,2},{4,5},{6,7},{9,8},{11,10},{12,13},{14,15},{17,16},{19,... | collective-permute-start | bytes 1572872 | tf_op jit(solution)/shard_map/ppermute | solution.py:75
  92.7 16.9 %collective-permute-start.13 = (bf16[128,2048]{1,0:T(8,128)(2,1)}, bf16[128,2048]{1,0:T(8,128)(2,1)}, u32[]{:S(2)}, u32[]{:S(2)}) collective-permute-start(bf16[128,2048]{1,0:T(8,128)(2,1)} %get-tuple-element.190.refs_4_), channel_id=1, source_target_pairs={{1,4},{3,6},{4,1},{6,3},{0,2},{2,0},{5,7},{7,5},{9,12},{11,14},{12... | collective-permute-start | bytes 1572872 | tf_op jit(solution)/shard_map/ppermute | solution.py:75
  106.1 65.5 %collective-permute-start.18 = (bf16[256,3072]{1,0:T(8,128)(2,1)S(1)}, bf16[256,3072]{1,0:T(8,128)(2,1)S(1)}, u32[]{:S(2)}, u32[]{:S(2)}) collective-permute-start(bf16[256,3072]{1,0:T(8,128)(2,1)S(1)} %pad_maximum_fusion.1), channel_id=1, source_target_pairs={{1,4},{3,6},{4,1},{6,3},{9,12},{11,14},{12,9},{14,11},{17,20},{19,... | collective-permute-start | bytes 4718600 | tf_op jit(solution)/shard_map/ppermute | solution.py:75
  109.5 14.3 %collective-permute-start.14 = (bf16[128,2048]{1,0:T(8,128)(2,1)}, bf16[128,2048]{1,0:T(8,128)(2,1)S(1)}, u32[]{:S(2)}, u32[]{:S(2)}) collective-permute-start(bf16[128,2048]{1,0:T(8,128)(2,1)} %get-tuple-element.190.refs_4_), channel_id=1, source_target_pairs={{0,4},{2,6},{5,1},{7,3},{1,2},{3,0},{4,7},{6,5},{8,12},{10,14},{13... | collective-permute-start | bytes 1572872 | tf_op jit(solution)/shard_map/ppermute | solution.py:75
  109.6 25.5 %collective-permute-start.17 = (bf16[128,2048]{1,0:T(8,128)(2,1)}, bf16[128,2048]{1,0:T(8,128)(2,1)S(1)}, u32[]{:S(2)}, u32[]{:S(2)}) collective-permute-start(bf16[128,2048]{1,0:T(8,128)(2,1)} %collective-permute-done.13.refs_0_), channel_id=1, source_target_pairs={{0,4},{2,6},{5,1},{7,3},{8,12},{10,14},{13,9},{15,11},{16,20},{18,... | collective-permute-start | bytes 1572872 | tf_op jit(solution)/shard_map/ppermute | solution.py:75
  110.9 39.8 %collective-permute-start.19 = (bf16[128,2048]{1,0:T(8,128)(2,1)S(1)}, bf16[128,2048]{1,0:T(8,128)(2,1)S(1)}, u32[]{:S(2)}, u32[]{:S(2)}) collective-permute-start(bf16[128,2048]{1,0:T(8,128)(2,1)S(1)} %get-tuple-element.198.refs_4_), channel_id=1, source_target_pairs={{1,4},{3,6},{4,1},{6,3},{0,2},{2,0},{5,7},{7,5},{9,12},{11,14},{12... | collective-permute-start | bytes 1572872 | tf_op jit(solution)/shard_map/ppermute | solution.py:75
  111.5 40.4 %collective-permute-start.16 = (bf16[128,2048]{1,0:T(8,128)(2,1)}, bf16[128,2048]{1,0:T(8,128)(2,1)}, u32[]{:S(2)}, u32[]{:S(2)}) collective-permute-start(bf16[128,2048]{1,0:T(8,128)(2,1)} %collective-permute-done.13.refs_0_), channel_id=1, source_target_pairs={{1,3},{3,1},{4,6},{6,4},{9,11},{11,9},{12,14},{14,12},{17,19},{19,... | collective-permute-start | bytes 1572872 | tf_op jit(solution)/shard_map/ppermute | solution.py:75
  123.8 43.2 %collective-permute-start.21 = (bf16[128,2048]{1,0:T(8,128)(2,1)S(1)}, bf16[128,2048]{1,0:T(8,128)(2,1)S(1)}, u32[]{:S(2)}, u32[]{:S(2)}) collective-permute-start(bf16[128,2048]{1,0:T(8,128)(2,1)S(1)} %get-tuple-element.198.refs_4_), channel_id=1, source_target_pairs={{1,0},{3,2},{4,5},{6,7},{9,8},{11,10},{12,13},{14,15},{17,16},{19,... | collective-permute-start | bytes 1572872 | tf_op jit(solution)/shard_map/ppermute | solution.py:75
  135.1 32.0 %collective-permute-start.20 = (bf16[128,2048]{1,0:T(8,128)(2,1)S(1)}, bf16[128,2048]{1,0:T(8,128)(2,1)S(1)}, u32[]{:S(2)}, u32[]{:S(2)}) collective-permute-start(bf16[128,2048]{1,0:T(8,128)(2,1)S(1)} %get-tuple-element.198.refs_4_), channel_id=1, source_target_pairs={{0,4},{2,6},{5,1},{7,3},{1,2},{3,0},{4,7},{6,5},{8,12},{10,14},{13... | collective-permute-start | bytes 1572872 | tf_op jit(solution)/shard_map/ppermute | solution.py:75
  150.7 16.4 %collective-permute-start.23 = (bf16[128,2048]{1,0:T(8,128)(2,1)S(1)}, bf16[128,2048]{1,0:T(8,128)(2,1)}, u32[]{:S(2)}, u32[]{:S(2)}) collective-permute-start(bf16[128,2048]{1,0:T(8,128)(2,1)S(1)} %collective-permute-done.19.refs_0_), channel_id=1, source_target_pairs={{0,4},{2,6},{5,1},{7,3},{8,12},{10,14},{13,9},{15,11},{16,20},{18,... | collective-permute-start | bytes 1572872 | tf_op jit(solution)/shard_map/ppermute | solution.py:75
  152.0 15.1 %collective-permute-start.22 = (bf16[128,2048]{1,0:T(8,128)(2,1)S(1)}, bf16[128,2048]{1,0:T(8,128)(2,1)}, u32[]{:S(2)}, u32[]{:S(2)}) collective-permute-start(bf16[128,2048]{1,0:T(8,128)(2,1)S(1)} %collective-permute-done.19.refs_0_), channel_id=1, source_target_pairs={{1,3},{3,1},{4,6},{6,4},{9,11},{11,9},{12,14},{14,12},{17,19},{19,... | collective-permute-start | bytes 1572872 | tf_op jit(solution)/shard_map/ppermute | solution.py:75
  173.0 360.2 %reduce-scatter.4.cloned.1.call-start = ((), (), s32[]{:S(2)}) async-start(), calls=%async_computation.6 | async-start | bytes 14155776 | tf_op jit(solution)/shard_map/reduce_scatter | solution.py:575
  179.3 15.0 %collective-permute-start.12 = (bf16[128,2048]{1,0:T(8,128)(2,1)}, bf16[128,2048]{1,0:T(8,128)(2,1)S(1)}, u32[]{:S(2)}, u32[]{:S(2)}) collective-permute-start(bf16[128,2048]{1,0:T(8,128)(2,1)} %get-tuple-element.183), channel_id=1, source_target_pairs={{0,1},{2,3},{5,4},{7,6},{8,9},{10,11},{13,12},{15,14},{16,17},{18,... | collective-permute-start | bytes 1572872 | tf_op jit(solution)/shard_map/ppermute | solution.py:75
  182.3 35.1 %collective-permute-start.11 = (bf16[128,2048]{1,0:T(8,128)(2,1)}, bf16[128,2048]{1,0:T(8,128)(2,1)S(1)}, u32[]{:S(2)}, u32[]{:S(2)}) collective-permute-start(bf16[128,2048]{1,0:T(8,128)(2,1)} %get-tuple-element.184), channel_id=1, source_target_pairs={{4,0},{6,2},{1,5},{3,7},{2,1},{0,3},{7,4},{5,6},{12,8},{14,10},{9,... | collective-permute-start | bytes 1572872 | tf_op jit(solution)/shard_map/ppermute | solution.py:75
  189.6 31.8 %collective-permute-start.10 = (bf16[128,2048]{1,0:T(8,128)(2,1)S(1)}, bf16[128,2048]{1,0:T(8,128)(2,1)S(1)}, u32[]{:S(2)}, u32[]{:S(2)}) collective-permute-start(bf16[128,2048]{1,0:T(8,128)(2,1)S(1)} %add_convert_fusion.7), channel_id=1, source_target_pairs={{4,1},{6,3},{1,4},{3,6},{2,0},{0,2},{7,5},{5,7},{12,9},{14,11},{9,... | collective-permute-start | bytes 1572872 | tf_op jit(solution)/shard_map/ppermute | solution.py:75
  192.9 29.8 %collective-permute-start.31 = (bf16[128,2048]{1,0:T(8,128)(2,1)S(1)}, bf16[128,2048]{1,0:T(8,128)(2,1)S(1)}, u32[]{:S(2)}, u32[]{:S(2)}) collective-permute-start(bf16[128,2048]{1,0:T(8,128)(2,1)S(1)} %get-tuple-element.215.refs_4_), channel_id=1, source_target_pairs={{1,0},{3,2},{4,5},{6,7},{9,8},{11,10},{12,13},{14,15},{17,16},{19,... | collective-permute-start | bytes 1572872 | tf_op jit(solution)/shard_map/ppermute | solution.py:75
  194.3 31.7 %collective-permute-start.30 = (bf16[128,2048]{1,0:T(8,128)(2,1)S(1)}, bf16[128,2048]{1,0:T(8,128)(2,1)S(1)}, u32[]{:S(2)}, u32[]{:S(2)}) collective-permute-start(bf16[128,2048]{1,0:T(8,128)(2,1)S(1)} %get-tuple-element.215.refs_4_), channel_id=1, source_target_pairs={{0,4},{2,6},{5,1},{7,3},{1,2},{3,0},{4,7},{6,5},{8,12},{10,14},{13... | collective-permute-start | bytes 1572872 | tf_op jit(solution)/shard_map/ppermute | solution.py:75
  194.3 34.5 %collective-permute-start.33 = (bf16[128,2048]{1,0:T(8,128)(2,1)S(1)}, bf16[128,2048]{1,0:T(8,128)(2,1)S(1)}, u32[]{:S(2)}, u32[]{:S(2)}) collective-permute-start(bf16[128,2048]{1,0:T(8,128)(2,1)S(1)} %collective-permute-done.29.refs_0_), channel_id=1, source_target_pairs={{0,4},{2,6},{5,1},{7,3},{8,12},{10,14},{13,9},{15,11},{16,20},{18,... | collective-permute-start | bytes 1572872 | tf_op jit(solution)/shard_map/ppermute | solution.py:75
  222.7 15.1 %collective-permute-start.34 = (bf16[128,2048]{1,0:T(8,128)(2,1)S(1)}, bf16[128,2048]{1,0:T(8,128)(2,1)S(1)}, u32[]{:S(2)}, u32[]{:S(2)}) collective-permute-start(bf16[128,2048]{1,0:T(8,128)(2,1)S(1)} %copy-done.33), channel_id=1, source_target_pairs={{4,0},{6,2},{1,5},{3,7},{12,8},{14,10},{9,13},{11,15},{20,16},{22,... | collective-permute-start | bytes 1572872 | tf_op jit(solution)/shard_map/ppermute | solution.py:75
  228.9 14.3 %collective-permute-start.26 = (bf16[128,2048]{1,0:T(8,128)(2,1)S(1)}, bf16[128,2048]{1,0:T(8,128)(2,1)S(1)}, u32[]{:S(2)}, u32[]{:S(2)}) collective-permute-start(bf16[128,2048]{1,0:T(8,128)(2,1)S(1)} %multiply_convert_fusion.7.refs_4_), channel_id=1, source_target_pairs={{1,0},{3,2},{4,5},{6,7},{9,8},{11,10},{12,13},{14,15},{17,16},{19,... | collective-permute-start | bytes 1572872 | tf_op jit(solution)/shard_map/ppermute | solution.py:75
  232.4 16.2 %collective-permute-start.25 = (bf16[128,2048]{1,0:T(8,128)(2,1)S(1)}, bf16[128,2048]{1,0:T(8,128)(2,1)S(1)}, u32[]{:S(2)}, u32[]{:S(2)}) collective-permute-start(bf16[128,2048]{1,0:T(8,128)(2,1)S(1)} %multiply_convert_fusion.7.refs_4_), channel_id=1, source_target_pairs={{0,4},{2,6},{5,1},{7,3},{1,2},{3,0},{4,7},{6,5},{8,12},{10,14},{13... | collective-permute-start | bytes 1572872 | tf_op jit(solution)/shard_map/ppermute | solution.py:75
  239.6 15.8 %collective-permute-start.27 = (bf16[128,2048]{1,0:T(8,128)(2,1)}, bf16[128,2048]{1,0:T(8,128)(2,1)}, u32[]{:S(2)}, u32[]{:S(2)}) collective-permute-start(bf16[128,2048]{1,0:T(8,128)(2,1)} %collective-permute-done.24.refs_0_), channel_id=1, source_target_pairs={{1,3},{3,1},{4,6},{6,4},{9,11},{11,9},{12,14},{14,12},{17,19},{19,... | collective-permute-start | bytes 1572872 | tf_op jit(solution)/shard_map/ppermute | solution.py:75
  243.2 15.7 %collective-permute-start.37 = (bf16[128,2048]{1,0:T(8,128)(2,1)}, bf16[128,2048]{1,0:T(8,128)(2,1)S(1)}, u32[]{:S(2)}, u32[]{:S(2)}) collective-permute-start(bf16[128,2048]{1,0:T(8,128)(2,1)} %get-tuple-element.225), channel_id=1, source_target_pairs={{4,0},{6,2},{1,5},{3,7},{2,1},{0,3},{7,4},{5,6},{12,8},{14,10},{9,... | collective-permute-start | bytes 1572872 | tf_op jit(solution)/shard_map/ppermute | solution.py:75
  243.8 16.6 %collective-permute-start.36 = (bf16[128,2048]{1,0:T(8,128)(2,1)S(1)}, bf16[128,2048]{1,0:T(8,128)(2,1)S(1)}, u32[]{:S(2)}, u32[]{:S(2)}) collective-permute-start(bf16[128,2048]{1,0:T(8,128)(2,1)S(1)} %add_convert_fusion.6), channel_id=1, source_target_pairs={{4,1},{6,3},{1,4},{3,6},{2,0},{0,2},{7,5},{5,7},{12,9},{14,11},{9,... | collective-permute-start | bytes 1572872 | tf_op jit(solution)/shard_map/ppermute | solution.py:75
  263.1 14.2 %collective-permute-start.41 = (bf16[128,2048]{1,0:T(8,128)(2,1)S(1)}, bf16[128,2048]{1,0:T(8,128)(2,1)S(1)}, u32[]{:S(2)}, u32[]{:S(2)}) collective-permute-start(bf16[128,2048]{1,0:T(8,128)(2,1)S(1)} %multiply_convert_fusion.6.refs_4_), channel_id=1, source_target_pairs={{1,0},{3,2},{4,5},{6,7},{9,8},{11,10},{12,13},{14,15},{17,16},{19,... | collective-permute-start | bytes 1572872 | tf_op jit(solution)/shard_map/ppermute | solution.py:75
  328.2 282.5 %reduce-scatter.6.cloned.1.call-start = ((), (), s32[]{:S(2)}) async-start(), calls=%async_computation.7 | async-start | bytes 14155776 | tf_op jit(solution)/shard_map/reduce_scatter | solution.py:575
  367.5 285.8 %reduce-scatter.8.cloned.1.call-start = ((), (), s32[]{:S(2)}) async-start(), calls=%async_computation.8 | async-start | bytes 5898240 | tf_op jit(solution)/shard_map/reduce_scatter | solution.py:575
  382.0 41.7 %collective-permute-start.54 = (bf16[128,2048]{1,0:T(8,128)(2,1)}, bf16[128,2048]{1,0:T(8,128)(2,1)S(1)}, u32[]{:S(2)}, u32[]{:S(2)}) collective-permute-start(bf16[128,2048]{1,0:T(8,128)(2,1)} %get-tuple-element.267), channel_id=1, source_target_pairs={{4,0},{6,2},{1,5},{3,7},{12,8},{14,10},{9,13},{11,15},{20,16},{22,... | collective-permute-start | bytes 1572872 | tf_op jit(solution)/shard_map/ppermute | solution.py:75
  383.3 41.8 %collective-permute-start.55 = (bf16[128,2048]{1,0:T(8,128)(2,1)}, bf16[128,2048]{1,0:T(8,128)(2,1)S(1)}, u32[]{:S(2)}, u32[]{:S(2)}) collective-permute-start(bf16[128,2048]{1,0:T(8,128)(2,1)} %get-tuple-element.268), channel_id=1, source_target_pairs={{3,1},{1,3},{6,4},{4,6},{11,9},{9,11},{14,12},{12,14},{19,17},{17,... | collective-permute-start | bytes 1572872 | tf_op jit(solution)/shard_map/ppermute | solution.py:75
  400.7 30.9 %collective-permute-start.53 = (bf16[128,2048]{1,0:T(8,128)(2,1)}, bf16[128,2048]{1,0:T(8,128)(2,1)}, u32[]{:S(2)}, u32[]{:S(2)}) collective-permute-start(bf16[128,2048]{1,0:T(8,128)(2,1)} %get-tuple-element.265), channel_id=1, source_target_pairs={{0,1},{2,3},{5,4},{7,6},{8,9},{10,11},{13,12},{15,14},{16,17},{18,... | collective-permute-start | bytes 1572872 | tf_op jit(solution)/shard_map/ppermute | solution.py:75
  402.0 39.3 %collective-permute-start.50 = (bf16[128,2048]{1,0:T(8,128)(2,1)}, bf16[128,2048]{1,0:T(8,128)(2,1)S(1)}, u32[]{:S(2)}, u32[]{:S(2)}) collective-permute-start(bf16[128,2048]{1,0:T(8,128)(2,1)} %get-tuple-element.265), channel_id=1, source_target_pairs={{3,1},{1,3},{6,4},{4,6},{11,9},{9,11},{14,12},{12,14},{19,17},{17,... | collective-permute-start | bytes 1572872 | tf_op jit(solution)/shard_map/ppermute | solution.py:75
  404.6 28.3 %collective-permute-start.58 = (bf16[128,2048]{1,0:T(8,128)(2,1)}, bf16[128,2048]{1,0:T(8,128)(2,1)}, u32[]{:S(2)}, u32[]{:S(2)}) collective-permute-start(bf16[128,2048]{1,0:T(8,128)(2,1)} %get-tuple-element.268), channel_id=1, source_target_pairs={{0,1},{2,3},{5,4},{7,6},{8,9},{10,11},{13,12},{15,14},{16,17},{18,... | collective-permute-start | bytes 1572872 | tf_op jit(solution)/shard_map/ppermute | solution.py:75
  423.7 47.9 %collective-permute-start.73 = (bf16[128,2048]{1,0:T(8,128)(2,1)}, bf16[128,2048]{1,0:T(8,128)(2,1)S(1)}, u32[]{:S(2)}, u32[]{:S(2)}) collective-permute-start(bf16[128,2048]{1,0:T(8,128)(2,1)} %get-tuple-element.295), channel_id=1, source_target_pairs={{0,1},{2,3},{5,4},{7,6},{8,9},{10,11},{13,12},{15,14},{16,17},{18,... | collective-permute-start | bytes 1572872 | tf_op jit(solution)/shard_map/ppermute | solution.py:75
  432.9 16.7 %collective-permute-start.56 = (bf16[128,2048]{1,0:T(8,128)(2,1)S(1)}, bf16[128,2048]{1,0:T(8,128)(2,1)S(1)}, u32[]{:S(2)}, u32[]{:S(2)}) collective-permute-start(bf16[128,2048]{1,0:T(8,128)(2,1)S(1)} %add_convert_fusion.3), channel_id=1, source_target_pairs={{4,1},{6,3},{1,4},{3,6},{2,0},{0,2},{7,5},{5,7},{12,9},{14,11},{9,... | collective-permute-start | bytes 1572872 | tf_op jit(solution)/shard_map/ppermute | solution.py:75
  437.7 35.1 %collective-permute-start.70 = (bf16[128,2048]{1,0:T(8,128)(2,1)}, bf16[128,2048]{1,0:T(8,128)(2,1)S(1)}, u32[]{:S(2)}, u32[]{:S(2)}) collective-permute-start(bf16[128,2048]{1,0:T(8,128)(2,1)} %get-tuple-element.295), channel_id=1, source_target_pairs={{3,1},{1,3},{6,4},{4,6},{11,9},{9,11},{14,12},{12,14},{19,17},{17,... | collective-permute-start | bytes 1572872 | tf_op jit(solution)/shard_map/ppermute | solution.py:75
  441.3 28.3 %collective-permute-start.69 = (bf16[128,2048]{1,0:T(8,128)(2,1)S(1)}, bf16[128,2048]{1,0:T(8,128)(2,1)S(1)}, u32[]{:S(2)}, u32[]{:S(2)}) collective-permute-start(bf16[128,2048]{1,0:T(8,128)(2,1)S(1)} %copy-done.32), channel_id=1, source_target_pairs={{4,0},{6,2},{1,5},{3,7},{12,8},{14,10},{9,13},{11,15},{20,16},{22,... | collective-permute-start | bytes 1572872 | tf_op jit(solution)/shard_map/ppermute | solution.py:75
  443.3 16.9 %collective-permute-start.52 = (bf16[128,2048]{1,0:T(8,128)(2,1)S(1)}, bf16[128,2048]{1,0:T(8,128)(2,1)S(1)}, u32[]{:S(2)}, u32[]{:S(2)}) collective-permute-start(bf16[128,2048]{1,0:T(8,128)(2,1)S(1)} %copy-done.64), channel_id=1, source_target_pairs={{4,0},{6,2},{1,5},{3,7},{2,1},{0,3},{7,4},{5,6},{12,8},{14,10},{9,... | collective-permute-start | bytes 1572872 | tf_op jit(solution)/shard_map/ppermute | solution.py:75
  449.6 16.7 %collective-permute-start.51 = (bf16[128,2048]{1,0:T(8,128)(2,1)S(1)}, bf16[128,2048]{1,0:T(8,128)(2,1)S(1)}, u32[]{:S(2)}, u32[]{:S(2)}) collective-permute-start(bf16[128,2048]{1,0:T(8,128)(2,1)S(1)} %add_convert_fusion.4), channel_id=1, source_target_pairs={{4,1},{6,3},{1,4},{3,6},{2,0},{0,2},{7,5},{5,7},{12,9},{14,11},{9,... | collective-permute-start | bytes 1572872 | tf_op jit(solution)/shard_map/ppermute | solution.py:75
  473.0 17.1 %collective-permute-start.68 = (bf16[128,2048]{1,0:T(8,128)(2,1)S(1)}, bf16[128,2048]{1,0:T(8,128)(2,1)S(1)}, u32[]{:S(2)}, u32[]{:S(2)}) collective-permute-start(bf16[128,2048]{1,0:T(8,128)(2,1)S(1)} %collective-permute-done.64.refs_0_), channel_id=1, source_target_pairs={{0,4},{2,6},{5,1},{7,3},{8,12},{10,14},{13,9},{15,11},{16,20},{18,... | collective-permute-start | bytes 1572872 | tf_op jit(solution)/shard_map/ppermute | solution.py:75
  474.3 15.9 %collective-permute-start.67 = (bf16[128,2048]{1,0:T(8,128)(2,1)S(1)}, bf16[128,2048]{1,0:T(8,128)(2,1)S(1)}, u32[]{:S(2)}, u32[]{:S(2)}) collective-permute-start(bf16[128,2048]{1,0:T(8,128)(2,1)S(1)} %collective-permute-done.64.refs_0_), channel_id=1, source_target_pairs={{1,3},{3,1},{4,6},{6,4},{9,11},{11,9},{12,14},{14,12},{17,19},{19,... | collective-permute-start | bytes 1572872 | tf_op jit(solution)/shard_map/ppermute | solution.py:75
  481.8 38.9 %collective-permute-start.60 = (bf16[128,2048]{1,0:T(8,128)(2,1)S(1)}, bf16[128,2048]{1,0:T(8,128)(2,1)}, u32[]{:S(2)}, u32[]{:S(2)}) collective-permute-start(bf16[128,2048]{1,0:T(8,128)(2,1)S(1)} %get-tuple-element.292.refs_4_), channel_id=1, source_target_pairs={{0,4},{2,6},{5,1},{7,3},{1,2},{3,0},{4,7},{6,5},{8,12},{10,14},{13... | collective-permute-start | bytes 1572872 | tf_op jit(solution)/shard_map/ppermute | solution.py:75
  481.8 43.8 %collective-permute-start.63 = (bf16[128,2048]{1,0:T(8,128)(2,1)S(1)}, bf16[128,2048]{1,0:T(8,128)(2,1)}, u32[]{:S(2)}, u32[]{:S(2)}) collective-permute-start(bf16[128,2048]{1,0:T(8,128)(2,1)S(1)} %collective-permute-done.59.refs_0_), channel_id=1, source_target_pairs={{0,4},{2,6},{5,1},{7,3},{8,12},{10,14},{13,9},{15,11},{16,20},{18,... | collective-permute-start | bytes 1572872 | tf_op jit(solution)/shard_map/ppermute | solution.py:75
  484.4 43.8 %collective-permute-start.62 = (bf16[128,2048]{1,0:T(8,128)(2,1)S(1)}, bf16[128,2048]{1,0:T(8,128)(2,1)}, u32[]{:S(2)}, u32[]{:S(2)}) collective-permute-start(bf16[128,2048]{1,0:T(8,128)(2,1)S(1)} %collective-permute-done.59.refs_0_), channel_id=1, source_target_pairs={{1,3},{3,1},{4,6},{6,4},{9,11},{11,9},{12,14},{14,12},{17,19},{19,... | collective-permute-start | bytes 1572872 | tf_op jit(solution)/shard_map/ppermute | solution.py:75
  490.0 41.8 %collective-permute-start.72 = (bf16[128,2048]{1,0:T(8,128)(2,1)}, bf16[128,2048]{1,0:T(8,128)(2,1)S(1)}, u32[]{:S(2)}, u32[]{:S(2)}) collective-permute-start(bf16[128,2048]{1,0:T(8,128)(2,1)} %get-tuple-element.296), channel_id=1, source_target_pairs={{4,0},{6,2},{1,5},{3,7},{2,1},{0,3},{7,4},{5,6},{12,8},{14,10},{9,... | collective-permute-start | bytes 1572872 | tf_op jit(solution)/shard_map/ppermute | solution.py:75
  490.3 41.6 %collective-permute-start.71 = (bf16[128,2048]{1,0:T(8,128)(2,1)S(1)}, bf16[128,2048]{1,0:T(8,128)(2,1)S(1)}, u32[]{:S(2)}, u32[]{:S(2)}) collective-permute-start(bf16[128,2048]{1,0:T(8,128)(2,1)S(1)} %add_convert_fusion.2), channel_id=1, source_target_pairs={{4,1},{6,3},{1,4},{3,6},{2,0},{0,2},{7,5},{5,7},{12,9},{14,11},{9,... | collective-permute-start | bytes 1572872 | tf_op jit(solution)/shard_map/ppermute | solution.py:75
  520.7 18.5 %collective-permute-start.44 = (bf16[128,2048]{1,0:T(8,128)(2,1)}, bf16[128,2048]{1,0:T(8,128)(2,1)}, u32[]{:S(2)}, u32[]{:S(2)}) collective-permute-start(bf16[128,2048]{1,0:T(8,128)(2,1)} %get-tuple-element.261), channel_id=1, source_target_pairs={{4,0},{6,2},{1,5},{3,7},{12,8},{14,10},{9,13},{11,15},{20,16},{22,... | collective-permute-start | bytes 1572872 | tf_op jit(solution)/shard_map/ppermute | solution.py:75
  533.1 34.9 %collective-permute-start.84 = (bf16[256,3072]{1,0:T(8,128)(2,1)}, bf16[256,3072]{1,0:T(8,128)(2,1)S(1)}, u32[]{:S(2)}, u32[]{:S(2)}) collective-permute-start(bf16[256,3072]{1,0:T(8,128)(2,1)} %bitcast.75), channel_id=1, source_target_pairs={{1,4},{3,6},{4,1},{6,3},{9,12},{11,14},{12,9},{14,11},{17,20},{19,... | collective-permute-start | bytes 4718600 | tf_op jit(solution)/shard_map/ppermute | solution.py:75
  537.6 23.8 %collective-permute-start.47 = (bf16[128,2048]{1,0:T(8,128)(2,1)}, bf16[128,2048]{1,0:T(8,128)(2,1)S(1)}, u32[]{:S(2)}, u32[]{:S(2)}) collective-permute-start(bf16[128,2048]{1,0:T(8,128)(2,1)} %get-tuple-element.263), channel_id=1, source_target_pairs={{4,0},{6,2},{1,5},{3,7},{2,1},{0,3},{7,4},{5,6},{12,8},{14,10},{9,... | collective-permute-start | bytes 1572872 | tf_op jit(solution)/shard_map/ppermute | solution.py:75
  540.6 26.1 %collective-permute-start.46 = (bf16[128,2048]{1,0:T(8,128)(2,1)S(1)}, bf16[128,2048]{1,0:T(8,128)(2,1)S(1)}, u32[]{:S(2)}, u32[]{:S(2)}) collective-permute-start(bf16[128,2048]{1,0:T(8,128)(2,1)S(1)} %add_convert_fusion.5), channel_id=1, source_target_pairs={{4,1},{6,3},{1,4},{3,6},{2,0},{0,2},{7,5},{5,7},{12,9},{14,11},{9,... | collective-permute-start | bytes 1572872 | tf_op jit(solution)/shard_map/ppermute | solution.py:75
  585.3 15.2 %collective-permute-start.83 = (bf16[128,2048]{1,0:T(8,128)(2,1)}, bf16[128,2048]{1,0:T(8,128)(2,1)S(1)}, u32[]{:S(2)}, u32[]{:S(2)}) collective-permute-start(bf16[128,2048]{1,0:T(8,128)(2,1)} %get-tuple-element.314), channel_id=1, source_target_pairs={{0,1},{2,3},{5,4},{7,6},{8,9},{10,11},{13,12},{15,14},{16,17},{18,... | collective-permute-start | bytes 1572872 | tf_op jit(solution)/shard_map/ppermute | solution.py:75
  586.8 26.0 %collective-permute-start.82 = (bf16[128,2048]{1,0:T(8,128)(2,1)}, bf16[128,2048]{1,0:T(8,128)(2,1)}, u32[]{:S(2)}, u32[]{:S(2)}) collective-permute-start(bf16[128,2048]{1,0:T(8,128)(2,1)} %get-tuple-element.315), channel_id=1, source_target_pairs={{4,0},{6,2},{1,5},{3,7},{2,1},{0,3},{7,4},{5,6},{12,8},{14,10},{9,... | collective-permute-start | bytes 1572872 | tf_op jit(solution)/shard_map/ppermute | solution.py:75
  588.5 14.1 %collective-permute-start.74 = (bf16[128,2048]{1,0:T(8,128)(2,1)}, bf16[128,2048]{1,0:T(8,128)(2,1)S(1)}, u32[]{:S(2)}, u32[]{:S(2)}) collective-permute-start(bf16[128,2048]{1,0:T(8,128)(2,1)} %get-tuple-element.310), channel_id=1, source_target_pairs={{4,0},{6,2},{1,5},{3,7},{12,8},{14,10},{9,13},{11,15},{20,16},{22,... | collective-permute-start | bytes 1572872 | tf_op jit(solution)/shard_map/ppermute | solution.py:75
  590.7 16.2 %collective-permute-start.75 = (bf16[128,2048]{1,0:T(8,128)(2,1)}, bf16[128,2048]{1,0:T(8,128)(2,1)S(1)}, u32[]{:S(2)}, u32[]{:S(2)}) collective-permute-start(bf16[128,2048]{1,0:T(8,128)(2,1)} %get-tuple-element.311), channel_id=1, source_target_pairs={{3,1},{1,3},{6,4},{4,6},{11,9},{9,11},{14,12},{12,14},{19,17},{17,... | collective-permute-start | bytes 1572872 | tf_op jit(solution)/shard_map/ppermute | solution.py:75
  597.8 14.9 %collective-permute-start.81 = (bf16[128,2048]{1,0:T(8,128)(2,1)}, bf16[128,2048]{1,0:T(8,128)(2,1)}, u32[]{:S(2)}, u32[]{:S(2)}) collective-permute-start(bf16[128,2048]{1,0:T(8,128)(2,1)} %add_convert_fusion), channel_id=1, source_target_pairs={{4,1},{6,3},{1,4},{3,6},{2,0},{0,2},{7,5},{5,7},{12,9},{14,11},{9,... | collective-permute-start | bytes 1572872 | tf_op jit(solution)/shard_map/ppermute | solution.py:75
  602.6 14.7 %collective-permute-start.77 = (bf16[128,2048]{1,0:T(8,128)(2,1)}, bf16[128,2048]{1,0:T(8,128)(2,1)}, u32[]{:S(2)}, u32[]{:S(2)}) collective-permute-start(bf16[128,2048]{1,0:T(8,128)(2,1)} %get-tuple-element.312), channel_id=1, source_target_pairs={{4,0},{6,2},{1,5},{3,7},{2,1},{0,3},{7,4},{5,6},{12,8},{14,10},{9,... | collective-permute-start | bytes 1572872 | tf_op jit(solution)/shard_map/ppermute | solution.py:75
  610.7 25.7 %collective-permute-start.85 = (bf16[256,3072]{1,0:T(8,128)(2,1)}, bf16[256,3072]{1,0:T(8,128)(2,1)S(1)}, u32[]{:S(2)}, u32[]{:S(2)}) collective-permute-start(bf16[256,3072]{1,0:T(8,128)(2,1)} %bitcast.73), channel_id=1, source_target_pairs={{1,4},{3,6},{4,1},{6,3},{9,12},{11,14},{12,9},{14,11},{17,20},{19,... | collective-permute-start | bytes 4718600 | tf_op jit(solution)/shard_map/ppermute | solution.py:75
  621.3 16.4 %collective-permute-start.86 = (f32[2,1024]{1,0:T(2,128)S(1)}, f32[2,1024]{1,0:T(2,128)S(1)}, u32[]{:S(2)}, u32[]{:S(2)}) collective-permute-start(f32[2,1024]{1,0:T(2,128)S(1)} %fusion.25), channel_id=1, source_target_pairs={{0,16},{8,24},{16,0},{24,8},{1,17},{9,25},{17,1},{25,9},{2,18},{10... | collective-permute-start | bytes 24584 | tf_op jit(solution)/shard_map/ppermute | solution.py:151
  (104 other events, 1200.9 us)
Sparse Core Ops, SparseCore 0:
  30.6 56.2 all-gather.3
  88.6 115.5 all-gather.5
  205.8 114.9 all-gather.7
  328.3 128.9 reduce-scatter.3
  459.4 127.5 reduce-scatter.5
  589.2 58.5 reduce-scatter.7

commit v4 on v3

--- a/solution.py
+++ b/solution.py
@@ -558,7 +558,6 @@
     )
     starts = jnp.append(starts * rows, same).astype(jnp.int32)
     length = lengths[0]
-    work_length = trade(lengths)
 
     order = Order()
 
@@ -626,10 +625,11 @@
         streams.append(stream)
         attn_factors.append(lax.rsqrt(jnp.mean(stream * stream, -1, keepdims=True) + EPS))
 
-    attn_piece = trade(after(attention_columns(), work_length))
+    attn_piece = trade(attention_columns())
+    work_length = trade(after(lengths, attn_piece))
     attn_weight = gather_z(attn_piece)
     here = [send_rows(after(tokens[0, 0], attn_piece))]
-    units_piece = [trade(after(unit_columns(0), attn_piece))]
+    units_piece = [trade(after(unit_columns(0), work_length))]
     tokens_all = [order(join_rows, here[0], starts)]
     here.append(send_rows(after(tokens[0, 1], attn_piece)))
     units_weight = [gather_z(order(lambda a: a, units_piece[0]))]

time: 689 us -> 690 us (level)
  transfers between devices with their start and end apart: 98 -> 98, of which waited for: 33 -> 36; matrix products, arithmetic and copies ran while one was open for 9% -> 8% of each run, Pallas kernels for 37% -> 37%
where the time goes in v4:
time: 690 us; the launch traced here: 679 us
  Pallas kernels  250 us (36%)
  starting transfers between devices  180 us (26%)
  waiting for transfers between devices  163 us (24%)
  other arithmetic  52.4 us (8%)
  between operations  17.7 us (3%)
  local copies, waits for them, and re-layouts  16.9 us (2%)
    ppermute x87, starting transfers between devices, send(): return lax.ppermute(values, ('lo', 'y', 'core'), pairs)  172 us
    ppermute x87, waiting for transfers between devices, send(): return lax.ppermute(values, ('lo', 'y', 'core'), pairs)  158 us
    pallas_call x8, Pallas kernels, project(): pl.pallas_call(functools.partial(project_kernel, len(lhs), rows), grid=(w...  68 us
    pallas_call x3, Pallas kernels, weight_grads(): pl.pallas_call(functools.partial(grads_kernel, plan), grid=(count * slab...  50.6 us
    pallas_call x2, Pallas kernels, mlp(): pl.pallas_call(functools.partial(mlp_kernel, count), grid=(steps,), out_s...  39.8 us
    pallas_call x2, Pallas kernels, attend_back(): pl.pallas_call(functools.partial(backward_kernel, m, heads, last), grid=(...  33.3 us
    pallas_call x2, Pallas kernels, attend(): pl.pallas_call(functools.partial(forward_kernel, m, heads), grid=(groups,...  29.4 us
    pallas_call x8, Pallas kernels, join_rows(): pl.pallas_call(assemble_kernel, out_shape=jax.ShapeDtypeStruct((4 * rows,...  28.6 us
  transfers between devices with their start and end apart: 98, of which 36 were waited for; matrix products, arithmetic and copies ran while one was open for 8% of the time, Pallas kernels for 37%

profile of v4, /device:TPU:1, one launch (start us, length us, event | category | flops | bytes accessed | tf_op | source)
XLA Modules:
  0.0 679.3 jit_solution(2517810379847672696)
XLA Ops:
  11.4 4.6 collective-permute-start
  16.1 8.2 %collective-permute-done = bf16[256,1280]{1,0:T(8,128)(2,1)S(1)} collective-permute-done((bf16[256,1280]{1,0:T(8,128)(2,1)S(1)}, bf16[256,1280]{1,0:T(8,128)(2,1)S(1)}, u32[]{:S(2)}, u32[]{:S(2)}) %collective-permute-start) | collective-permute-done | bytes 655392 | tf_op jit(solution)/shard_map/ppermute | solution.py:75
  29.9 3.8 collective-permute-start.1
  35.6 3.8 collective-permute-start.7
  42.5 26.6 %collective-permute-done.2.refs_0_ = bf16[128,2048]{1,0:T(8,128)(2,1)} collective-permute-done((bf16[128,2048]{1,0:T(8,128)(2,1)}, bf16[128,2048]{1,0:T(8,128)(2,1)}, u32[]{:S(2)}, u32[]{:S(2)}) %collective-permute-start.2) | collective-permute-done | bytes 524320 | tf_op jit(solution)/shard_map/ppermute | solution.py:75
  70.4 3.2 collective-permute-start.5
  74.2 5.4 collective-permute-done.6.refs_5_
  80.9 3.5 assemble.8.refs_0_
  96.1 12.9 %attend.2 = (bf16[512,512]{1,0:T(8,128)(2,1)}, bf16[512,256]{1,0:T(8,128)(2,1)}, f32[2,4,512]{2,1,0:T(4,128)}, bf16[512,512]{1,0:T(8,128)(2,1)}, f32[512,128]{1,0:T(8,128)}) custom-call(s32[1]{0:T(128)S(6)} %select_n.167.lengths, bf16[512,2048]{1,0:T(8,128)(2,1)} %assemble.8.refs_0_, bf16[2048,1280]{1,0:T(8,128)(2,1)} %all-gather.4.cloned.1.call-done.refs_1_, ...), custom_call_target="tpu_custom_call" | custom-call | tf_op jit(solution)/shard_map/attend/pallas_call | solution.py:378
  114.5 3.2 collective-permute-start.16
  117.6 8.0 %collective-permute-done.14.refs_1_ = bf16[128,2048]{1,0:T(8,128)(2,1)S(1)} collective-permute-done((bf16[128,2048]{1,0:T(8,128)(2,1)}, bf16[128,2048]{1,0:T(8,128)(2,1)S(1)}, u32[]{:S(2)}, u32[]{:S(2)}) %collective-permute-start.14) | collective-permute-done | bytes 524320 | tf_op jit(solution)/shard_map/ppermute | solution.py:75
  128.1 8.7 %collective-permute-done.17.refs_5_ = bf16[128,2048]{1,0:T(8,128)(2,1)S(1)} collective-permute-done((bf16[128,2048]{1,0:T(8,128)(2,1)}, bf16[128,2048]{1,0:T(8,128)(2,1)S(1)}, u32[]{:S(2)}, u32[]{:S(2)}) %collective-permute-start.17) | collective-permute-done | bytes 524320 | tf_op jit(solution)/shard_map/ppermute | solution.py:75
  138.6 15.0 %collective-permute-done.19.refs_0_ = bf16[128,2048]{1,0:T(8,128)(2,1)S(1)} collective-permute-done((bf16[128,2048]{1,0:T(8,128)(2,1)S(1)}, bf16[128,2048]{1,0:T(8,128)(2,1)S(1)}, u32[]{:S(2)}, u32[]{:S(2)}) %collective-permute-start.19) | collective-permute-done | bytes 524320 | tf_op jit(solution)/shard_map/ppermute | solution.py:75
  154.9 3.4 collective-permute-start.22
  161.4 5.1 project.8
  166.4 3.5 assemble.9.refs_0_.refs_2_
  170.9 3.6 assemble.10.refs_2_.refs_6_
  175.9 3.1 collective-permute-start.8
  179.0 3.2 collective-permute-start.9
  185.4 5.8 collective-permute-done.9
  198.0 16.6 %attend.3 = (bf16[512,512]{1,0:T(8,128)(2,1)}, bf16[512,256]{1,0:T(8,128)(2,1)}, f32[2,4,512]{2,1,0:T(4,128)}, bf16[512,512]{1,0:T(8,128)(2,1)}, f32[512,128]{1,0:T(8,128)}) custom-call(s32[1]{0:T(128)S(6)} %select_n.167.lengths, bf16[512,2048]{1,0:T(8,128)(2,1)} %assemble.9.refs_0_.refs_2_, bf16[2048,1280]{1,0:T(8,128)(2,1)} %all-gather.4.cloned.1.call-done.refs_1_, ...), custom_call_target="tpu_custom_call" | custom-call | tf_op jit(solution)/shard_map/attend/pallas_call | solution.py:378
  214.6 5.0 project.9
  219.6 3.4 collective-permute-start.32
  224.4 3.4 collective-permute-start.34
  234.0 5.6 collective-permute-start.25
  241.2 3.4 collective-permute-start.27
  246.7 3.6 assemble.11.refs_3_.refs_8_
  253.5 3.5 collective-permute-done.27.refs_3_
  257.0 3.5 assemble.12.refs_0_
  264.6 3.7 collective-permute-start.41
  268.4 4.4 collective-permute-done.39.refs_0_
  274.0 5.1 collective-permute-start.42
  279.2 6.3 collective-permute-done.43.refs_5_
  287.1 3.6 assemble.13.refs_1_.refs_2_
  290.8 19.9 %mlp.2 = (bf16[512,1024]{1,0:T(8,128)(2,1)}, bf16[512,1024]{1,0:T(8,128)(2,1)}, bf16[512,1024]{1,0:T(8,128)(2,1)}, bf16[512,1024]{1,0:T(8,128)(2,1)}, bf16[512,1...) custom-call(bf16[512,2048]{1,0:T(8,128)(2,1)} %assemble.12.refs_0_, bf16[512,2048]{1,0:T(8,128)(2,1)} %assemble.13.refs_1_.refs_2_, ...), custom_call_target="tpu_custom_call" | custom-call | tf_op jit(solution)/shard_map/mlp/pallas_call | solution.py:233
  310.6 19.3 %grads.3 = bf16[8,256,3072]{2,1,0:T(8,128)(2,1)} custom-call(bf16[512,2048]{1,0:T(8,128)(2,1)} %assemble.12.refs_0_, bf16[512,1024]{1,0:T(8,128)(2,1)} %get-tuple-element.255.refs_1_.refs_0_, bf16[512,2048]{1,0:T(8,128)(2,1)} %assemble.13.refs_1_.refs_2_, bf16[512,1024]{1,0:T(8,128)(2,1)} %get-tuple-element.253.refs_3_.refs_0_, ...), custom_call_target="tpu_custom_call" | custom-call | tf_op jit(solution)/shard_map/grads/pallas_call | solution.py:285
  330.0 20.0 %mlp.3 = (bf16[512,1024]{1,0:T(8,128)(2,1)}, bf16[512,1024]{1,0:T(8,128)(2,1)}, bf16[512,1024]{1,0:T(8,128)(2,1)}, bf16[512,1024]{1,0:T(8,128)(2,1)}, bf16[512,1...) custom-call(bf16[512,2048]{1,0:T(8,128)(2,1)} %assemble.12.refs_0_, bf16[512,2048]{1,0:T(8,128)(2,1)} %assemble.13.refs_1_.refs_2_, ...), custom_call_target="tpu_custom_call" | custom-call | tf_op jit(solution)/shard_map/mlp/pallas_call | solution.py:233
  350.0 19.2 %grads.4 = bf16[8,256,3072]{2,1,0:T(8,128)(2,1)} custom-call(bf16[512,2048]{1,0:T(8,128)(2,1)} %assemble.12.refs_0_, bf16[512,1024]{1,0:T(8,128)(2,1)} %get-tuple-element.248.refs_1_.refs_2_, bf16[512,2048]{1,0:T(8,128)(2,1)} %assemble.13.refs_1_.refs_2_, bf16[512,1024]{1,0:T(8,128)(2,1)} %get-tuple-element.249.refs_3_.refs_2_, ...), custom_call_target="tpu_custom_call" | custom-call | tf_op jit(solution)/shard_map/grads/pallas_call | solution.py:285
  369.3 14.5 %project.10 = (bf16[128,2048]{1,0:T(8,128)(2,1)}, bf16[128,2048]{1,0:T(8,128)(2,1)}, bf16[128,2048]{1,0:T(8,128)(2,1)}, bf16[128,2048]{1,0:T(8,128)(2,1)}) custom-call(s32[5]{0:T(128)} %pad_add_fusion.starts, bf16[512,1024]{1,0:T(8,128)(2,1)} %get-tuple-element.253.refs_3_.refs_0_, bf16[512,1024]{1,0:T(8,128)(2,1)} %get-tuple-element.243.refs_5_.refs_1_, ...), custom_call_target="tpu_custom_call" | custom-call | tf_op jit(solution)/shard_map/project/pallas_call | solution.py:193
  388.0 14.5 %project.11 = (bf16[128,2048]{1,0:T(8,128)(2,1)}, bf16[128,2048]{1,0:T(8,128)(2,1)}, bf16[128,2048]{1,0:T(8,128)(2,1)}, bf16[128,2048]{1,0:T(8,128)(2,1)}) custom-call(s32[5]{0:T(128)} %pad_add_fusion.starts, bf16[512,1024]{1,0:T(8,128)(2,1)} %get-tuple-element.255.refs_1_.refs_0_, bf16[512,1024]{1,0:T(8,128)(2,1)} %get-tuple-element.242.refs_4_.refs_1_, ...), custom_call_target="tpu_custom_call" | custom-call | tf_op jit(solution)/shard_map/project/pallas_call | solution.py:193
  407.7 8.8 %project.12 = (bf16[128,2048]{1,0:T(8,128)(2,1)}, bf16[128,2048]{1,0:T(8,128)(2,1)}, bf16[128,2048]{1,0:T(8,128)(2,1)}, bf16[128,2048]{1,0:T(8,128)(2,1)}) custom-call(s32[5]{0:T(128)} %pad_add_fusion.starts, bf16[512,1024]{1,0:T(8,128)(2,1)} %get-tuple-element.257.refs_9_.refs_0_, bf16[512,1024]{1,0:T(8,128)(2,1)} %get-tuple-element.252.refs_9_.refs_1_, ...), custom_call_target="tpu_custom_call" | custom-call | tf_op jit(solution)/shard_map/project/pallas_call | solution.py:193
  416.5 8.9 %project.13 = (bf16[128,2048]{1,0:T(8,128)(2,1)}, bf16[128,2048]{1,0:T(8,128)(2,1)}, bf16[128,2048]{1,0:T(8,128)(2,1)}, bf16[128,2048]{1,0:T(8,128)(2,1)}) custom-call(s32[5]{0:T(128)} %pad_add_fusion.starts, bf16[512,1024]{1,0:T(8,128)(2,1)} %get-tuple-element.259.refs_7_.refs_0_, bf16[512,1024]{1,0:T(8,128)(2,1)} %get-tuple-element.247.refs_7_.refs_1_, ...), custom_call_target="tpu_custom_call" | custom-call | tf_op jit(solution)/shard_map/project/pallas_call | solution.py:193
  426.9 6.1 collective-permute-start.49
  435.9 3.5 collective-permute-done.49
  439.5 3.5 collective-permute-start.70
  447.3 4.1 collective-permute-done.56
  455.0 6.8 %collective-permute-done.52 = bf16[128,2048]{1,0:T(8,128)(2,1)S(1)} collective-permute-done((bf16[128,2048]{1,0:T(8,128)(2,1)S(1)}, bf16[128,2048]{1,0:T(8,128)(2,1)S(1)}, u32[]{:S(2)}, u32[]{:S(2)}) %collective-permute-start.52) | collective-permute-done | bytes 524320 | tf_op jit(solution)/shard_map/ppermute | solution.py:75
  462.1 6.1 collective-permute-done.51
  476.0 3.5 collective-permute-start.67
  479.5 4.0 collective-permute-done.59.refs_0_
  486.1 3.5 collective-permute-start.62
  493.5 3.5 assemble.14.refs_0_.refs_6_
  497.1 19.8 %attend_back.2 = (bf16[512,768]{1,0:T(8,128)(2,1)}, bf16[512,768]{1,0:T(8,128)(2,1)}, f32[512,256]{1,0:T(8,128)}) custom-call(s32[1]{0:T(128)S(6)} %select_n.167.lengths, bf16[512,2048]{1,0:T(8,128)(2,1)} %assemble.14.refs_0_.refs_6_, bf16[2048,1280]{1,0:T(8,128)(2,1)} %all-gather.4.cloned.1.call-done.refs_1_, bf16[512,512]{1,0:T(8,128)(2,1)} %get-tuple-element.204.refs_2_, ...), custom_call_target="tpu_custom_call" | custom-call | tf_op jit(solution)/shard_map/attend_back/pallas_call | solution.py:473
  516.9 5.5 project.14
  522.4 4.9 collective-permute-start.44
  529.9 3.6 assemble.15.refs_0_.refs_4_
  534.9 3.1 collective-permute-start.84
  543.9 13.5 %attend_back.3 = (bf16[512,768]{1,0:T(8,128)(2,1)}, bf16[512,768]{1,0:T(8,128)(2,1)}) custom-call(s32[1]{0:T(128)S(6)} %select_n.167.lengths, bf16[512,2048]{1,0:T(8,128)(2,1)} %assemble.15.refs_0_.refs_4_, bf16[2048,1280]{1,0:T(8,128)(2,1)} %all-gather.4.cloned.1.call-done.refs_1_, bf16[512,512]{1,0:T(8,128)(2,1)} %get-tuple-element.179.refs_2_, ...), custom_call_target="tpu_custom_call" | custom-call | tf_op jit(solution)/shard_map/attend_back/pallas_call | solution.py:473
  557.4 5.6 project.15
  563.0 5.4 collective-permute-done.46
  569.9 12.1 %grads.5 = bf16[8,256,1280]{2,1,0:T(8,128)(2,1)} custom-call(bf16[512,2048]{1,0:T(8,128)(2,1)} %assemble.8.refs_0_, bf16[512,768]{1,0:T(8,128)(2,1)} %get-tuple-element.318.refs_1_, bf16[512,2048]{1,0:T(8,128)(2,1)} %assemble.9.refs_0_.refs_2_, bf16[512,768]{1,0:T(8,128)(2,1)} %get-tuple-element.319.refs_3_, bf16[512,2048]{1,0:T(8,128)(2,1)} %assemble.15.refs_0_.refs_4_, ...), custom_call_target="tpu_custom_call" | custom-call | tf_op jit(solution)/shard_map/grads/pallas_call | solution.py:285
  605.2 3.5 collective-permute-done.75
  628.0 10.1 %collective-permute-done.85 = bf16[256,3072]{1,0:T(8,128)(2,1)S(1)} collective-permute-done((bf16[256,3072]{1,0:T(8,128)(2,1)}, bf16[256,3072]{1,0:T(8,128)(2,1)S(1)}, u32[]{:S(2)}, u32[]{:S(2)}) %collective-permute-start.85) | collective-permute-done | bytes 1572896 | tf_op jit(solution)/shard_map/ppermute | solution.py:75
  661.6 5.5 collective-permute-done.91
  (405 shorter events, 193.6 us)
Async XLA Ops:
  7.2 89.0 %all-gather.4.cloned.1.call-start = ((), (), s32[]{:S(2)}) async-start(), calls=%async_computation.3 | async-start | bytes 5898240 | tf_op jit(solution)/shard_map/all_gather | solution.py:565
  25.3 265.4 %all-gather.6.cloned.1.call-start = ((), (), s32[]{:S(2)}) async-start(), calls=%async_computation.4 | async-start | bytes 14155776 | tf_op jit(solution)/shard_map/all_gather | solution.py:565
  35.6 48.9 %collective-permute-start.7 = (bf16[256,3072]{1,0:T(8,128)(2,1)S(1)}, bf16[256,3072]{1,0:T(8,128)(2,1)}, u32[]{:S(2)}, u32[]{:S(2)}) collective-permute-start(bf16[256,3072]{1,0:T(8,128)(2,1)S(1)} %pad_maximum_fusion), channel_id=1, source_target_pairs={{1,4},{3,6},{4,1},{6,3},{9,12},{11,14},{12,9},{14,11},{17,20},{19,... | collective-permute-start | bytes 4718600 | tf_op jit(solution)/shard_map/ppermute | solution.py:75
  40.4 28.7 %collective-permute-start.2 = (bf16[128,2048]{1,0:T(8,128)(2,1)}, bf16[128,2048]{1,0:T(8,128)(2,1)}, u32[]{:S(2)}, u32[]{:S(2)}) collective-permute-start(bf16[128,2048]{1,0:T(8,128)(2,1)} %get-tuple-element.174.refs_4_), channel_id=1, source_target_pairs={{1,4},{3,6},{4,1},{6,3},{0,2},{2,0},{5,7},{7,5},{9,12},{11,14},{12... | collective-permute-start | bytes 1572872 | tf_op jit(solution)/shard_map/ppermute | solution.py:75
  40.4 33.8 %collective-permute-start.4 = (bf16[128,2048]{1,0:T(8,128)(2,1)}, bf16[128,2048]{1,0:T(8,128)(2,1)}, u32[]{:S(2)}, u32[]{:S(2)}) collective-permute-start(bf16[128,2048]{1,0:T(8,128)(2,1)} %get-tuple-element.174.refs_4_), channel_id=1, source_target_pairs={{1,0},{3,2},{4,5},{6,7},{9,8},{11,10},{12,13},{14,15},{17,16},{19,... | collective-permute-start | bytes 1572872 | tf_op jit(solution)/shard_map/ppermute | solution.py:75
  42.5 31.7 %collective-permute-start.3 = (bf16[128,2048]{1,0:T(8,128)(2,1)}, bf16[128,2048]{1,0:T(8,128)(2,1)}, u32[]{:S(2)}, u32[]{:S(2)}) collective-permute-start(bf16[128,2048]{1,0:T(8,128)(2,1)} %get-tuple-element.174.refs_4_), channel_id=1, source_target_pairs={{0,4},{2,6},{5,1},{7,3},{1,2},{3,0},{4,7},{6,5},{8,12},{10,14},{13... | collective-permute-start | bytes 1572872 | tf_op jit(solution)/shard_map/ppermute | solution.py:75
  87.2 242.8 %all-gather.8.cloned.1.call-start = ((), (), s32[]{:S(2)}) async-start(), calls=%async_computation.5 | async-start | bytes 14155776 | tf_op jit(solution)/shard_map/all_gather | solution.py:565
  91.8 22.7 %collective-permute-start.15 = (bf16[128,2048]{1,0:T(8,128)(2,1)}, bf16[128,2048]{1,0:T(8,128)(2,1)}, u32[]{:S(2)}, u32[]{:S(2)}) collective-permute-start(bf16[128,2048]{1,0:T(8,128)(2,1)} %get-tuple-element.190.refs_4_), channel_id=1, source_target_pairs={{1,0},{3,2},{4,5},{6,7},{9,8},{11,10},{12,13},{14,15},{17,16},{19,... | collective-permute-start | bytes 1572872 | tf_op jit(solution)/shard_map/ppermute | solution.py:75
  93.8 17.5 %collective-permute-start.13 = (bf16[128,2048]{1,0:T(8,128)(2,1)}, bf16[128,2048]{1,0:T(8,128)(2,1)}, u32[]{:S(2)}, u32[]{:S(2)}) collective-permute-start(bf16[128,2048]{1,0:T(8,128)(2,1)} %get-tuple-element.190.refs_4_), channel_id=1, source_target_pairs={{1,4},{3,6},{4,1},{6,3},{0,2},{2,0},{5,7},{7,5},{9,12},{11,14},{12... | collective-permute-start | bytes 1572872 | tf_op jit(solution)/shard_map/ppermute | solution.py:75
  109.0 65.5 %collective-permute-start.18 = (bf16[256,3072]{1,0:T(8,128)(2,1)S(1)}, bf16[256,3072]{1,0:T(8,128)(2,1)S(1)}, u32[]{:S(2)}, u32[]{:S(2)}) collective-permute-start(bf16[256,3072]{1,0:T(8,128)(2,1)S(1)} %pad_maximum_fusion.1), channel_id=1, source_target_pairs={{1,4},{3,6},{4,1},{6,3},{9,12},{11,14},{12,9},{14,11},{17,20},{19,... | collective-permute-start | bytes 4718600 | tf_op jit(solution)/shard_map/ppermute | solution.py:75
  111.3 14.3 %collective-permute-start.14 = (bf16[128,2048]{1,0:T(8,128)(2,1)}, bf16[128,2048]{1,0:T(8,128)(2,1)S(1)}, u32[]{:S(2)}, u32[]{:S(2)}) collective-permute-start(bf16[128,2048]{1,0:T(8,128)(2,1)} %get-tuple-element.190.refs_4_), channel_id=1, source_target_pairs={{0,4},{2,6},{5,1},{7,3},{1,2},{3,0},{4,7},{6,5},{8,12},{10,14},{13... | collective-permute-start | bytes 1572872 | tf_op jit(solution)/shard_map/ppermute | solution.py:75
  111.4 25.5 %collective-permute-start.17 = (bf16[128,2048]{1,0:T(8,128)(2,1)}, bf16[128,2048]{1,0:T(8,128)(2,1)S(1)}, u32[]{:S(2)}, u32[]{:S(2)}) collective-permute-start(bf16[128,2048]{1,0:T(8,128)(2,1)} %collective-permute-done.13.refs_0_), channel_id=1, source_target_pairs={{0,4},{2,6},{5,1},{7,3},{8,12},{10,14},{13,9},{15,11},{16,20},{18,... | collective-permute-start | bytes 1572872 | tf_op jit(solution)/shard_map/ppermute | solution.py:75
  112.7 40.9 %collective-permute-start.19 = (bf16[128,2048]{1,0:T(8,128)(2,1)S(1)}, bf16[128,2048]{1,0:T(8,128)(2,1)S(1)}, u32[]{:S(2)}, u32[]{:S(2)}) collective-permute-start(bf16[128,2048]{1,0:T(8,128)(2,1)S(1)} %get-tuple-element.198.refs_4_), channel_id=1, source_target_pairs={{1,4},{3,6},{4,1},{6,3},{0,2},{2,0},{5,7},{7,5},{9,12},{11,14},{12... | collective-permute-start | bytes 1572872 | tf_op jit(solution)/shard_map/ppermute | solution.py:75
  114.5 40.4 %collective-permute-start.16 = (bf16[128,2048]{1,0:T(8,128)(2,1)}, bf16[128,2048]{1,0:T(8,128)(2,1)}, u32[]{:S(2)}, u32[]{:S(2)}) collective-permute-start(bf16[128,2048]{1,0:T(8,128)(2,1)} %collective-permute-done.13.refs_0_), channel_id=1, source_target_pairs={{1,3},{3,1},{4,6},{6,4},{9,11},{11,9},{12,14},{14,12},{17,19},{19,... | collective-permute-start | bytes 1572872 | tf_op jit(solution)/shard_map/ppermute | solution.py:75
  125.6 44.4 %collective-permute-start.21 = (bf16[128,2048]{1,0:T(8,128)(2,1)S(1)}, bf16[128,2048]{1,0:T(8,128)(2,1)S(1)}, u32[]{:S(2)}, u32[]{:S(2)}) collective-permute-start(bf16[128,2048]{1,0:T(8,128)(2,1)S(1)} %get-tuple-element.198.refs_4_), channel_id=1, source_target_pairs={{1,0},{3,2},{4,5},{6,7},{9,8},{11,10},{12,13},{14,15},{17,16},{19,... | collective-permute-start | bytes 1572872 | tf_op jit(solution)/shard_map/ppermute | solution.py:75
  136.8 33.1 %collective-permute-start.20 = (bf16[128,2048]{1,0:T(8,128)(2,1)S(1)}, bf16[128,2048]{1,0:T(8,128)(2,1)S(1)}, u32[]{:S(2)}, u32[]{:S(2)}) collective-permute-start(bf16[128,2048]{1,0:T(8,128)(2,1)S(1)} %get-tuple-element.198.refs_4_), channel_id=1, source_target_pairs={{0,4},{2,6},{5,1},{7,3},{1,2},{3,0},{4,7},{6,5},{8,12},{10,14},{13... | collective-permute-start | bytes 1572872 | tf_op jit(solution)/shard_map/ppermute | solution.py:75
  153.6 16.4 %collective-permute-start.23 = (bf16[128,2048]{1,0:T(8,128)(2,1)S(1)}, bf16[128,2048]{1,0:T(8,128)(2,1)}, u32[]{:S(2)}, u32[]{:S(2)}) collective-permute-start(bf16[128,2048]{1,0:T(8,128)(2,1)S(1)} %collective-permute-done.19.refs_0_), channel_id=1, source_target_pairs={{0,4},{2,6},{5,1},{7,3},{8,12},{10,14},{13,9},{15,11},{16,20},{18,... | collective-permute-start | bytes 1572872 | tf_op jit(solution)/shard_map/ppermute | solution.py:75
  154.9 15.1 %collective-permute-start.22 = (bf16[128,2048]{1,0:T(8,128)(2,1)S(1)}, bf16[128,2048]{1,0:T(8,128)(2,1)}, u32[]{:S(2)}, u32[]{:S(2)}) collective-permute-start(bf16[128,2048]{1,0:T(8,128)(2,1)S(1)} %collective-permute-done.19.refs_0_), channel_id=1, source_target_pairs={{1,3},{3,1},{4,6},{6,4},{9,11},{11,9},{12,14},{14,12},{17,19},{19,... | collective-permute-start | bytes 1572872 | tf_op jit(solution)/shard_map/ppermute | solution.py:75
  175.9 359.0 %reduce-scatter.4.cloned.1.call-start = ((), (), s32[]{:S(2)}) async-start(), calls=%async_computation.6 | async-start | bytes 14155776 | tf_op jit(solution)/shard_map/reduce_scatter | solution.py:574
  182.2 14.4 %collective-permute-start.12 = (bf16[128,2048]{1,0:T(8,128)(2,1)}, bf16[128,2048]{1,0:T(8,128)(2,1)S(1)}, u32[]{:S(2)}, u32[]{:S(2)}) collective-permute-start(bf16[128,2048]{1,0:T(8,128)(2,1)} %get-tuple-element.183), channel_id=1, source_target_pairs={{0,1},{2,3},{5,4},{7,6},{8,9},{10,11},{13,12},{15,14},{16,17},{18,... | collective-permute-start | bytes 1572872 | tf_op jit(solution)/shard_map/ppermute | solution.py:75
  184.0 35.6 %collective-permute-start.11 = (bf16[128,2048]{1,0:T(8,128)(2,1)}, bf16[128,2048]{1,0:T(8,128)(2,1)S(1)}, u32[]{:S(2)}, u32[]{:S(2)}) collective-permute-start(bf16[128,2048]{1,0:T(8,128)(2,1)} %get-tuple-element.184), channel_id=1, source_target_pairs={{4,0},{6,2},{1,5},{3,7},{2,1},{0,3},{7,4},{5,6},{12,8},{14,10},{9,... | collective-permute-start | bytes 1572872 | tf_op jit(solution)/shard_map/ppermute | solution.py:75
  192.5 30.5 %collective-permute-start.10 = (bf16[128,2048]{1,0:T(8,128)(2,1)S(1)}, bf16[128,2048]{1,0:T(8,128)(2,1)S(1)}, u32[]{:S(2)}, u32[]{:S(2)}) collective-permute-start(bf16[128,2048]{1,0:T(8,128)(2,1)S(1)} %add_convert_fusion.7), channel_id=1, source_target_pairs={{4,1},{6,3},{1,4},{3,6},{2,0},{0,2},{7,5},{5,7},{12,9},{14,11},{9,... | collective-permute-start | bytes 1572872 | tf_op jit(solution)/shard_map/ppermute | solution.py:75
  194.7 29.7 %collective-permute-start.31 = (bf16[128,2048]{1,0:T(8,128)(2,1)S(1)}, bf16[128,2048]{1,0:T(8,128)(2,1)S(1)}, u32[]{:S(2)}, u32[]{:S(2)}) collective-permute-start(bf16[128,2048]{1,0:T(8,128)(2,1)S(1)} %get-tuple-element.215.refs_4_), channel_id=1, source_target_pairs={{1,0},{3,2},{4,5},{6,7},{9,8},{11,10},{12,13},{14,15},{17,16},{19,... | collective-permute-start | bytes 1572872 | tf_op jit(solution)/shard_map/ppermute | solution.py:75
  196.0 31.7 %collective-permute-start.30 = (bf16[128,2048]{1,0:T(8,128)(2,1)S(1)}, bf16[128,2048]{1,0:T(8,128)(2,1)S(1)}, u32[]{:S(2)}, u32[]{:S(2)}) collective-permute-start(bf16[128,2048]{1,0:T(8,128)(2,1)S(1)} %get-tuple-element.215.refs_4_), channel_id=1, source_target_pairs={{0,4},{2,6},{5,1},{7,3},{1,2},{3,0},{4,7},{6,5},{8,12},{10,14},{13... | collective-permute-start | bytes 1572872 | tf_op jit(solution)/shard_map/ppermute | solution.py:75
  196.6 34.0 %collective-permute-start.33 = (bf16[128,2048]{1,0:T(8,128)(2,1)S(1)}, bf16[128,2048]{1,0:T(8,128)(2,1)S(1)}, u32[]{:S(2)}, u32[]{:S(2)}) collective-permute-start(bf16[128,2048]{1,0:T(8,128)(2,1)S(1)} %collective-permute-done.29.refs_0_), channel_id=1, source_target_pairs={{0,4},{2,6},{5,1},{7,3},{8,12},{10,14},{13,9},{15,11},{16,20},{18,... | collective-permute-start | bytes 1572872 | tf_op jit(solution)/shard_map/ppermute | solution.py:75
  224.4 15.3 %collective-permute-start.34 = (bf16[128,2048]{1,0:T(8,128)(2,1)S(1)}, bf16[128,2048]{1,0:T(8,128)(2,1)S(1)}, u32[]{:S(2)}, u32[]{:S(2)}) collective-permute-start(bf16[128,2048]{1,0:T(8,128)(2,1)S(1)} %copy-done.33), channel_id=1, source_target_pairs={{4,0},{6,2},{1,5},{3,7},{12,8},{14,10},{9,13},{11,15},{20,16},{22,... | collective-permute-start | bytes 1572872 | tf_op jit(solution)/shard_map/ppermute | solution.py:75
  230.7 14.2 %collective-permute-start.26 = (bf16[128,2048]{1,0:T(8,128)(2,1)S(1)}, bf16[128,2048]{1,0:T(8,128)(2,1)S(1)}, u32[]{:S(2)}, u32[]{:S(2)}) collective-permute-start(bf16[128,2048]{1,0:T(8,128)(2,1)S(1)} %multiply_convert_fusion.7.refs_4_), channel_id=1, source_target_pairs={{1,0},{3,2},{4,5},{6,7},{9,8},{11,10},{12,13},{14,15},{17,16},{19,... | collective-permute-start | bytes 1572872 | tf_op jit(solution)/shard_map/ppermute | solution.py:75
  234.0 16.5 %collective-permute-start.25 = (bf16[128,2048]{1,0:T(8,128)(2,1)S(1)}, bf16[128,2048]{1,0:T(8,128)(2,1)S(1)}, u32[]{:S(2)}, u32[]{:S(2)}) collective-permute-start(bf16[128,2048]{1,0:T(8,128)(2,1)S(1)} %multiply_convert_fusion.7.refs_4_), channel_id=1, source_target_pairs={{0,4},{2,6},{5,1},{7,3},{1,2},{3,0},{4,7},{6,5},{8,12},{10,14},{13... | collective-permute-start | bytes 1572872 | tf_op jit(solution)/shard_map/ppermute | solution.py:75
  241.2 15.8 %collective-permute-start.27 = (bf16[128,2048]{1,0:T(8,128)(2,1)}, bf16[128,2048]{1,0:T(8,128)(2,1)}, u32[]{:S(2)}, u32[]{:S(2)}) collective-permute-start(bf16[128,2048]{1,0:T(8,128)(2,1)} %collective-permute-done.24.refs_0_), channel_id=1, source_target_pairs={{1,3},{3,1},{4,6},{6,4},{9,11},{11,9},{12,14},{14,12},{17,19},{19,... | collective-permute-start | bytes 1572872 | tf_op jit(solution)/shard_map/ppermute | solution.py:75
  244.8 15.7 %collective-permute-start.37 = (bf16[128,2048]{1,0:T(8,128)(2,1)}, bf16[128,2048]{1,0:T(8,128)(2,1)S(1)}, u32[]{:S(2)}, u32[]{:S(2)}) collective-permute-start(bf16[128,2048]{1,0:T(8,128)(2,1)} %get-tuple-element.225), channel_id=1, source_target_pairs={{4,0},{6,2},{1,5},{3,7},{2,1},{0,3},{7,4},{5,6},{12,8},{14,10},{9,... | collective-permute-start | bytes 1572872 | tf_op jit(solution)/shard_map/ppermute | solution.py:75
  245.7 16.7 %collective-permute-start.36 = (bf16[128,2048]{1,0:T(8,128)(2,1)S(1)}, bf16[128,2048]{1,0:T(8,128)(2,1)S(1)}, u32[]{:S(2)}, u32[]{:S(2)}) collective-permute-start(bf16[128,2048]{1,0:T(8,128)(2,1)S(1)} %add_convert_fusion.6), channel_id=1, source_target_pairs={{4,1},{6,3},{1,4},{3,6},{2,0},{0,2},{7,5},{5,7},{12,9},{14,11},{9,... | collective-permute-start | bytes 1572872 | tf_op jit(solution)/shard_map/ppermute | solution.py:75
  264.6 14.5 %collective-permute-start.41 = (bf16[128,2048]{1,0:T(8,128)(2,1)S(1)}, bf16[128,2048]{1,0:T(8,128)(2,1)S(1)}, u32[]{:S(2)}, u32[]{:S(2)}) collective-permute-start(bf16[128,2048]{1,0:T(8,128)(2,1)S(1)} %multiply_convert_fusion.6.refs_4_), channel_id=1, source_target_pairs={{1,0},{3,2},{4,5},{6,7},{9,8},{11,10},{12,13},{14,15},{17,16},{19,... | collective-permute-start | bytes 1572872 | tf_op jit(solution)/shard_map/ppermute | solution.py:75
  329.9 282.4 %reduce-scatter.6.cloned.1.call-start = ((), (), s32[]{:S(2)}) async-start(), calls=%async_computation.7 | async-start | bytes 14155776 | tf_op jit(solution)/shard_map/reduce_scatter | solution.py:574
  369.2 285.7 %reduce-scatter.8.cloned.1.call-start = ((), (), s32[]{:S(2)}) async-start(), calls=%async_computation.8 | async-start | bytes 5898240 | tf_op jit(solution)/shard_map/reduce_scatter | solution.py:574
  383.8 41.7 %collective-permute-start.54 = (bf16[128,2048]{1,0:T(8,128)(2,1)}, bf16[128,2048]{1,0:T(8,128)(2,1)S(1)}, u32[]{:S(2)}, u32[]{:S(2)}) collective-permute-start(bf16[128,2048]{1,0:T(8,128)(2,1)} %get-tuple-element.267), channel_id=1, source_target_pairs={{4,0},{6,2},{1,5},{3,7},{12,8},{14,10},{9,13},{11,15},{20,16},{22,... | collective-permute-start | bytes 1572872 | tf_op jit(solution)/shard_map/ppermute | solution.py:75
  385.1 41.8 %collective-permute-start.55 = (bf16[128,2048]{1,0:T(8,128)(2,1)}, bf16[128,2048]{1,0:T(8,128)(2,1)S(1)}, u32[]{:S(2)}, u32[]{:S(2)}) collective-permute-start(bf16[128,2048]{1,0:T(8,128)(2,1)} %get-tuple-element.268), channel_id=1, source_target_pairs={{3,1},{1,3},{6,4},{4,6},{11,9},{9,11},{14,12},{12,14},{19,17},{17,... | collective-permute-start | bytes 1572872 | tf_op jit(solution)/shard_map/ppermute | solution.py:75
  402.5 30.8 %collective-permute-start.53 = (bf16[128,2048]{1,0:T(8,128)(2,1)}, bf16[128,2048]{1,0:T(8,128)(2,1)}, u32[]{:S(2)}, u32[]{:S(2)}) collective-permute-start(bf16[128,2048]{1,0:T(8,128)(2,1)} %get-tuple-element.265), channel_id=1, source_target_pairs={{0,1},{2,3},{5,4},{7,6},{8,9},{10,11},{13,12},{15,14},{16,17},{18,... | collective-permute-start | bytes 1572872 | tf_op jit(solution)/shard_map/ppermute | solution.py:75
  403.8 39.2 %collective-permute-start.50 = (bf16[128,2048]{1,0:T(8,128)(2,1)}, bf16[128,2048]{1,0:T(8,128)(2,1)S(1)}, u32[]{:S(2)}, u32[]{:S(2)}) collective-permute-start(bf16[128,2048]{1,0:T(8,128)(2,1)} %get-tuple-element.265), channel_id=1, source_target_pairs={{3,1},{1,3},{6,4},{4,6},{11,9},{9,11},{14,12},{12,14},{19,17},{17,... | collective-permute-start | bytes 1572872 | tf_op jit(solution)/shard_map/ppermute | solution.py:75
  406.4 28.2 %collective-permute-start.58 = (bf16[128,2048]{1,0:T(8,128)(2,1)}, bf16[128,2048]{1,0:T(8,128)(2,1)}, u32[]{:S(2)}, u32[]{:S(2)}) collective-permute-start(bf16[128,2048]{1,0:T(8,128)(2,1)} %get-tuple-element.268), channel_id=1, source_target_pairs={{0,1},{2,3},{5,4},{7,6},{8,9},{10,11},{13,12},{15,14},{16,17},{18,... | collective-permute-start | bytes 1572872 | tf_op jit(solution)/shard_map/ppermute | solution.py:75
  425.5 47.8 %collective-permute-start.73 = (bf16[128,2048]{1,0:T(8,128)(2,1)}, bf16[128,2048]{1,0:T(8,128)(2,1)S(1)}, u32[]{:S(2)}, u32[]{:S(2)}) collective-permute-start(bf16[128,2048]{1,0:T(8,128)(2,1)} %get-tuple-element.295), channel_id=1, source_target_pairs={{0,1},{2,3},{5,4},{7,6},{8,9},{10,11},{13,12},{15,14},{16,17},{18,... | collective-permute-start | bytes 1572872 | tf_op jit(solution)/shard_map/ppermute | solution.py:75
  434.6 16.7 %collective-permute-start.56 = (bf16[128,2048]{1,0:T(8,128)(2,1)S(1)}, bf16[128,2048]{1,0:T(8,128)(2,1)S(1)}, u32[]{:S(2)}, u32[]{:S(2)}) collective-permute-start(bf16[128,2048]{1,0:T(8,128)(2,1)S(1)} %add_convert_fusion.3), channel_id=1, source_target_pairs={{4,1},{6,3},{1,4},{3,6},{2,0},{0,2},{7,5},{5,7},{12,9},{14,11},{9,... | collective-permute-start | bytes 1572872 | tf_op jit(solution)/shard_map/ppermute | solution.py:75
  439.5 35.1 %collective-permute-start.70 = (bf16[128,2048]{1,0:T(8,128)(2,1)}, bf16[128,2048]{1,0:T(8,128)(2,1)S(1)}, u32[]{:S(2)}, u32[]{:S(2)}) collective-permute-start(bf16[128,2048]{1,0:T(8,128)(2,1)} %get-tuple-element.295), channel_id=1, source_target_pairs={{3,1},{1,3},{6,4},{4,6},{11,9},{9,11},{14,12},{12,14},{19,17},{17,... | collective-permute-start | bytes 1572872 | tf_op jit(solution)/shard_map/ppermute | solution.py:75
  443.0 28.4 %collective-permute-start.69 = (bf16[128,2048]{1,0:T(8,128)(2,1)S(1)}, bf16[128,2048]{1,0:T(8,128)(2,1)S(1)}, u32[]{:S(2)}, u32[]{:S(2)}) collective-permute-start(bf16[128,2048]{1,0:T(8,128)(2,1)S(1)} %copy-done.32), channel_id=1, source_target_pairs={{4,0},{6,2},{1,5},{3,7},{12,8},{14,10},{9,13},{11,15},{20,16},{22,... | collective-permute-start | bytes 1572872 | tf_op jit(solution)/shard_map/ppermute | solution.py:75
  445.0 16.9 %collective-permute-start.52 = (bf16[128,2048]{1,0:T(8,128)(2,1)S(1)}, bf16[128,2048]{1,0:T(8,128)(2,1)S(1)}, u32[]{:S(2)}, u32[]{:S(2)}) collective-permute-start(bf16[128,2048]{1,0:T(8,128)(2,1)S(1)} %copy-done.64), channel_id=1, source_target_pairs={{4,0},{6,2},{1,5},{3,7},{2,1},{0,3},{7,4},{5,6},{12,8},{14,10},{9,... | collective-permute-start | bytes 1572872 | tf_op jit(solution)/shard_map/ppermute | solution.py:75
  451.4 16.7 %collective-permute-start.51 = (bf16[128,2048]{1,0:T(8,128)(2,1)S(1)}, bf16[128,2048]{1,0:T(8,128)(2,1)S(1)}, u32[]{:S(2)}, u32[]{:S(2)}) collective-permute-start(bf16[128,2048]{1,0:T(8,128)(2,1)S(1)} %add_convert_fusion.4), channel_id=1, source_target_pairs={{4,1},{6,3},{1,4},{3,6},{2,0},{0,2},{7,5},{5,7},{12,9},{14,11},{9,... | collective-permute-start | bytes 1572872 | tf_op jit(solution)/shard_map/ppermute | solution.py:75
  474.7 17.1 %collective-permute-start.68 = (bf16[128,2048]{1,0:T(8,128)(2,1)S(1)}, bf16[128,2048]{1,0:T(8,128)(2,1)S(1)}, u32[]{:S(2)}, u32[]{:S(2)}) collective-permute-start(bf16[128,2048]{1,0:T(8,128)(2,1)S(1)} %collective-permute-done.64.refs_0_), channel_id=1, source_target_pairs={{0,4},{2,6},{5,1},{7,3},{8,12},{10,14},{13,9},{15,11},{16,20},{18,... | collective-permute-start | bytes 1572872 | tf_op jit(solution)/shard_map/ppermute | solution.py:75
  476.0 15.9 %collective-permute-start.67 = (bf16[128,2048]{1,0:T(8,128)(2,1)S(1)}, bf16[128,2048]{1,0:T(8,128)(2,1)S(1)}, u32[]{:S(2)}, u32[]{:S(2)}) collective-permute-start(bf16[128,2048]{1,0:T(8,128)(2,1)S(1)} %collective-permute-done.64.refs_0_), channel_id=1, source_target_pairs={{1,3},{3,1},{4,6},{6,4},{9,11},{11,9},{12,14},{14,12},{17,19},{19,... | collective-permute-start | bytes 1572872 | tf_op jit(solution)/shard_map/ppermute | solution.py:75
  483.5 38.9 %collective-permute-start.60 = (bf16[128,2048]{1,0:T(8,128)(2,1)S(1)}, bf16[128,2048]{1,0:T(8,128)(2,1)}, u32[]{:S(2)}, u32[]{:S(2)}) collective-permute-start(bf16[128,2048]{1,0:T(8,128)(2,1)S(1)} %get-tuple-element.292.refs_4_), channel_id=1, source_target_pairs={{0,4},{2,6},{5,1},{7,3},{1,2},{3,0},{4,7},{6,5},{8,12},{10,14},{13... | collective-permute-start | bytes 1572872 | tf_op jit(solution)/shard_map/ppermute | solution.py:75
  483.5 43.8 %collective-permute-start.63 = (bf16[128,2048]{1,0:T(8,128)(2,1)S(1)}, bf16[128,2048]{1,0:T(8,128)(2,1)}, u32[]{:S(2)}, u32[]{:S(2)}) collective-permute-start(bf16[128,2048]{1,0:T(8,128)(2,1)S(1)} %collective-permute-done.59.refs_0_), channel_id=1, source_target_pairs={{0,4},{2,6},{5,1},{7,3},{8,12},{10,14},{13,9},{15,11},{16,20},{18,... | collective-permute-start | bytes 1572872 | tf_op jit(solution)/shard_map/ppermute | solution.py:75
  486.1 43.8 %collective-permute-start.62 = (bf16[128,2048]{1,0:T(8,128)(2,1)S(1)}, bf16[128,2048]{1,0:T(8,128)(2,1)}, u32[]{:S(2)}, u32[]{:S(2)}) collective-permute-start(bf16[128,2048]{1,0:T(8,128)(2,1)S(1)} %collective-permute-done.59.refs_0_), channel_id=1, source_target_pairs={{1,3},{3,1},{4,6},{6,4},{9,11},{11,9},{12,14},{14,12},{17,19},{19,... | collective-permute-start | bytes 1572872 | tf_op jit(solution)/shard_map/ppermute | solution.py:75
  491.8 41.8 %collective-permute-start.72 = (bf16[128,2048]{1,0:T(8,128)(2,1)}, bf16[128,2048]{1,0:T(8,128)(2,1)S(1)}, u32[]{:S(2)}, u32[]{:S(2)}) collective-permute-start(bf16[128,2048]{1,0:T(8,128)(2,1)} %get-tuple-element.296), channel_id=1, source_target_pairs={{4,0},{6,2},{1,5},{3,7},{2,1},{0,3},{7,4},{5,6},{12,8},{14,10},{9,... | collective-permute-start | bytes 1572872 | tf_op jit(solution)/shard_map/ppermute | solution.py:75
  492.0 41.6 %collective-permute-start.71 = (bf16[128,2048]{1,0:T(8,128)(2,1)S(1)}, bf16[128,2048]{1,0:T(8,128)(2,1)S(1)}, u32[]{:S(2)}, u32[]{:S(2)}) collective-permute-start(bf16[128,2048]{1,0:T(8,128)(2,1)S(1)} %add_convert_fusion.2), channel_id=1, source_target_pairs={{4,1},{6,3},{1,4},{3,6},{2,0},{0,2},{7,5},{5,7},{12,9},{14,11},{9,... | collective-permute-start | bytes 1572872 | tf_op jit(solution)/shard_map/ppermute | solution.py:75
  522.4 18.5 %collective-permute-start.44 = (bf16[128,2048]{1,0:T(8,128)(2,1)}, bf16[128,2048]{1,0:T(8,128)(2,1)}, u32[]{:S(2)}, u32[]{:S(2)}) collective-permute-start(bf16[128,2048]{1,0:T(8,128)(2,1)} %get-tuple-element.261), channel_id=1, source_target_pairs={{4,0},{6,2},{1,5},{3,7},{12,8},{14,10},{9,13},{11,15},{20,16},{22,... | collective-permute-start | bytes 1572872 | tf_op jit(solution)/shard_map/ppermute | solution.py:75
  534.9 34.9 %collective-permute-start.84 = (bf16[256,3072]{1,0:T(8,128)(2,1)}, bf16[256,3072]{1,0:T(8,128)(2,1)S(1)}, u32[]{:S(2)}, u32[]{:S(2)}) collective-permute-start(bf16[256,3072]{1,0:T(8,128)(2,1)} %bitcast.77), channel_id=1, source_target_pairs={{1,4},{3,6},{4,1},{6,3},{9,12},{11,14},{12,9},{14,11},{17,20},{19,... | collective-permute-start | bytes 4718600 | tf_op jit(solution)/shard_map/ppermute | solution.py:75
  539.3 23.8 %collective-permute-start.47 = (bf16[128,2048]{1,0:T(8,128)(2,1)}, bf16[128,2048]{1,0:T(8,128)(2,1)S(1)}, u32[]{:S(2)}, u32[]{:S(2)}) collective-permute-start(bf16[128,2048]{1,0:T(8,128)(2,1)} %get-tuple-element.263), channel_id=1, source_target_pairs={{4,0},{6,2},{1,5},{3,7},{2,1},{0,3},{7,4},{5,6},{12,8},{14,10},{9,... | collective-permute-start | bytes 1572872 | tf_op jit(solution)/shard_map/ppermute | solution.py:75
  542.3 26.1 %collective-permute-start.46 = (bf16[128,2048]{1,0:T(8,128)(2,1)S(1)}, bf16[128,2048]{1,0:T(8,128)(2,1)S(1)}, u32[]{:S(2)}, u32[]{:S(2)}) collective-permute-start(bf16[128,2048]{1,0:T(8,128)(2,1)S(1)} %add_convert_fusion.5), channel_id=1, source_target_pairs={{4,1},{6,3},{1,4},{3,6},{2,0},{0,2},{7,5},{5,7},{12,9},{14,11},{9,... | collective-permute-start | bytes 1572872 | tf_op jit(solution)/shard_map/ppermute | solution.py:75
  587.0 15.1 %collective-permute-start.83 = (bf16[128,2048]{1,0:T(8,128)(2,1)}, bf16[128,2048]{1,0:T(8,128)(2,1)S(1)}, u32[]{:S(2)}, u32[]{:S(2)}) collective-permute-start(bf16[128,2048]{1,0:T(8,128)(2,1)} %get-tuple-element.314), channel_id=1, source_target_pairs={{0,1},{2,3},{5,4},{7,6},{8,9},{10,11},{13,12},{15,14},{16,17},{18,... | collective-permute-start | bytes 1572872 | tf_op jit(solution)/shard_map/ppermute | solution.py:75
  588.5 25.9 %collective-permute-start.82 = (bf16[128,2048]{1,0:T(8,128)(2,1)}, bf16[128,2048]{1,0:T(8,128)(2,1)}, u32[]{:S(2)}, u32[]{:S(2)}) collective-permute-start(bf16[128,2048]{1,0:T(8,128)(2,1)} %get-tuple-element.315), channel_id=1, source_target_pairs={{4,0},{6,2},{1,5},{3,7},{2,1},{0,3},{7,4},{5,6},{12,8},{14,10},{9,... | collective-permute-start | bytes 1572872 | tf_op jit(solution)/shard_map/ppermute | solution.py:75
  590.2 14.1 %collective-permute-start.74 = (bf16[128,2048]{1,0:T(8,128)(2,1)}, bf16[128,2048]{1,0:T(8,128)(2,1)S(1)}, u32[]{:S(2)}, u32[]{:S(2)}) collective-permute-start(bf16[128,2048]{1,0:T(8,128)(2,1)} %get-tuple-element.310), channel_id=1, source_target_pairs={{4,0},{6,2},{1,5},{3,7},{12,8},{14,10},{9,13},{11,15},{20,16},{22,... | collective-permute-start | bytes 1572872 | tf_op jit(solution)/shard_map/ppermute | solution.py:75
  592.4 16.3 %collective-permute-start.75 = (bf16[128,2048]{1,0:T(8,128)(2,1)}, bf16[128,2048]{1,0:T(8,128)(2,1)S(1)}, u32[]{:S(2)}, u32[]{:S(2)}) collective-permute-start(bf16[128,2048]{1,0:T(8,128)(2,1)} %get-tuple-element.311), channel_id=1, source_target_pairs={{3,1},{1,3},{6,4},{4,6},{11,9},{9,11},{14,12},{12,14},{19,17},{17,... | collective-permute-start | bytes 1572872 | tf_op jit(solution)/shard_map/ppermute | solution.py:75
  599.6 14.8 %collective-permute-start.81 = (bf16[128,2048]{1,0:T(8,128)(2,1)}, bf16[128,2048]{1,0:T(8,128)(2,1)}, u32[]{:S(2)}, u32[]{:S(2)}) collective-permute-start(bf16[128,2048]{1,0:T(8,128)(2,1)} %add_convert_fusion), channel_id=1, source_target_pairs={{4,1},{6,3},{1,4},{3,6},{2,0},{0,2},{7,5},{5,7},{12,9},{14,11},{9,... | collective-permute-start | bytes 1572872 | tf_op jit(solution)/shard_map/ppermute | solution.py:75
  604.3 14.7 %collective-permute-start.77 = (bf16[128,2048]{1,0:T(8,128)(2,1)}, bf16[128,2048]{1,0:T(8,128)(2,1)}, u32[]{:S(2)}, u32[]{:S(2)}) collective-permute-start(bf16[128,2048]{1,0:T(8,128)(2,1)} %get-tuple-element.312), channel_id=1, source_target_pairs={{4,0},{6,2},{1,5},{3,7},{2,1},{0,3},{7,4},{5,6},{12,8},{14,10},{9,... | collective-permute-start | bytes 1572872 | tf_op jit(solution)/shard_map/ppermute | solution.py:75
  612.3 25.8 %collective-permute-start.85 = (bf16[256,3072]{1,0:T(8,128)(2,1)}, bf16[256,3072]{1,0:T(8,128)(2,1)S(1)}, u32[]{:S(2)}, u32[]{:S(2)}) collective-permute-start(bf16[256,3072]{1,0:T(8,128)(2,1)} %bitcast.75), channel_id=1, source_target_pairs={{1,4},{3,6},{4,1},{6,3},{9,12},{11,14},{12,9},{14,11},{17,20},{19,... | collective-permute-start | bytes 4718600 | tf_op jit(solution)/shard_map/ppermute | solution.py:75
  623.0 16.4 %collective-permute-start.86 = (f32[2,1024]{1,0:T(2,128)S(1)}, f32[2,1024]{1,0:T(2,128)S(1)}, u32[]{:S(2)}, u32[]{:S(2)}) collective-permute-start(f32[2,1024]{1,0:T(2,128)S(1)} %fusion.25), channel_id=1, source_target_pairs={{0,16},{8,24},{16,0},{24,8},{1,17},{9,25},{17,1},{25,9},{2,18},{10... | collective-permute-start | bytes 24584 | tf_op jit(solution)/shard_map/ppermute | solution.py:151
  (104 other events, 1206.4 us)
Sparse Core Ops, SparseCore 0:
  25.4 57.6 all-gather.3
  87.4 118.9 all-gather.5
  208.0 114.9 all-gather.7
  330.1 128.7 reduce-scatter.3
  461.0 127.5 reduce-scatter.5
  590.8 58.5 reduce-scatter.7
